TPU v7x, 32 devices: a whole 2x2x4 slice. The times are simulated.
32 devices in a mesh: row: 8 (over z, x), col: 4 (over y, core).
Axes of the slice: x: 2, y: 2, z: 4, core: 2. Of those that a mesh axis runs over, the one named last changes fastest.
Arguments:
- stereo_neuron_outputs: bfloat16 [2, 64, 64, 512], P(None, 'row', None, 'col'), may hold values from -6 to 6
- filter_tap_coefficients: bfloat16 [3, 3, 3, 64, 64], replicated, may hold values from -0.25 to 0.25
- filter_stack_intercepts: float32 [3, 64], replicated, may hold values from -3 to 3
- reference_picture_present: int32 [64, 512], P('row', 'col'), may hold values 0 or 1
- tile_shift_amounts: int32 [8, 4], P('row', 'col'), may hold values from 0 to 256, as said below
- smoothness_charges: int32 [2], replicated, may hold values from 4 to 96, as said below
Outputs:
- aggregated: float32 [64, 512, 128], P('row', 'col')
Inputs may be any that keep to these rules, and one draw needn't show every extreme that they name: `tile_shift_amounts`: every tile's offset is a whole number of 0 to 256; some tile has exactly 256. smoothness_charges[0] lies in 4 to 16; smoothness_charges[1] is 96.
All inputs are finite; a program needn't handle non-finite values. No bound on the sum of `reference_picture_present` on one device may be relied on, other than what follows from the above.
Results may differ from a plain program's by a relative error of at most 0.006.
Values may be sent and summed in bfloat16 or wider, within the bound.
No kernel may reach another device: no remote copies, remote signals or barrier semaphores. Data moves between devices by JAX's collectives and lax.ppermute only.
A program may use at most 64 MiB of HBM per device.

v0:
```python
import functools

import jax
import jax.numpy as jnp
from jax import lax
from jax.experimental import pallas as pl
from jax.experimental.pallas import tpu as pltpu
from jax.sharding import PartitionSpec as P

DISPARITIES = 128
OFF_MOST = 256
SUB = 8
REGS = DISPARITIES // SUB
MEBI = 1024 * 1024


def lane_to_disparity(lane):
    return (lane % SUB) * REGS + lane // SUB


def disparity_to_lane(disparity):
    return (disparity % REGS) * SUB + disparity // REGS


def least_of(values):
    while len(values) > 1:
        values = [jnp.minimum(a, b) for a, b in zip(values[::2], values[1::2])]
    turned = values + [pltpu.roll(values[0], turn, 0) for turn in range(1, SUB)]
    while len(turned) > 1:
        turned = [jnp.minimum(a, b) for a, b in zip(turned[::2], turned[1::2])]
    return turned[0]


def stepped(state, p1):
    row = lax.broadcasted_iota(jnp.int32, state[0].shape, 0)
    below = jnp.where(row == 0, jnp.inf, pltpu.roll(state[-1], 1, 0))
    above = jnp.where(row == SUB - 1, jnp.inf, pltpu.roll(state[0], SUB - 1, 0))
    lower = [below] + state[:-1]
    upper = state[1:] + [above]
    return [
        jnp.minimum(s, jnp.minimum(l, u) + p1) for s, l, u in zip(state, lower, upper)
    ]


def advance(state, cost, p1, p2):
    least = least_of(state)
    return [c + jnp.minimum(t - least, p2) for t, c in zip(stepped(state, p1), cost)]


def ends(values, depth):
    row = lax.broadcasted_iota(jnp.int32, values[0].shape, 0)
    low = [jnp.where(row == 0, jnp.inf, pltpu.roll(v, 1, 0)) for v in values[-depth:]]
    high = [jnp.where(row == SUB - 1, jnp.inf, pltpu.roll(v, SUB - 1, 0)) for v in values[:depth]]
    return low, high


def walk(wide, cost, p1):
    return [
        c + jnp.minimum(s, jnp.minimum(l, u) + p1)
        for l, s, u, c in zip(wide[:-2], wide[1:-1], wide[2:], cost)
    ]


def leap(walked, cost, jump):
    return [jnp.minimum(w, c + jump) for w, c in zip(walked, cost)]


def next_jump(walked, cost, jump, p2):
    cheapest = cost
    while len(cheapest) > 1:
        cheapest = [jnp.minimum(a, b) for a, b in zip(cheapest[::2], cheapest[1::2])]
    cheapest = cheapest[0]
    for turn in (4, 2, 1):
        cheapest = jnp.minimum(cheapest, pltpu.roll(cheapest, turn, 0))
    return jnp.minimum(least_of(walked) + p2, (cheapest + p2) + jump)


def advance_pair(wide, jump, first, second, p1, p2):
    low, high = ends(first, 1)
    beyond = low + first + high
    walked = walk(wide, beyond, p1)
    middle = leap(walked, beyond, jump)
    jump_between = next_jump(walked[1:-1], first, jump, p2)
    walked = walk(middle, second, p1)
    low, high = ends(walked, 2)
    cost_low, cost_high = ends(second, 2)
    wide = leap(low + walked + high, cost_low + second + cost_high, jump_between)
    return wide, middle[1:-1], jump_between, next_jump(walked, second, jump_between, p2)


def charges(charge_ref):
    return (
        charge_ref[0].astype(jnp.float32) * (1.0 / 64.0),
        charge_ref[1].astype(jnp.float32) * (1.0 / 64.0),
    )


def registers(array):
    return [array[SUB * v : SUB * (v + 1)] for v in range(REGS)]


def band_kernel(masks, place_ref, filter_ref, bias_ref, *refs):
    parts = len(masks)
    tile_refs, edge_refs, refs = refs[:parts], refs[parts : 2 * parts], refs[2 * parts :]
    cost_ref, own_ref, maps_a, maps_b, left_unit, right_unit, present, shifts, taps_ref = refs
    _, channels, width = tile_refs[0].shape
    layers = filter_ref.shape[0]
    rows = own_ref.shape[0]
    cols = parts * width
    high = rows + 2 * layers
    first_row = place_ref[0] * rows
    rows_total = place_ref[1] * rows
    own = place_ref[2]
    lead = (OFF_MOST + 2 * width - 1) // width * width

    for layer in range(layers):
        for a in range(3):
            for b in range(3):
                taps_ref[
                    layer, b * channels : (b + 1) * channels, a * channels : (a + 1) * channels
                ] = filter_ref[layer, a, b]

    for mask, edge_ref in zip(masks, edge_refs):
        member = own ^ mask
        extra = edge_ref[4 * layers].astype(jnp.float32)
        present[:, pl.ds(pl.multiple_of(member * width, width), width)] = extra[0:16]
        shifts[member] = extra[16:24]
    right_unit[:, 0:lead] = jnp.zeros((rows * channels, lead), jnp.bfloat16)
    right_unit[:, lead + cols :] = jnp.zeros((rows * channels, width), jnp.bfloat16)

    column = lax.broadcasted_iota(jnp.int32, (1, cols), 1)
    for image in range(2):

        for mask, tile_ref, edge_ref in zip(masks, tile_refs, edge_refs):
            there = pl.ds(pl.multiple_of((own ^ mask) * width, width), width)
            for row in range(high):
                if row < layers:
                    value = edge_ref[image * layers + row]
                elif row < layers + rows:
                    value = tile_ref[image * rows + row - layers]
                else:
                    value = edge_ref[(2 + image) * layers + row - layers - rows]
                maps_a[row * channels : (row + 1) * channels, there] = value

        for layer in range(layers):
            source, target = (maps_a, maps_b) if layer % 2 == 0 else (maps_b, maps_a)
            margin = layers - 1 - layer

            steps = rows + 2 * margin

            @pl.loop(0, steps, unroll=max(k for k in range(1, 6) if steps % k == 0))
            def _(row):
                start = pl.multiple_of(row * channels, channels)
                window = source[pl.ds(start, 3 * channels), :]
                taps = jnp.dot(taps_ref[layer], window, preferred_element_type=jnp.float32)
                before = pltpu.roll(taps[:channels], 1, 1)
                after = pltpu.roll(taps[2 * channels :], cols - 1, 1)
                z = taps[channels : 2 * channels] + jnp.where(column == 0, 0.0, before)
                z = z + jnp.where(column == cols - 1, 0.0, after) + bias_ref[layer]
                if layer < layers - 1:
                    there = first_row - margin + row
                    inside = jnp.logical_and(there >= 0, there < rows_total)
                    z = jnp.maximum(z, 0.0) * jnp.where(inside, 1.0, 0.0)
                    target[pl.ds(start, channels), :] = z.astype(jnp.bfloat16)
                else:
                    scale = lax.rsqrt(jnp.sum(z * z, axis=0, keepdims=True) + 1e-06)
                    unit = (z * scale).astype(jnp.bfloat16)
                    if image == 0:
                        seen = present[pl.ds(row, 1), :]
                        unit = jnp.where(seen > 0.5, unit.astype(jnp.float32), 0.0)
                        left_unit[pl.ds(start, channels), :] = unit.astype(jnp.bfloat16)
                    else:
                        right_unit[pl.ds(start, channels), lead : lead + cols] = unit

    lane = lax.broadcasted_iota(jnp.int32, (width, DISPARITIES), 1)
    place = lax.broadcasted_iota(jnp.int32, (width, DISPARITIES), 0)

    @pl.loop(0, parts)
    def _(p):
        shift = jnp.max(shifts[p]).astype(jnp.int32)
        base = p * width - shift + lead
        block = base // width
        ahead = place + (base - block * width)
        index = (ahead - lane_to_disparity(lane)) & (DISPARITIES - 1)
        start = pl.multiple_of((block - 1) * width, width)
        here = pl.multiple_of(p * width, width)

        def tile_costs(mine):
            for y in range(rows):
                left = left_unit[y * channels : (y + 1) * channels, pl.ds(here, width)]
                right = right_unit[y * channels : (y + 1) * channels, pl.ds(start, 3 * width)]
                product = lax.dot_general(
                    left, right, (((0,), (0,)), ((), ())), preferred_element_type=jnp.float32
                )
                chosen = jnp.where(lane <= ahead, product[:, width : 2 * width], product[:, :width])
                chosen = jnp.where(lane <= ahead - width, product[:, 2 * width :], chosen)
                chosen = jnp.take_along_axis(chosen, index, axis=1, mode="promise_in_bounds")
                chosen = 1.0 - chosen
                cost_ref[pl.ds(here, width), y, :] = chosen
                if mine:
                    own_ref[y] = chosen.T.astype(jnp.bfloat16)

        pl.when(p == own)(functools.partial(tile_costs, True))
        pl.when(p != own)(functools.partial(tile_costs, False))


def across_kernel(second, place_ref, charge_ref, cost_ref, *refs):
    kept_ref, last_ref, same_ref = refs[-3:]
    cols = cost_ref.shape[0]
    width, rows, _ = kept_ref.shape
    parts = cols // width
    own = place_ref[2]
    p1, p2 = charges(charge_ref)

    place = lax.broadcasted_iota(jnp.int32, (DISPARITIES, 2 * DISPARITIES), 0)
    other = lax.broadcasted_iota(jnp.int32, (DISPARITIES, 2 * DISPARITIES), 1)
    same_ref[...] = jnp.where(place == other % DISPARITIES, 1.0, 0.0).astype(jnp.bfloat16)
    same = same_ref[...]

    def cost_at(step):
        step = jnp.minimum(step, cols - 1)
        pair = jnp.concatenate([cost_ref[step], cost_ref[cols - 1 - step]], axis=0)
        coarse = pair.astype(jnp.bfloat16)
        fine = (pair - coarse.astype(jnp.float32)).astype(jnp.bfloat16)
        return registers(
            lax.dot_general(
                same,
                jnp.concatenate([coarse, fine], axis=1),
                (((1,), (1,)), ((), ())),
                preferred_element_type=jnp.float32,
            )
        )

    def segment(p, state):
        first_step = p * width

        def run(keep_right, keep_left, state):
            def keep(i, values, jump):
                back = jnp.concatenate([v - (jump - p2) for v in values], axis=0).T
                if keep_right:
                    kept_ref[i] = back[0:rows]
                else:
                    kept_ref[width - 1 - i] = back[rows : 2 * rows]

            def body(i, carry):
                wide, jump, first = carry
                second = cost_at(first_step + 2 * i + 1)
                ahead = cost_at(first_step + 2 * i + 2)
                wide, middle, between, following = advance_pair(
                    list(wide), jump, list(first), second, p1, p2
                )
                if keep_right or keep_left:
                    keep(2 * i, middle, jump)
                    keep(2 * i + 1, wide[2:-2], between)
                return tuple(wide), following, tuple(ahead)

            low, high = ends(list(state), 2)
            level = jnp.zeros((SUB, 2 * rows), jnp.float32) + p2
            carry = (tuple(low + list(state) + high), level, tuple(cost_at(first_step)))
            wide, jump, _ = lax.fori_loop(0, width // 2, body, carry, unroll=8)
            return tuple(s - (jump - p2) for s in wide[2:-2])

        choice = jnp.where(p == own, 1, 0) + jnp.where(parts - 1 - p == own, 2, 0)
        return lax.switch(
            choice,
            [functools.partial(run, k == 1, k == 2) for k in range(3)],
            state,
        )

    if second:
        state = tuple(registers(refs[0][...]))
        span = (parts // 2, parts)
    else:
        state = tuple(jnp.zeros((SUB, 2 * rows), jnp.float32) for _ in range(REGS))
        span = (0, parts // 2)
    last_ref[...] = jnp.concatenate(lax.fori_loop(*span, segment, state), axis=0)


def down_or_up(forward, first_own, cost_ref, state, p1, p2, keep):
    group, rows = cost_ref.shape[:2]

    def block(b, state):
        member = jnp.where(forward, b, group - 1 - b)

        def run(kept, state):
            for i in range(rows):
                inner = jnp.where(forward, i, rows - 1 - i)
                cost = cost_ref[member, inner].astype(jnp.float32)
                state = advance(list(state), registers(cost), p1, p2)
                if kept:
                    keep(inner, jnp.concatenate(state, axis=0))
            return tuple(state)

        return lax.cond(
            member == first_own,
            functools.partial(run, True),
            functools.partial(run, False),
            state,
        )

    return lax.fori_loop(0, group, block, state)


def first_vertical_kernel(place_ref, charge_ref, *refs):
    *block_refs, kept_ref, last_ref, cost_ref = refs
    p1, p2 = charges(charge_ref)
    group, _, _, width = cost_ref.shape
    for k, block_ref in enumerate(block_refs):
        cost_ref[lax.rem(place_ref[4] + group - k, group)] = block_ref[...]
    state = tuple(jnp.zeros((SUB, width), jnp.float32) for _ in range(REGS))

    def keep(row, value):
        kept_ref[row] = value

    final = down_or_up(place_ref[3] == 0, place_ref[4], cost_ref, state, p1, p2, keep)
    last_ref[...] = jnp.concatenate(final, axis=0).astype(jnp.bfloat16)


def second_vertical_kernel(place_ref, charge_ref, *refs):
    *block_refs, kept_ref, came_ref, early_ref, late_ref, out_ref, total, cost_ref = refs
    p1, p2 = charges(charge_ref)
    group = cost_ref.shape[0]
    for k, block_ref in enumerate(block_refs):
        cost_ref[lax.rem(place_ref[4] + group - k, group)] = block_ref[...]
    rows, _, width = kept_ref.shape
    state = tuple(registers(came_ref[...].astype(jnp.float32)))

    def keep(row, value):
        total[row] = value + kept_ref[row]

    down_or_up(place_ref[3] != 0, place_ref[4], cost_ref, state, p1, p2, keep)
    lane = lax.broadcasted_iota(jnp.int32, (width, DISPARITIES), 1)
    index = disparity_to_lane(lane)
    for row in range(rows):
        value = total[row].T + (early_ref[:, row, :] + late_ref[:, row, :])
        out_ref[row] = jnp.take_along_axis(value, index, axis=1, mode="promise_in_bounds")


SMEM = functools.partial(pl.BlockSpec, memory_space=pltpu.SMEM)
VMEM = functools.partial(pl.BlockSpec, memory_space=pltpu.VMEM)


def call(kernel, outs, specs, scratch=(), flops=0, vmem=20):
    return pl.pallas_call(
        kernel,
        out_shape=outs,
        in_specs=specs,
        out_specs=jax.tree.map(lambda _: VMEM(), outs),
        scratch_shapes=list(scratch),
        compiler_params=pltpu.CompilerParams(vmem_limit_bytes=vmem * MEBI),
        cost_estimate=pl.CostEstimate(flops=flops, bytes_accessed=1 << 22, transcendentals=0),
    )


def spread(block, parts):
    masks, blocks = [0], [block]
    bit = parts // 2
    while bit:
        route = [(i, i ^ bit) for i in range(parts)]
        blocks += [lax.ppermute(held, "col", route) for held in blocks]
        masks += [mask ^ bit for mask in masks]
        bit //= 2
    return masks, blocks


def per_device(activations, filters, biases, present, shifts, smooth):
    _, rows, channels, width = activations.shape
    layers = filters.shape[0]
    high = rows + 2 * layers
    row_rank, row_count = lax.axis_index("row"), lax.axis_size("row")
    col_rank, parts = lax.axis_index("col"), lax.axis_size("col")
    half = row_count // 2
    cols = parts * width
    place = jnp.stack(
        [row_rank, jnp.int32(row_count), col_rank, row_rank // half, row_rank % half]
    ).astype(jnp.int32)

    downward = [(i, i + 1) for i in range(row_count - 1)]
    upward = [(i + 1, i) for i in range(row_count - 1)]
    before = lax.ppermute(activations[:, rows - layers :], "row", downward)
    after = lax.ppermute(activations[:, :layers], "row", upward)
    extra = jnp.concatenate(
        [
            present.astype(jnp.bfloat16),
            jnp.zeros((16 - rows, width), jnp.bfloat16),
            jnp.broadcast_to(shifts.astype(jnp.bfloat16), (channels - 16, width)),
        ],
        axis=0,
    )
    edges = jnp.concatenate(
        [before.reshape(-1, channels, width), after.reshape(-1, channels, width), extra[None]],
        axis=0,
    )
    masks, tiles = spread(activations.reshape(2 * rows, channels, width), parts)
    _, edges = spread(edges, parts)

    f32, bf16 = jnp.float32, jnp.bfloat16
    lead = (OFF_MOST + 2 * width - 1) // width * width
    cost, own = call(
        functools.partial(band_kernel, masks),
        (
            jax.ShapeDtypeStruct((cols, rows, DISPARITIES), f32),
            jax.ShapeDtypeStruct((rows, DISPARITIES, width), bf16),
        ),
        [SMEM()] + [VMEM()] * (2 + 2 * parts),
        [
            pltpu.VMEM((high * channels, cols), bf16),
            pltpu.VMEM(((high - 2) * channels, cols), bf16),
            pltpu.VMEM((rows * channels, cols), bf16),
            pltpu.VMEM((rows * channels, lead + cols + width), bf16),
            pltpu.VMEM((16, cols), f32),
            pltpu.VMEM((parts, SUB, width), f32),
            pltpu.VMEM((layers, 3 * channels, 3 * channels), bf16),
        ],
        flops=10**10,
        vmem=40,
    )(place, filters, biases[:, :, None], *tiles, *edges)

    blocks = [own]
    for k in range(1, half):
        turn = [(i, i // half * half + (i + k) % half) for i in range(row_count)]
        blocks.append(lax.ppermute(own, "row", turn))

    halves = (
        jax.ShapeDtypeStruct((width, rows, DISPARITIES), f32),
        jax.ShapeDtypeStruct((DISPARITIES, 2 * rows), f32),
    )
    identity = [pltpu.VMEM((DISPARITIES, 2 * DISPARITIES), bf16)]
    early, state = call(
        functools.partial(across_kernel, False),
        halves,
        [SMEM(), SMEM(), VMEM()],
        identity,
        flops=10**10,
    )(place, smooth, cost)
    *blocks, state = lax.optimization_barrier((*blocks, state))

    joined = pltpu.VMEM((half, rows, DISPARITIES, width), bf16)
    kept, last = call(
        first_vertical_kernel,
        (
            jax.ShapeDtypeStruct((rows, DISPARITIES, width), f32),
            jax.ShapeDtypeStruct((DISPARITIES, width), bf16),
        ),
        [SMEM(), SMEM()] + [VMEM()] * half,
        [joined],
        flops=2 * 10**9,
    )(place, smooth, *blocks)

    swap = [(i, (i + half) % row_count) for i in range(row_count)]
    last, state = lax.optimization_barrier((last, state))
    came = lax.ppermute(last, "row", swap)
    late, _ = call(
        functools.partial(across_kernel, True),
        halves,
        [SMEM(), SMEM(), VMEM(), VMEM()],
        identity,
        flops=10**10,
    )(place, smooth, cost, state)

    return call(
        second_vertical_kernel,
        jax.ShapeDtypeStruct((rows, width, DISPARITIES), f32),
        [SMEM(), SMEM()] + [VMEM()] * (half + 4),
        [pltpu.VMEM((rows, DISPARITIES, width), f32), joined],
        flops=3 * 10**9,
    )(place, smooth, *blocks, kept, came, early, late)


def solution(mesh):
    return jax.shard_map(
        per_device,
        mesh=mesh,
        in_specs=(P(None, "row", None, "col"), P(), P(), P("row", "col"), P("row", "col"), P()),
        out_specs=P("row", "col", None),
        check_vma=False,
    )
```

profile of v0, /device:TPU:0, one launch (start us, length us, event | category | flops | bytes accessed | tf_op | source)
XLA Modules:
  0.0 68.4 jit_solution(5488780109372206968)
XLA Ops:
  0.0 3.0 %collective-permute-start = (bf16[16,64,128]{2,1,0:T(8,128)(2,1)}, bf16[16,64,128]{2,1,0:T(8,128)(2,1)S(1)}, u32[]{:S(2)}, u32[]{:S(2)}) collective-permute-start(bf16[16,64,128]{2,1,0:T(8,128)(2,1)} %bitcast.11), channel_id=1, source_target_pairs={{0,2},{1,3},{2,0},{3,1},{4,6},{5,7},{6,4},{7,5},{8,10},{9,11},{10,... | collective-permute-start | bytes 786440 | tf_op jit(solution)/shard_map/ppermute | solution.py:360
  3.0 1.0 %fusion = (bf16[2,3,64,128]{3,2,1,0:T(8,128)(2,1)S(1)}, bf16[2,3,64,128]{3,2,1,0:T(8,128)(2,1)S(1)}) fusion(bf16[2,8,64,128]{3,2,1,0:T(8,128)(2,1)} %param.6), kind=kLoop, calls=%fused_computation.2 | loop fusion | bytes 393216 | tf_op jit(solution)/shard_map/slice | solution.py:380
  3.9 1.3 %collective-permute-start.4 = (bf16[2,3,64,128]{3,2,1,0:T(8,128)(2,1)S(1)}, bf16[2,3,64,128]{3,2,1,0:T(8,128)(2,1)S(1)}, u32[]{:S(2)}, u32[]{:S(2)}) collective-permute-start(bf16[2,3,64,128]{3,2,1,0:T(8,128)(2,1)S(1)} %get-tuple-element.34), channel_id=1, source_target_pairs={{4,0},{8,4},{12,8},{16,12},{20,16},{24,20},{28,24},{5,1},{9,5},{13... | collective-permute-start | bytes 294920 | tf_op jit(solution)/shard_map/ppermute | solution.py:381
  5.2 4.6 %collective-permute-start.3 = (bf16[2,3,64,128]{3,2,1,0:T(8,128)(2,1)S(1)}, bf16[2,3,64,128]{3,2,1,0:T(8,128)(2,1)S(1)}, u32[]{:S(2)}, u32[]{:S(2)}) collective-permute-start(bf16[2,3,64,128]{3,2,1,0:T(8,128)(2,1)S(1)} %get-tuple-element.33), channel_id=1, source_target_pairs={{0,4},{4,8},{8,12},{12,16},{16,20},{20,24},{24,28},{1,5},{5,9},{9,... | collective-permute-start | bytes 294920 | tf_op jit(solution)/shard_map/ppermute | solution.py:380
  9.8 0.7 %convert_element_type.6 = bf16[8,128]{1,0:T(8,128)(2,1)S(1)} convert(s32[8,128]{1,0:T(8,128)} %param.9) | non-fusion elementwise | flops 1024 | bytes 6144 | tf_op jit(solution)/shard_map/convert_element_type | solution.py:384
  11.2 0.1 pad.5.clone
  11.2 0.1 pad.4.clone
  11.3 0.1 maximum_bitcast_fusion
  11.4 0.0 collective-permute-done.4
  11.4 0.9 %collective-permute-done.3 = bf16[2,3,64,128]{3,2,1,0:T(8,128)(2,1)S(1)} collective-permute-done((bf16[2,3,64,128]{3,2,1,0:T(8,128)(2,1)S(1)}, bf16[2,3,64,128]{3,2,1,0:T(8,128)(2,1)S(1)}, u32[]{:S(2)}, u32[]{:S(2)}) %collective-permute-start.3) | collective-permute-done | bytes 98336 | tf_op jit(solution)/shard_map/ppermute | solution.py:380
  12.4 0.4 collective-permute-start.5
  12.7 0.0 collective-permute-start.1
  12.7 0.0 collective-permute-done.refs_1_
  12.7 0.5 collective-permute-start.2
  13.2 0.0 collective-permute-start.6
  13.2 5.8 %collective-permute-done.5.refs_5_ = bf16[13,64,128]{2,1,0:T(8,128)(2,1)S(1)} collective-permute-done((bf16[13,64,128]{2,1,0:T(8,128)(2,1)S(1)}, bf16[13,64,128]{2,1,0:T(8,128)(2,1)S(1)}, u32[]{:S(2)}, u32[]{:S(2)}) %collective-permute-start.5) | collective-permute-done | bytes 213024 | tf_op jit(solution)/shard_map/ppermute | solution.py:360
  19.0 0.0 collective-permute-start.7
  19.0 0.8 %copy.7.bias_ref = f32[3,64,1]{2,1,0:T(8,128)S(1)} copy(f32[3,64,1]{1,0,2:T(4,128)} %bitcast.16) | data formatting | bytes 1536 | tf_op jit(solution)/shard_map/broadcast_in_dim | solution.py:417
  19.8 0.0 copy-start.2
  19.8 0.1 stack.19.place_ref
  19.9 0.5 collective-permute-done.7.refs_7_
  20.5 0.9 %copy-done = bf16[2,8,64,128]{3,2,1,0:T(8,128)(2,1)S(1)} copy-done((bf16[2,8,64,128]{3,2,1,0:T(8,128)(2,1)S(1)}, bf16[2,8,64,128]{3,2,1,0:T(8,128)(2,1)}, u32[]{:S(2)}) %copy-start) | copy-done | bytes 262168
  21.4 1.0 %copy-done.1 = bf16[3,3,3,64,64]{4,3,2,1,0:T(8,128)(2,1)S(1)} copy-done((bf16[3,3,3,64,64]{4,3,2,1,0:T(8,128)(2,1)S(1)}, bf16[3,3,3,64,64]{4,3,2,1,0:T(8,128)(2,1)}, u32[]{:S(2)}) %copy-start.1) | copy-done | bytes 221208
  22.4 12.2 %shard_map.64 = (f32[512,8,128]{2,1,0:T(8,128)S(1)}, bf16[8,128,128]{2,1,0:T(8,128)(2,1)S(1)}) custom-call(s32[5]{0:T(128)S(1)} %stack.19.place_ref, bf16[3,3,3,64,64]{4,3,2,1,0:T(8,128)(2,1)S(1)} %copy-done.1, f32[3,64,1]{2,1,0:T(8,128)S(1)} %copy.7.bias_ref, bf16[16,64,128]{2,1,0:T(8,128)(2,1)S(1)} %bitcast.13, ...), custom_call_target="tpu_custom_call" | custom-call | flops 10000000000 | bytes 4194304 | tf_op jit(solution)/shard_map/pallas_call | solution.py:399
  34.6 2.5 %collective-permute-start.8 = (bf16[8,128,128]{2,1,0:T(8,128)(2,1)S(1)}, bf16[8,128,128]{2,1,0:T(8,128)(2,1)S(1)}, u32[]{:S(2)}, u32[]{:S(2)}) collective-permute-start(bf16[8,128,128]{2,1,0:T(8,128)(2,1)S(1)} %get-tuple-element.22.refs_0_), channel_id=1, source_target_pairs={{0,4},{4,8},{8,12},{12,0},{16,20},{20,24},{24,28},{28,16},{1,5},{5... | collective-permute-start | bytes 786440 | tf_op jit(solution)/shard_map/ppermute | solution.py:422
  37.2 1.6 %collective-permute-start.9 = (bf16[8,128,128]{2,1,0:T(8,128)(2,1)S(1)}, bf16[8,128,128]{2,1,0:T(8,128)(2,1)S(1)}, u32[]{:S(2)}, u32[]{:S(2)}) collective-permute-start(bf16[8,128,128]{2,1,0:T(8,128)(2,1)S(1)} %get-tuple-element.22.refs_0_), channel_id=1, source_target_pairs={{0,8},{4,12},{8,0},{12,4},{16,24},{20,28},{24,16},{28,20},{1,9},{5... | collective-permute-start | bytes 786440 | tf_op jit(solution)/shard_map/ppermute | solution.py:422
  38.7 2.1 %collective-permute-start.10 = (bf16[8,128,128]{2,1,0:T(8,128)(2,1)S(1)}, bf16[8,128,128]{2,1,0:T(8,128)(2,1)S(1)}, u32[]{:S(2)}, u32[]{:S(2)}) collective-permute-start(bf16[8,128,128]{2,1,0:T(8,128)(2,1)S(1)} %get-tuple-element.22.refs_0_), channel_id=1, source_target_pairs={{0,12},{4,0},{8,4},{12,8},{16,28},{20,16},{24,20},{28,24},{1,13},{... | collective-permute-start | bytes 786440 | tf_op jit(solution)/shard_map/ppermute | solution.py:422
  40.8 9.9 %shard_map.65 = (f32[128,8,128]{2,1,0:T(8,128)S(1)}, f32[128,16]{1,0:T(8,128)S(1)}) custom-call(s32[5]{0:T(128)S(1)} %stack.19.place_ref, s32[2]{0:T(128)S(1)} %copy-done.2, f32[512,8,128]{2,1,0:T(8,128)S(1)} %get-tuple-element.20.cost_ref), custom_call_target="tpu_custom_call" | custom-call | flops 10000000000 | bytes 4194304 | tf_op jit(solution)/shard_map/pallas_call | solution.py:429
  50.7 1.3 %shard_map.66 = (f32[8,128,128]{2,1,0:T(8,128)S(1)}, bf16[128,128]{1,0:T(8,128)(2,1)S(1)}) custom-call(s32[5]{0:T(128)S(1)} %stack.19.place_ref, s32[2]{0:T(128)S(1)} %copy-done.2, bf16[8,128,128]{2,1,0:T(8,128)(2,1)S(1)} %get-tuple-element.22.refs_0_, bf16[8,128,128]{2,1,0:T(8,128)(2,1)S(1)} %collective-permute-done.8.refs_1_, ...), custom_call_target="tpu_custom_call" | custom-call | flops 2000000000 | bytes 4194304 | tf_op jit(solution)/shard_map/pallas_call | solution.py:439
  52.0 3.1 %collective-permute-start.11 = (bf16[128,128]{1,0:T(8,128)(2,1)S(1)}, bf16[128,128]{1,0:T(8,128)(2,1)S(1)}, u32[]{:S(2)}, u32[]{:S(2)}) collective-permute-start(bf16[128,128]{1,0:T(8,128)(2,1)S(1)} %get-tuple-element.29), channel_id=1, source_target_pairs={{0,16},{4,20},{8,24},{12,28},{16,0},{20,4},{24,8},{28,12},{1,17},{... | collective-permute-start | bytes 98312 | tf_op jit(solution)/shard_map/ppermute | solution.py:452
  55.1 10.5 %shard_map.67 = (f32[128,8,128]{2,1,0:T(8,128)S(1)}, f32[128,16]{1,0:T(8,128)}) custom-call(s32[5]{0:T(128)S(1)} %stack.19.place_ref, s32[2]{0:T(128)S(1)} %copy-done.2, f32[512,8,128]{2,1,0:T(8,128)S(1)} %get-tuple-element.20.cost_ref, f32[128,16]{1,0:T(8,128)S(1)} %get-tuple-element.31.refs_0_), custom_call_target="tpu_custom_call" | custom-call | flops 10000000000 | bytes 4194304 | tf_op jit(solution)/shard_map/pallas_call | solution.py:453
  65.6 2.8 %shard_map.68 = f32[8,128,128]{2,1,0:T(8,128)} custom-call(s32[5]{0:T(128)S(1)} %stack.19.place_ref, s32[2]{0:T(128)S(1)} %copy-done.2, bf16[8,128,128]{2,1,0:T(8,128)(2,1)S(1)} %get-tuple-element.22.refs_0_, bf16[8,128,128]{2,1,0:T(8,128)(2,1)S(1)} %collective-permute-done.8.refs_1_, bf16[8,128,128]{2,1,0:T(8,128)(2,1)S(1)} %collective-permute-done.9.refs_2_, ...), custom_call_target="tpu_custom_call" | custom-call | flops 3000000000 | bytes 4194304 | tf_op jit(solution)/shard_map/pallas_call | solution.py:461
  (13 shorter events, 0.1 us)
Async XLA Ops:
  0.0 12.7 %collective-permute-start = (bf16[16,64,128]{2,1,0:T(8,128)(2,1)}, bf16[16,64,128]{2,1,0:T(8,128)(2,1)S(1)}, u32[]{:S(2)}, u32[]{:S(2)}) collective-permute-start(bf16[16,64,128]{2,1,0:T(8,128)(2,1)} %bitcast.11), channel_id=1, source_target_pairs={{0,2},{1,3},{2,0},{3,1},{4,6},{5,7},{6,4},{7,5},{8,10},{9,11},{10,... | collective-permute-start | bytes 786440 | tf_op jit(solution)/shard_map/ppermute | solution.py:360
  3.9 7.5 %collective-permute-start.4 = (bf16[2,3,64,128]{3,2,1,0:T(8,128)(2,1)S(1)}, bf16[2,3,64,128]{3,2,1,0:T(8,128)(2,1)S(1)}, u32[]{:S(2)}, u32[]{:S(2)}) collective-permute-start(bf16[2,3,64,128]{3,2,1,0:T(8,128)(2,1)S(1)} %get-tuple-element.34), channel_id=1, source_target_pairs={{4,0},{8,4},{12,8},{16,12},{20,16},{24,20},{28,24},{5,1},{9,5},{13... | collective-permute-start | bytes 294920 | tf_op jit(solution)/shard_map/ppermute | solution.py:381
  5.2 7.1 %collective-permute-start.3 = (bf16[2,3,64,128]{3,2,1,0:T(8,128)(2,1)S(1)}, bf16[2,3,64,128]{3,2,1,0:T(8,128)(2,1)S(1)}, u32[]{:S(2)}, u32[]{:S(2)}) collective-permute-start(bf16[2,3,64,128]{3,2,1,0:T(8,128)(2,1)S(1)} %get-tuple-element.33), channel_id=1, source_target_pairs={{0,4},{4,8},{8,12},{12,16},{16,20},{20,24},{24,28},{1,5},{5,9},{9,... | collective-permute-start | bytes 294920 | tf_op jit(solution)/shard_map/ppermute | solution.py:380
  12.4 6.6 %collective-permute-start.5 = (bf16[13,64,128]{2,1,0:T(8,128)(2,1)S(1)}, bf16[13,64,128]{2,1,0:T(8,128)(2,1)S(1)}, u32[]{:S(2)}, u32[]{:S(2)}) collective-permute-start(bf16[13,64,128]{2,1,0:T(8,128)(2,1)S(1)} %pad_maximum_fusion.refs_4_), channel_id=1, source_target_pairs={{0,2},{1,3},{2,0},{3,1},{4,6},{5,7},{6,4},{7,5},{8,10},{9,11},{10,... | collective-permute-start | bytes 638984 | tf_op jit(solution)/shard_map/ppermute | solution.py:360
  12.7 7.2 %collective-permute-start.1 = (bf16[16,64,128]{2,1,0:T(8,128)(2,1)}, bf16[16,64,128]{2,1,0:T(8,128)(2,1)S(1)}, u32[]{:S(2)}, u32[]{:S(2)}) collective-permute-start(bf16[16,64,128]{2,1,0:T(8,128)(2,1)} %bitcast.12), channel_id=1, source_target_pairs={{0,1},{1,0},{2,3},{3,2},{4,5},{5,4},{6,7},{7,6},{8,9},{9,8},{10,11... | collective-permute-start | bytes 786440 | tf_op jit(solution)/shard_map/ppermute | solution.py:360
  12.7 7.2 %collective-permute-start.2 = (bf16[16,64,128]{2,1,0:T(8,128)(2,1)S(1)}, bf16[16,64,128]{2,1,0:T(8,128)(2,1)S(1)}, u32[]{:S(2)}, u32[]{:S(2)}) collective-permute-start(bf16[16,64,128]{2,1,0:T(8,128)(2,1)S(1)} %collective-permute-done.refs_1_), channel_id=1, source_target_pairs={{0,1},{1,0},{2,3},{3,2},{4,5},{5,4},{6,7},{7,6},{8,9},{9,8},{10,11... | collective-permute-start | bytes 786440 | tf_op jit(solution)/shard_map/ppermute | solution.py:360
  13.2 6.7 %collective-permute-start.6 = (bf16[13,64,128]{2,1,0:T(8,128)(2,1)S(1)}, bf16[13,64,128]{2,1,0:T(8,128)(2,1)S(1)}, u32[]{:S(2)}, u32[]{:S(2)}) collective-permute-start(bf16[13,64,128]{2,1,0:T(8,128)(2,1)S(1)} %pad_maximum_fusion.refs_4_), channel_id=1, source_target_pairs={{0,1},{1,0},{2,3},{3,2},{4,5},{5,4},{6,7},{7,6},{8,9},{9,8},{10,11... | collective-permute-start | bytes 638984 | tf_op jit(solution)/shard_map/ppermute | solution.py:360
  19.0 1.5 %collective-permute-start.7 = (bf16[13,64,128]{2,1,0:T(8,128)(2,1)S(1)}, bf16[13,64,128]{2,1,0:T(8,128)(2,1)S(1)}, u32[]{:S(2)}, u32[]{:S(2)}) collective-permute-start(bf16[13,64,128]{2,1,0:T(8,128)(2,1)S(1)} %collective-permute-done.5.refs_5_), channel_id=1, source_target_pairs={{0,1},{1,0},{2,3},{3,2},{4,5},{5,4},{6,7},{7,6},{8,9},{9,8},{10,11... | collective-permute-start | bytes 638984 | tf_op jit(solution)/shard_map/ppermute | solution.py:360
  19.8 21.0 %copy-start.2 = (s32[2]{0:T(128)S(1)}, s32[2]{0:T(128)}, u32[]{:S(2)}) copy-start(s32[2]{0:T(128)} %charge_ref.7) | copy-start | bytes 28
  20.5 1.0 %copy-start = (bf16[2,8,64,128]{3,2,1,0:T(8,128)(2,1)S(1)}, bf16[2,8,64,128]{3,2,1,0:T(8,128)(2,1)}, u32[]{:S(2)}) copy-start(bf16[2,8,64,128]{3,2,1,0:T(8,128)(2,1)} %param.6) | copy-start | bytes 786436
  21.4 1.0 %copy-start.1 = (bf16[3,3,3,64,64]{4,3,2,1,0:T(8,128)(2,1)S(1)}, bf16[3,3,3,64,64]{4,3,2,1,0:T(8,128)(2,1)}, u32[]{:S(2)}) copy-start(bf16[3,3,3,64,64]{4,3,2,1,0:T(8,128)(2,1)} %filter_ref.1) | copy-start | bytes 663556
  34.6 16.1 %collective-permute-start.8 = (bf16[8,128,128]{2,1,0:T(8,128)(2,1)S(1)}, bf16[8,128,128]{2,1,0:T(8,128)(2,1)S(1)}, u32[]{:S(2)}, u32[]{:S(2)}) collective-permute-start(bf16[8,128,128]{2,1,0:T(8,128)(2,1)S(1)} %get-tuple-element.22.refs_0_), channel_id=1, source_target_pairs={{0,4},{4,8},{8,12},{12,0},{16,20},{20,24},{24,28},{28,16},{1,5},{5... | collective-permute-start | bytes 786440 | tf_op jit(solution)/shard_map/ppermute | solution.py:422
  37.2 13.5 %collective-permute-start.9 = (bf16[8,128,128]{2,1,0:T(8,128)(2,1)S(1)}, bf16[8,128,128]{2,1,0:T(8,128)(2,1)S(1)}, u32[]{:S(2)}, u32[]{:S(2)}) collective-permute-start(bf16[8,128,128]{2,1,0:T(8,128)(2,1)S(1)} %get-tuple-element.22.refs_0_), channel_id=1, source_target_pairs={{0,8},{4,12},{8,0},{12,4},{16,24},{20,28},{24,16},{28,20},{1,9},{5... | collective-permute-start | bytes 786440 | tf_op jit(solution)/shard_map/ppermute | solution.py:422
  38.7 12.0 %collective-permute-start.10 = (bf16[8,128,128]{2,1,0:T(8,128)(2,1)S(1)}, bf16[8,128,128]{2,1,0:T(8,128)(2,1)S(1)}, u32[]{:S(2)}, u32[]{:S(2)}) collective-permute-start(bf16[8,128,128]{2,1,0:T(8,128)(2,1)S(1)} %get-tuple-element.22.refs_0_), channel_id=1, source_target_pairs={{0,12},{4,0},{8,4},{12,8},{16,28},{20,16},{24,20},{28,24},{1,13},{... | collective-permute-start | bytes 786440 | tf_op jit(solution)/shard_map/ppermute | solution.py:422
  52.0 13.6 %collective-permute-start.11 = (bf16[128,128]{1,0:T(8,128)(2,1)S(1)}, bf16[128,128]{1,0:T(8,128)(2,1)S(1)}, u32[]{:S(2)}, u32[]{:S(2)}) collective-permute-start(bf16[128,128]{1,0:T(8,128)(2,1)S(1)} %get-tuple-element.29), channel_id=1, source_target_pairs={{0,16},{4,20},{8,24},{12,28},{16,0},{20,4},{24,8},{28,12},{1,17},{... | collective-permute-start | bytes 98312 | tf_op jit(solution)/shard_map/ppermute | solution.py:452
where the time goes:
time: 68.7 us; the launch traced here: 68.4 us
  Pallas kernels  36.6 us (53%)
  starting transfers between devices  18.9 us (28%)
  waiting for transfers between devices  7.23 us (11%)
  local copies, waits for them, and re-layouts  3.98 us (6%)
  other arithmetic  0.81 us (1%)
  between operations  0.79 us (1%)
    pallas_call x1, Pallas kernels, per_device(): call(functools.partial(band_kernel, masks), (jax.ShapeDtypeStruct((cols,...  12.2 us
    pallas_call x1, Pallas kernels, per_device(): call(functools.partial(across_kernel, True), halves, [SMEM(), SMEM(), VME...  10.5 us
    pallas_call x1, Pallas kernels, per_device(): call(functools.partial(across_kernel, False), halves, [SMEM(), SMEM(), VM...  9.89 us
    ppermute x6, waiting for transfers between devices, spread(): blocks += [lax.ppermute(held, 'col', route) for held in blocks]  6.31 us
    ppermute x3, starting transfers between devices, per_device(): blocks.append(lax.ppermute(own, 'row', turn))  6.16 us
    ppermute x1, starting transfers between devices, per_device(): before = lax.ppermute(activations[:, rows - layers:], 'row', downward)  4.55 us
    ppermute x6, starting transfers between devices, spread(): blocks += [lax.ppermute(held, 'col', route) for held in blocks]  3.84 us
    ppermute x1, starting transfers between devices, per_device(): came = lax.ppermute(last, 'row', swap)  3.09 us
  transfers between devices with their start and end apart: 12, of which 3 were waited for; matrix products, arithmetic and copies ran while one was open for 4% of the time, Pallas kernels for 30%

commit v1 on v0

--- a/solution.py
+++ b/solution.py
@@ -236,7 +236,13 @@
 
         def run(keep_right, keep_left, state):
             def keep(i, values, jump):
-                back = jnp.concatenate([v - (jump - p2) for v in values], axis=0).T
+                values = jnp.concatenate([v - (jump - p2) for v in values], axis=0)
+                back = lax.dot_general(
+                    same[: 2 * rows, : 2 * rows],
+                    values.astype(jnp.bfloat16),
+                    (((1,), (1,)), ((), ())),
+                    preferred_element_type=jnp.float32,
+                )
                 if keep_right:
                     kept_ref[i] = back[0:rows]
                 else:

time: 68.7 us -> 75.6 us (1.10)
  Pallas kernels: 36.6 us -> 44 us
    pallas_call x1, Pallas kernels: 10.5 us -> 14.2 us  [per_device(): call(functools.partial(across_kernel, True), halves, [SMEM(), SMEM(), VME...]
    pallas_call x1, Pallas kernels: 9.89 us -> 13.6 us  [per_device(): call(functools.partial(across_kernel, False), halves, [SMEM(), SMEM(), VM...]
  transfers between devices with their start and end apart: 12 -> 12, of which waited for: 3 -> 3; matrix products, arithmetic and copies ran while one was open for 4% -> 4% of each run, Pallas kernels for 30% -> 37%
where the time goes in v1:
time: 75.6 us; the launch traced here: 75.3 us
  Pallas kernels  44 us (58%)
  starting transfers between devices  18.5 us (24%)
  waiting for transfers between devices  7.23 us (10%)
  local copies, waits for them, and re-layouts  3.98 us (5%)
  other arithmetic  0.81 us (1%)
  between operations  0.79 us (1%)
    pallas_call x1, Pallas kernels, per_device(): call(functools.partial(across_kernel, True), halves, [SMEM(), SMEM(), VME...  14.2 us
    pallas_call x1, Pallas kernels, per_device(): call(functools.partial(across_kernel, False), halves, [SMEM(), SMEM(), VM...  13.6 us
    pallas_call x1, Pallas kernels, per_device(): call(functools.partial(band_kernel, masks), (jax.ShapeDtypeStruct((cols,...  12.2 us
    ppermute x6, waiting for transfers between devices, spread(): blocks += [lax.ppermute(held, 'col', route) for held in blocks]  6.31 us
    ppermute x3, starting transfers between devices, per_device(): blocks.append(lax.ppermute(own, 'row', turn))  6.16 us
    ppermute x1, starting transfers between devices, per_device(): before = lax.ppermute(activations[:, rows - layers:], 'row', downward)  4.55 us
    ppermute x6, starting transfers between devices, spread(): blocks += [lax.ppermute(held, 'col', route) for held in blocks]  3.84 us
    pallas_call x1, Pallas kernels, per_device(): call(second_vertical_kernel, jax.ShapeDtypeStruct((rows, width, DISPARITI...  2.78 us
  transfers between devices with their start and end apart: 12, of which 3 were waited for; matrix products, arithmetic and copies ran while one was open for 4% of the time, Pallas kernels for 37%

profile of v1, /device:TPU:0, one launch (start us, length us, event | category | flops | bytes accessed | tf_op | source)
XLA Modules:
  0.0 75.3 jit_solution(279649006265988852)
XLA Ops:
  0.0 3.0 %collective-permute-start = (bf16[16,64,128]{2,1,0:T(8,128)(2,1)}, bf16[16,64,128]{2,1,0:T(8,128)(2,1)S(1)}, u32[]{:S(2)}, u32[]{:S(2)}) collective-permute-start(bf16[16,64,128]{2,1,0:T(8,128)(2,1)} %bitcast.11), channel_id=1, source_target_pairs={{0,2},{1,3},{2,0},{3,1},{4,6},{5,7},{6,4},{7,5},{8,10},{9,11},{10,... | collective-permute-start | bytes 786440 | tf_op jit(solution)/shard_map/ppermute | solution.py:366
  3.0 1.0 %fusion = (bf16[2,3,64,128]{3,2,1,0:T(8,128)(2,1)S(1)}, bf16[2,3,64,128]{3,2,1,0:T(8,128)(2,1)S(1)}) fusion(bf16[2,8,64,128]{3,2,1,0:T(8,128)(2,1)} %param.6), kind=kLoop, calls=%fused_computation.2 | loop fusion | bytes 393216 | tf_op jit(solution)/shard_map/slice | solution.py:386
  3.9 1.3 %collective-permute-start.4 = (bf16[2,3,64,128]{3,2,1,0:T(8,128)(2,1)S(1)}, bf16[2,3,64,128]{3,2,1,0:T(8,128)(2,1)S(1)}, u32[]{:S(2)}, u32[]{:S(2)}) collective-permute-start(bf16[2,3,64,128]{3,2,1,0:T(8,128)(2,1)S(1)} %get-tuple-element.34), channel_id=1, source_target_pairs={{4,0},{8,4},{12,8},{16,12},{20,16},{24,20},{28,24},{5,1},{9,5},{13... | collective-permute-start | bytes 294920 | tf_op jit(solution)/shard_map/ppermute | solution.py:387
  5.2 4.6 %collective-permute-start.3 = (bf16[2,3,64,128]{3,2,1,0:T(8,128)(2,1)S(1)}, bf16[2,3,64,128]{3,2,1,0:T(8,128)(2,1)S(1)}, u32[]{:S(2)}, u32[]{:S(2)}) collective-permute-start(bf16[2,3,64,128]{3,2,1,0:T(8,128)(2,1)S(1)} %get-tuple-element.33), channel_id=1, source_target_pairs={{0,4},{4,8},{8,12},{12,16},{16,20},{20,24},{24,28},{1,5},{5,9},{9,... | collective-permute-start | bytes 294920 | tf_op jit(solution)/shard_map/ppermute | solution.py:386
  9.8 0.7 convert_element_type.6
  11.2 0.1 pad.5.clone
  11.2 0.1 pad.4.clone
  11.3 0.1 maximum_bitcast_fusion
  11.4 0.0 collective-permute-done.4
  11.4 0.9 %collective-permute-done.3 = bf16[2,3,64,128]{3,2,1,0:T(8,128)(2,1)S(1)} collective-permute-done((bf16[2,3,64,128]{3,2,1,0:T(8,128)(2,1)S(1)}, bf16[2,3,64,128]{3,2,1,0:T(8,128)(2,1)S(1)}, u32[]{:S(2)}, u32[]{:S(2)}) %collective-permute-start.3) | collective-permute-done | bytes 98336 | tf_op jit(solution)/shard_map/ppermute | solution.py:386
  12.4 0.4 collective-permute-start.5
  12.7 0.0 collective-permute-start.1
  12.7 0.0 collective-permute-done.refs_1_
  12.7 0.5 collective-permute-start.2
  13.2 0.0 collective-permute-start.6
  13.2 5.8 %collective-permute-done.5.refs_5_ = bf16[13,64,128]{2,1,0:T(8,128)(2,1)S(1)} collective-permute-done((bf16[13,64,128]{2,1,0:T(8,128)(2,1)S(1)}, bf16[13,64,128]{2,1,0:T(8,128)(2,1)S(1)}, u32[]{:S(2)}, u32[]{:S(2)}) %collective-permute-start.5) | collective-permute-done | bytes 213024 | tf_op jit(solution)/shard_map/ppermute | solution.py:366
  19.0 0.0 collective-permute-start.7
  19.0 0.8 %copy.7.bias_ref = f32[3,64,1]{2,1,0:T(8,128)S(1)} copy(f32[3,64,1]{1,0,2:T(4,128)} %bitcast.16) | data formatting | bytes 1536 | tf_op jit(solution)/shard_map/broadcast_in_dim | solution.py:423
  19.8 0.0 copy-start.2
  19.8 0.1 stack.19.place_ref
  19.9 0.5 collective-permute-done.7.refs_7_
  20.5 0.9 %copy-done = bf16[2,8,64,128]{3,2,1,0:T(8,128)(2,1)S(1)} copy-done((bf16[2,8,64,128]{3,2,1,0:T(8,128)(2,1)S(1)}, bf16[2,8,64,128]{3,2,1,0:T(8,128)(2,1)}, u32[]{:S(2)}) %copy-start) | copy-done | bytes 262168
  21.4 1.0 %copy-done.1 = bf16[3,3,3,64,64]{4,3,2,1,0:T(8,128)(2,1)S(1)} copy-done((bf16[3,3,3,64,64]{4,3,2,1,0:T(8,128)(2,1)S(1)}, bf16[3,3,3,64,64]{4,3,2,1,0:T(8,128)(2,1)}, u32[]{:S(2)}) %copy-start.1) | copy-done | bytes 221208
  22.4 12.2 %shard_map.64 = (f32[512,8,128]{2,1,0:T(8,128)S(1)}, bf16[8,128,128]{2,1,0:T(8,128)(2,1)S(1)}) custom-call(s32[5]{0:T(128)S(1)} %stack.19.place_ref, bf16[3,3,3,64,64]{4,3,2,1,0:T(8,128)(2,1)S(1)} %copy-done.1, f32[3,64,1]{2,1,0:T(8,128)S(1)} %copy.7.bias_ref, bf16[16,64,128]{2,1,0:T(8,128)(2,1)S(1)} %bitcast.13, ...), custom_call_target="tpu_custom_call" | custom-call | flops 10000000000 | bytes 4194304 | tf_op jit(solution)/shard_map/pallas_call | solution.py:405
  34.6 2.5 %collective-permute-start.8 = (bf16[8,128,128]{2,1,0:T(8,128)(2,1)S(1)}, bf16[8,128,128]{2,1,0:T(8,128)(2,1)S(1)}, u32[]{:S(2)}, u32[]{:S(2)}) collective-permute-start(bf16[8,128,128]{2,1,0:T(8,128)(2,1)S(1)} %get-tuple-element.22.refs_0_), channel_id=1, source_target_pairs={{0,4},{4,8},{8,12},{12,0},{16,20},{20,24},{24,28},{28,16},{1,5},{5... | collective-permute-start | bytes 786440 | tf_op jit(solution)/shard_map/ppermute | solution.py:428
  37.1 1.6 %collective-permute-start.9 = (bf16[8,128,128]{2,1,0:T(8,128)(2,1)S(1)}, bf16[8,128,128]{2,1,0:T(8,128)(2,1)S(1)}, u32[]{:S(2)}, u32[]{:S(2)}) collective-permute-start(bf16[8,128,128]{2,1,0:T(8,128)(2,1)S(1)} %get-tuple-element.22.refs_0_), channel_id=1, source_target_pairs={{0,8},{4,12},{8,0},{12,4},{16,24},{20,28},{24,16},{28,20},{1,9},{5... | collective-permute-start | bytes 786440 | tf_op jit(solution)/shard_map/ppermute | solution.py:428
  38.7 2.1 %collective-permute-start.10 = (bf16[8,128,128]{2,1,0:T(8,128)(2,1)S(1)}, bf16[8,128,128]{2,1,0:T(8,128)(2,1)S(1)}, u32[]{:S(2)}, u32[]{:S(2)}) collective-permute-start(bf16[8,128,128]{2,1,0:T(8,128)(2,1)S(1)} %get-tuple-element.22.refs_0_), channel_id=1, source_target_pairs={{0,12},{4,0},{8,4},{12,8},{16,28},{20,16},{24,20},{28,24},{1,13},{... | collective-permute-start | bytes 786440 | tf_op jit(solution)/shard_map/ppermute | solution.py:428
  40.8 13.6 %shard_map.65 = (f32[128,8,128]{2,1,0:T(8,128)S(1)}, f32[128,16]{1,0:T(8,128)S(1)}) custom-call(s32[5]{0:T(128)S(1)} %stack.19.place_ref, s32[2]{0:T(128)S(1)} %copy-done.2, f32[512,8,128]{2,1,0:T(8,128)S(1)} %get-tuple-element.20.cost_ref), custom_call_target="tpu_custom_call" | custom-call | flops 10000000000 | bytes 4194304 | tf_op jit(solution)/shard_map/pallas_call | solution.py:435
  54.4 1.3 %shard_map.66 = (f32[8,128,128]{2,1,0:T(8,128)S(1)}, bf16[128,128]{1,0:T(8,128)(2,1)S(1)}) custom-call(s32[5]{0:T(128)S(1)} %stack.19.place_ref, s32[2]{0:T(128)S(1)} %copy-done.2, bf16[8,128,128]{2,1,0:T(8,128)(2,1)S(1)} %get-tuple-element.22.refs_0_, bf16[8,128,128]{2,1,0:T(8,128)(2,1)S(1)} %collective-permute-done.8.refs_1_, ...), custom_call_target="tpu_custom_call" | custom-call | flops 2000000000 | bytes 4194304 | tf_op jit(solution)/shard_map/pallas_call | solution.py:445
  55.7 2.7 %collective-permute-start.11 = (bf16[128,128]{1,0:T(8,128)(2,1)S(1)}, bf16[128,128]{1,0:T(8,128)(2,1)S(1)}, u32[]{:S(2)}, u32[]{:S(2)}) collective-permute-start(bf16[128,128]{1,0:T(8,128)(2,1)S(1)} %get-tuple-element.29), channel_id=1, source_target_pairs={{0,16},{4,20},{8,24},{12,28},{16,0},{20,4},{24,8},{28,12},{1,17},{... | collective-permute-start | bytes 98312 | tf_op jit(solution)/shard_map/ppermute | solution.py:458
  58.4 14.2 %shard_map.67 = (f32[128,8,128]{2,1,0:T(8,128)S(1)}, f32[128,16]{1,0:T(8,128)}) custom-call(s32[5]{0:T(128)S(1)} %stack.19.place_ref, s32[2]{0:T(128)S(1)} %copy-done.2, f32[512,8,128]{2,1,0:T(8,128)S(1)} %get-tuple-element.20.cost_ref, f32[128,16]{1,0:T(8,128)S(1)} %get-tuple-element.31.refs_0_), custom_call_target="tpu_custom_call" | custom-call | flops 10000000000 | bytes 4194304 | tf_op jit(solution)/shard_map/pallas_call | solution.py:459
  72.5 2.8 %shard_map.68 = f32[8,128,128]{2,1,0:T(8,128)} custom-call(s32[5]{0:T(128)S(1)} %stack.19.place_ref, s32[2]{0:T(128)S(1)} %copy-done.2, bf16[8,128,128]{2,1,0:T(8,128)(2,1)S(1)} %get-tuple-element.22.refs_0_, bf16[8,128,128]{2,1,0:T(8,128)(2,1)S(1)} %collective-permute-done.8.refs_1_, bf16[8,128,128]{2,1,0:T(8,128)(2,1)S(1)} %collective-permute-done.9.refs_2_, ...), custom_call_target="tpu_custom_call" | custom-call | flops 3000000000 | bytes 4194304 | tf_op jit(solution)/shard_map/pallas_call | solution.py:467
  (13 shorter events, 0.1 us)
Async XLA Ops:
  0.0 12.7 %collective-permute-start = (bf16[16,64,128]{2,1,0:T(8,128)(2,1)}, bf16[16,64,128]{2,1,0:T(8,128)(2,1)S(1)}, u32[]{:S(2)}, u32[]{:S(2)}) collective-permute-start(bf16[16,64,128]{2,1,0:T(8,128)(2,1)} %bitcast.11), channel_id=1, source_target_pairs={{0,2},{1,3},{2,0},{3,1},{4,6},{5,7},{6,4},{7,5},{8,10},{9,11},{10,... | collective-permute-start | bytes 786440 | tf_op jit(solution)/shard_map/ppermute | solution.py:366
  3.9 7.5 %collective-permute-start.4 = (bf16[2,3,64,128]{3,2,1,0:T(8,128)(2,1)S(1)}, bf16[2,3,64,128]{3,2,1,0:T(8,128)(2,1)S(1)}, u32[]{:S(2)}, u32[]{:S(2)}) collective-permute-start(bf16[2,3,64,128]{3,2,1,0:T(8,128)(2,1)S(1)} %get-tuple-element.34), channel_id=1, source_target_pairs={{4,0},{8,4},{12,8},{16,12},{20,16},{24,20},{28,24},{5,1},{9,5},{13... | collective-permute-start | bytes 294920 | tf_op jit(solution)/shard_map/ppermute | solution.py:387
  5.2 7.1 %collective-permute-start.3 = (bf16[2,3,64,128]{3,2,1,0:T(8,128)(2,1)S(1)}, bf16[2,3,64,128]{3,2,1,0:T(8,128)(2,1)S(1)}, u32[]{:S(2)}, u32[]{:S(2)}) collective-permute-start(bf16[2,3,64,128]{3,2,1,0:T(8,128)(2,1)S(1)} %get-tuple-element.33), channel_id=1, source_target_pairs={{0,4},{4,8},{8,12},{12,16},{16,20},{20,24},{24,28},{1,5},{5,9},{9,... | collective-permute-start | bytes 294920 | tf_op jit(solution)/shard_map/ppermute | solution.py:386
  12.4 6.6 %collective-permute-start.5 = (bf16[13,64,128]{2,1,0:T(8,128)(2,1)S(1)}, bf16[13,64,128]{2,1,0:T(8,128)(2,1)S(1)}, u32[]{:S(2)}, u32[]{:S(2)}) collective-permute-start(bf16[13,64,128]{2,1,0:T(8,128)(2,1)S(1)} %pad_maximum_fusion.refs_4_), channel_id=1, source_target_pairs={{0,2},{1,3},{2,0},{3,1},{4,6},{5,7},{6,4},{7,5},{8,10},{9,11},{10,... | collective-permute-start | bytes 638984 | tf_op jit(solution)/shard_map/ppermute | solution.py:366
  12.7 7.2 %collective-permute-start.1 = (bf16[16,64,128]{2,1,0:T(8,128)(2,1)}, bf16[16,64,128]{2,1,0:T(8,128)(2,1)S(1)}, u32[]{:S(2)}, u32[]{:S(2)}) collective-permute-start(bf16[16,64,128]{2,1,0:T(8,128)(2,1)} %bitcast.12), channel_id=1, source_target_pairs={{0,1},{1,0},{2,3},{3,2},{4,5},{5,4},{6,7},{7,6},{8,9},{9,8},{10,11... | collective-permute-start | bytes 786440 | tf_op jit(solution)/shard_map/ppermute | solution.py:366
  12.7 7.2 %collective-permute-start.2 = (bf16[16,64,128]{2,1,0:T(8,128)(2,1)S(1)}, bf16[16,64,128]{2,1,0:T(8,128)(2,1)S(1)}, u32[]{:S(2)}, u32[]{:S(2)}) collective-permute-start(bf16[16,64,128]{2,1,0:T(8,128)(2,1)S(1)} %collective-permute-done.refs_1_), channel_id=1, source_target_pairs={{0,1},{1,0},{2,3},{3,2},{4,5},{5,4},{6,7},{7,6},{8,9},{9,8},{10,11... | collective-permute-start | bytes 786440 | tf_op jit(solution)/shard_map/ppermute | solution.py:366
  13.2 6.7 %collective-permute-start.6 = (bf16[13,64,128]{2,1,0:T(8,128)(2,1)S(1)}, bf16[13,64,128]{2,1,0:T(8,128)(2,1)S(1)}, u32[]{:S(2)}, u32[]{:S(2)}) collective-permute-start(bf16[13,64,128]{2,1,0:T(8,128)(2,1)S(1)} %pad_maximum_fusion.refs_4_), channel_id=1, source_target_pairs={{0,1},{1,0},{2,3},{3,2},{4,5},{5,4},{6,7},{7,6},{8,9},{9,8},{10,11... | collective-permute-start | bytes 638984 | tf_op jit(solution)/shard_map/ppermute | solution.py:366
  19.0 1.5 %collective-permute-start.7 = (bf16[13,64,128]{2,1,0:T(8,128)(2,1)S(1)}, bf16[13,64,128]{2,1,0:T(8,128)(2,1)S(1)}, u32[]{:S(2)}, u32[]{:S(2)}) collective-permute-start(bf16[13,64,128]{2,1,0:T(8,128)(2,1)S(1)} %collective-permute-done.5.refs_5_), channel_id=1, source_target_pairs={{0,1},{1,0},{2,3},{3,2},{4,5},{5,4},{6,7},{7,6},{8,9},{9,8},{10,11... | collective-permute-start | bytes 638984 | tf_op jit(solution)/shard_map/ppermute | solution.py:366
  19.8 21.0 %copy-start.2 = (s32[2]{0:T(128)S(1)}, s32[2]{0:T(128)}, u32[]{:S(2)}) copy-start(s32[2]{0:T(128)} %charge_ref.7) | copy-start | bytes 28
  20.5 1.0 %copy-start = (bf16[2,8,64,128]{3,2,1,0:T(8,128)(2,1)S(1)}, bf16[2,8,64,128]{3,2,1,0:T(8,128)(2,1)}, u32[]{:S(2)}) copy-start(bf16[2,8,64,128]{3,2,1,0:T(8,128)(2,1)} %param.6) | copy-start | bytes 786436
  21.4 1.0 %copy-start.1 = (bf16[3,3,3,64,64]{4,3,2,1,0:T(8,128)(2,1)S(1)}, bf16[3,3,3,64,64]{4,3,2,1,0:T(8,128)(2,1)}, u32[]{:S(2)}) copy-start(bf16[3,3,3,64,64]{4,3,2,1,0:T(8,128)(2,1)} %filter_ref.1) | copy-start | bytes 663556
  34.6 19.7 %collective-permute-start.8 = (bf16[8,128,128]{2,1,0:T(8,128)(2,1)S(1)}, bf16[8,128,128]{2,1,0:T(8,128)(2,1)S(1)}, u32[]{:S(2)}, u32[]{:S(2)}) collective-permute-start(bf16[8,128,128]{2,1,0:T(8,128)(2,1)S(1)} %get-tuple-element.22.refs_0_), channel_id=1, source_target_pairs={{0,4},{4,8},{8,12},{12,0},{16,20},{20,24},{24,28},{28,16},{1,5},{5... | collective-permute-start | bytes 786440 | tf_op jit(solution)/shard_map/ppermute | solution.py:428
  37.1 17.2 %collective-permute-start.9 = (bf16[8,128,128]{2,1,0:T(8,128)(2,1)S(1)}, bf16[8,128,128]{2,1,0:T(8,128)(2,1)S(1)}, u32[]{:S(2)}, u32[]{:S(2)}) collective-permute-start(bf16[8,128,128]{2,1,0:T(8,128)(2,1)S(1)} %get-tuple-element.22.refs_0_), channel_id=1, source_target_pairs={{0,8},{4,12},{8,0},{12,4},{16,24},{20,28},{24,16},{28,20},{1,9},{5... | collective-permute-start | bytes 786440 | tf_op jit(solution)/shard_map/ppermute | solution.py:428
  38.7 15.7 %collective-permute-start.10 = (bf16[8,128,128]{2,1,0:T(8,128)(2,1)S(1)}, bf16[8,128,128]{2,1,0:T(8,128)(2,1)S(1)}, u32[]{:S(2)}, u32[]{:S(2)}) collective-permute-start(bf16[8,128,128]{2,1,0:T(8,128)(2,1)S(1)} %get-tuple-element.22.refs_0_), channel_id=1, source_target_pairs={{0,12},{4,0},{8,4},{12,8},{16,28},{20,16},{24,20},{28,24},{1,13},{... | collective-permute-start | bytes 786440 | tf_op jit(solution)/shard_map/ppermute | solution.py:428
  55.7 16.8 %collective-permute-start.11 = (bf16[128,128]{1,0:T(8,128)(2,1)S(1)}, bf16[128,128]{1,0:T(8,128)(2,1)S(1)}, u32[]{:S(2)}, u32[]{:S(2)}) collective-permute-start(bf16[128,128]{1,0:T(8,128)(2,1)S(1)} %get-tuple-element.29), channel_id=1, source_target_pairs={{0,16},{4,20},{8,24},{12,28},{16,0},{20,4},{24,8},{28,12},{1,17},{... | collective-permute-start | bytes 98312 | tf_op jit(solution)/shard_map/ppermute | solution.py:458

commit v2 on v0

--- a/solution.py
+++ b/solution.py
@@ -99,26 +99,73 @@
     return [array[SUB * v : SUB * (v + 1)] for v in range(REGS)]
 
 
-def band_kernel(masks, place_ref, filter_ref, bias_ref, *refs):
+def convolved(taps, window, bias):
+    channels, cols = bias.shape[0], window.shape[1]
+    column = lax.broadcasted_iota(jnp.int32, (1, cols), 1)
+    by_tap = jnp.dot(taps, window, preferred_element_type=jnp.float32)
+    before = pltpu.roll(by_tap[:channels], 1, 1)
+    after = pltpu.roll(by_tap[2 * channels :], cols - 1, 1)
+    z = by_tap[channels : 2 * channels] + jnp.where(column == 0, 0.0, before)
+    return z + jnp.where(column == cols - 1, 0.0, after) + bias
+
+
+def grouping(steps):
+    return max(k for k in range(1, 6) if steps % k == 0)
+
+
+def inner_kernel(masks, place_ref, filter_ref, bias_ref, *refs):
     parts = len(masks)
-    tile_refs, edge_refs, refs = refs[:parts], refs[parts : 2 * parts], refs[2 * parts :]
-    cost_ref, own_ref, maps_a, maps_b, left_unit, right_unit, present, shifts, taps_ref = refs
-    _, channels, width = tile_refs[0].shape
-    layers = filter_ref.shape[0]
-    rows = own_ref.shape[0]
-    cols = parts * width
-    high = rows + 2 * layers
-    first_row = place_ref[0] * rows
-    rows_total = place_ref[1] * rows
+    tile_refs, (taps_ref, shift_ref, own_ref, *hidden_refs) = refs[:parts], refs[parts:]
+    layers, _, _, channels, _ = filter_ref.shape
+    width = tile_refs[0].shape[-1]
+    rows = tile_refs[0].shape[0] // 2
     own = place_ref[2]
-    lead = (OFF_MOST + 2 * width - 1) // width * width
-
+
+    one = lax.broadcasted_iota(jnp.int32, (channels, channels), 0)
+    two = lax.broadcasted_iota(jnp.int32, (channels, channels), 1)
     for layer in range(layers):
         for a in range(3):
             for b in range(3):
                 taps_ref[
                     layer, b * channels : (b + 1) * channels, a * channels : (a + 1) * channels
                 ] = filter_ref[layer, a, b]
+        spread_out = jnp.where(one == two, bias_ref[layer : layer + 1, :], 0.0)
+        shift_ref[layer] = jnp.sum(spread_out, axis=1, keepdims=True)
+
+    for image in range(2):
+        for mask, tile_ref in zip(masks, tile_refs):
+            there = pl.ds(pl.multiple_of((own ^ mask) * width, width), width)
+            for row in range(rows):
+                own_ref[image, row * channels : (row + 1) * channels, there] = tile_ref[
+                    image * rows + row
+                ]
+        source = own_ref
+        for layer, target in enumerate(hidden_refs):
+            steps = rows - 2 * (layer + 1)
+
+            @pl.loop(0, steps, unroll=grouping(steps))
+            def _(row):
+                start = pl.multiple_of(row * channels, channels)
+                window = source[image, pl.ds(start, 3 * channels), :]
+                z = convolved(taps_ref[layer], window, shift_ref[layer])
+                target[image, pl.ds(start, channels), :] = jnp.maximum(z, 0.0).astype(jnp.bfloat16)
+
+            source = target
+
+
+def band_kernel(masks, place_ref, taps_ref, bias_ref, rows_ref, *refs):
+    layers = taps_ref.shape[0]
+    parts = len(masks)
+    inner_refs, refs = (rows_ref, *refs[: layers - 1]), refs[layers - 1 :]
+    edge_refs, refs = refs[:parts], refs[parts:]
+    cost_ref, own_ref, left_unit, right_unit, present, shifts, *maps = refs
+    _, channels, width = edge_refs[0].shape
+    rows = own_ref.shape[0]
+    cols = parts * width
+    first_row = place_ref[0] * rows
+    rows_total = place_ref[1] * rows
+    own = place_ref[2]
+    lead = (OFF_MOST + 2 * width - 1) // width * width
 
     for mask, edge_ref in zip(masks, edge_refs):
         member = own ^ mask
@@ -128,40 +175,34 @@
     right_unit[:, 0:lead] = jnp.zeros((rows * channels, lead), jnp.bfloat16)
     right_unit[:, lead + cols :] = jnp.zeros((rows * channels, width), jnp.bfloat16)
 
-    column = lax.broadcasted_iota(jnp.int32, (1, cols), 1)
     for image in range(2):
-
-        for mask, tile_ref, edge_ref in zip(masks, tile_refs, edge_refs):
+        for inner_ref, held in zip(inner_refs, maps):
+            held[layers * channels : held.shape[0] - layers * channels, :] = inner_ref[image]
+        for mask, edge_ref in zip(masks, edge_refs):
             there = pl.ds(pl.multiple_of((own ^ mask) * width, width), width)
-            for row in range(high):
-                if row < layers:
-                    value = edge_ref[image * layers + row]
-                elif row < layers + rows:
-                    value = tile_ref[image * rows + row - layers]
-                else:
-                    value = edge_ref[(2 + image) * layers + row - layers - rows]
-                maps_a[row * channels : (row + 1) * channels, there] = value
+            for row in range(layers):
+                above, below = row * channels, (layers + rows + row) * channels
+                maps[0][above : above + channels, there] = edge_ref[image * layers + row]
+                maps[0][below : below + channels, there] = edge_ref[(2 + image) * layers + row]
 
         for layer in range(layers):
-            source, target = (maps_a, maps_b) if layer % 2 == 0 else (maps_b, maps_a)
             margin = layers - 1 - layer
-
-            steps = rows + 2 * margin
-
-            @pl.loop(0, steps, unroll=max(k for k in range(1, 6) if steps % k == 0))
+            last = layer == layers - 1
+            skipped = 0 if last else rows - 2 * (layer + 1)
+            steps = rows + 2 * margin - skipped
+
+            @pl.loop(0, steps, unroll=grouping(steps))
             def _(row):
+                if not last:
+                    row = jnp.where(row < layers, row, row + skipped)
                 start = pl.multiple_of(row * channels, channels)
-                window = source[pl.ds(start, 3 * channels), :]
-                taps = jnp.dot(taps_ref[layer], window, preferred_element_type=jnp.float32)
-                before = pltpu.roll(taps[:channels], 1, 1)
-                after = pltpu.roll(taps[2 * channels :], cols - 1, 1)
-                z = taps[channels : 2 * channels] + jnp.where(column == 0, 0.0, before)
-                z = z + jnp.where(column == cols - 1, 0.0, after) + bias_ref[layer]
-                if layer < layers - 1:
+                window = maps[layer][pl.ds(start, 3 * channels), :]
+                z = convolved(taps_ref[layer], window, bias_ref[layer])
+                if not last:
                     there = first_row - margin + row
                     inside = jnp.logical_and(there >= 0, there < rows_total)
                     z = jnp.maximum(z, 0.0) * jnp.where(inside, 1.0, 0.0)
-                    target[pl.ds(start, channels), :] = z.astype(jnp.bfloat16)
+                    maps[layer + 1][pl.ds(start, channels), :] = z.astype(jnp.bfloat16)
                 else:
                     scale = lax.rsqrt(jnp.sum(z * z, axis=0, keepdims=True) + 1e-06)
                     unit = (z * scale).astype(jnp.bfloat16)
@@ -352,15 +393,18 @@
     )
 
 
-def spread(block, parts):
+def spread(block, parts, beside=()):
     masks, blocks = [0], [block]
     bit = parts // 2
     while bit:
         route = [(i, i ^ bit) for i in range(parts)]
         blocks += [lax.ppermute(held, "col", route) for held in blocks]
         masks += [mask ^ bit for mask in masks]
+        if beside and bit == parts // 2:
+            first, *beside = lax.optimization_barrier((blocks[1], *beside))
+            blocks[1] = first
         bit //= 2
-    return masks, blocks
+    return masks, blocks, beside
 
 
 def per_device(activations, filters, biases, present, shifts, smooth):
@@ -391,30 +435,45 @@
         [before.reshape(-1, channels, width), after.reshape(-1, channels, width), extra[None]],
         axis=0,
     )
-    masks, tiles = spread(activations.reshape(2 * rows, channels, width), parts)
-    _, edges = spread(edges, parts)
+    masks, tiles, _ = spread(activations.reshape(2 * rows, channels, width), parts)
 
     f32, bf16 = jnp.float32, jnp.bfloat16
     lead = (OFF_MOST + 2 * width - 1) // width * width
+    inner = call(
+        functools.partial(inner_kernel, masks),
+        (
+            jax.ShapeDtypeStruct((layers, 3 * channels, 3 * channels), bf16),
+            jax.ShapeDtypeStruct((layers, channels, 1), f32),
+            *(
+                jax.ShapeDtypeStruct((2, (rows - 2 * layer) * channels, cols), bf16)
+                for layer in range(layers)
+            ),
+        ),
+        [SMEM()] + [VMEM()] * (2 + parts),
+        flops=2 * 10**9,
+        vmem=32,
+    )(place, filters, biases, *tiles)
+    _, edges, inner = spread(edges, parts, inner)
     cost, own = call(
         functools.partial(band_kernel, masks),
         (
             jax.ShapeDtypeStruct((cols, rows, DISPARITIES), f32),
             jax.ShapeDtypeStruct((rows, DISPARITIES, width), bf16),
         ),
-        [SMEM()] + [VMEM()] * (2 + 2 * parts),
+        [SMEM()] + [VMEM()] * (2 + layers + parts),
         [
-            pltpu.VMEM((high * channels, cols), bf16),
-            pltpu.VMEM(((high - 2) * channels, cols), bf16),
             pltpu.VMEM((rows * channels, cols), bf16),
             pltpu.VMEM((rows * channels, lead + cols + width), bf16),
             pltpu.VMEM((16, cols), f32),
             pltpu.VMEM((parts, SUB, width), f32),
-            pltpu.VMEM((layers, 3 * channels, 3 * channels), bf16),
+            *(
+                pltpu.VMEM(((high - 2 * layer) * channels, cols), bf16)
+                for layer in range(layers)
+            ),
         ],
         flops=10**10,
         vmem=40,
-    )(place, filters, biases[:, :, None], *tiles, *edges)
+    )(place, *inner, *edges)
 
     blocks = [own]
     for k in range(1, half):

time: 68.7 us -> 66.8 us (0.972)
  starting transfers between devices: 18.9 us -> 15.8 us
  Pallas kernels: 36.6 us -> 38.2 us
    ppermute x6, waiting for transfers between devices: 6.31 us -> 1.1 us  [spread(): blocks += [lax.ppermute(held, 'col', route) for held in blocks]]
    ppermute x1, waiting for transfers between devices: 0.01 us -> 3.68 us  [per_device(): after = lax.ppermute(activations[:, :layers], 'row', upward)]
    pallas_call x0 -> x1, Pallas kernels: none -> 3.57 us  [per_device(): call(functools.partial(inner_kernel, masks), (jax.ShapeDtypeStruct((layer...]
    ppermute x3, waiting for transfers between devices: 0.01 us -> 2.13 us  [per_device(): blocks.append(lax.ppermute(own, 'row', turn))]
    pallas_call x1, Pallas kernels: 12.2 us -> 10.2 us  [per_device(): call(functools.partial(band_kernel, masks), (jax.ShapeDtypeStruct((cols,...]
    ppermute x3, starting transfers between devices: 6.16 us -> 4.2 us  [per_device(): blocks.append(lax.ppermute(own, 'row', turn))]
    ppermute x1, starting transfers between devices: 4.55 us -> 3.4 us  [per_device(): before = lax.ppermute(activations[:, rows - layers:], 'row', downward)]
    ppermute x1, waiting for transfers between devices: 0.9 us -> 0.01 us  [per_device(): before = lax.ppermute(activations[:, rows - layers:], 'row', downward)]
  transfers between devices with their start and end apart: 12 -> 12, of which waited for: 3 -> 3; matrix products, arithmetic and copies ran while one was open for 4% -> 3% of each run, Pallas kernels for 30% -> 36%
where the time goes in v2:
time: 66.8 us; the launch traced here: 66.5 us
  Pallas kernels  38.2 us (57%)
  starting transfers between devices  15.8 us (24%)
  waiting for transfers between devices  6.92 us (10%)
  local copies, waits for them, and re-layouts  3.86 us (6%)
  other arithmetic  0.8 us (1%)
  between operations  0.8 us (1%)
    pallas_call x1, Pallas kernels, per_device(): call(functools.partial(across_kernel, True), halves, [SMEM(), SMEM(), VME...  10.5 us
    pallas_call x1, Pallas kernels, per_device(): call(functools.partial(band_kernel, masks), (jax.ShapeDtypeStruct((cols,...  10.2 us
    pallas_call x1, Pallas kernels, per_device(): call(functools.partial(across_kernel, False), halves, [SMEM(), SMEM(), VM...  9.88 us
    ppermute x6, starting transfers between devices, spread(): blocks += [lax.ppermute(held, 'col', route) for held in blocks]  4.3 us
    ppermute x3, starting transfers between devices, per_device(): blocks.append(lax.ppermute(own, 'row', turn))  4.2 us
    ppermute x1, waiting for transfers between devices, per_device(): after = lax.ppermute(activations[:, :layers], 'row', upward)  3.68 us
    pallas_call x1, Pallas kernels, per_device(): call(functools.partial(inner_kernel, masks), (jax.ShapeDtypeStruct((layer...  3.57 us
    ppermute x1, starting transfers between devices, per_device(): before = lax.ppermute(activations[:, rows - layers:], 'row', downward)  3.4 us
  transfers between devices with their start and end apart: 12, of which 3 were waited for; matrix products, arithmetic and copies ran while one was open for 3% of the time, Pallas kernels for 36%

profile of v2, /device:TPU:0, one launch (start us, length us, event | category | flops | bytes accessed | tf_op | source)
XLA Modules:
  0.0 66.5 jit_solution(3433716403848425517)
XLA Ops:
  0.0 3.0 %collective-permute-start.3 = (bf16[16,64,128]{2,1,0:T(8,128)(2,1)}, bf16[16,64,128]{2,1,0:T(8,128)(2,1)S(1)}, u32[]{:S(2)}, u32[]{:S(2)}) collective-permute-start(bf16[16,64,128]{2,1,0:T(8,128)(2,1)} %bitcast.10), channel_id=1, source_target_pairs={{0,2},{1,3},{2,0},{3,1},{4,6},{5,7},{6,4},{7,5},{8,10},{9,11},{10,... | collective-permute-start | bytes 786440 | tf_op jit(solution)/shard_map/ppermute | solution.py:401
  3.0 0.0 collective-permute-start.4
  3.0 1.0 %fusion = (bf16[2,3,64,128]{3,2,1,0:T(8,128)(2,1)S(1)}, bf16[2,3,64,128]{3,2,1,0:T(8,128)(2,1)S(1)}) fusion(bf16[2,8,64,128]{3,2,1,0:T(8,128)(2,1)} %param.6), kind=kLoop, calls=%fused_computation.2 | loop fusion | bytes 393216 | tf_op jit(solution)/shard_map/slice | solution.py:424
  3.9 3.4 %collective-permute-start = (bf16[2,3,64,128]{3,2,1,0:T(8,128)(2,1)S(1)}, bf16[2,3,64,128]{3,2,1,0:T(8,128)(2,1)S(1)}, u32[]{:S(2)}, u32[]{:S(2)}) collective-permute-start(bf16[2,3,64,128]{3,2,1,0:T(8,128)(2,1)S(1)} %get-tuple-element.55), channel_id=1, source_target_pairs={{0,4},{4,8},{8,12},{12,16},{16,20},{20,24},{24,28},{1,5},{5,9},{9,... | collective-permute-start | bytes 294920 | tf_op jit(solution)/shard_map/ppermute | solution.py:424
  7.4 1.3 %collective-permute-start.1 = (bf16[2,3,64,128]{3,2,1,0:T(8,128)(2,1)S(1)}, bf16[2,3,64,128]{3,2,1,0:T(8,128)(2,1)S(1)}, u32[]{:S(2)}, u32[]{:S(2)}) collective-permute-start(bf16[2,3,64,128]{3,2,1,0:T(8,128)(2,1)S(1)} %get-tuple-element.56), channel_id=1, source_target_pairs={{4,0},{8,4},{12,8},{16,12},{20,16},{24,20},{28,24},{5,1},{9,5},{13... | collective-permute-start | bytes 294920 | tf_op jit(solution)/shard_map/ppermute | solution.py:425
  9.3 0.1 pad.5.clone
  9.4 0.1 pad.4.clone
  9.5 0.7 %convert_element_type.6 = bf16[8,128]{1,0:T(8,128)(2,1)S(1)} convert(s32[8,128]{1,0:T(8,128)} %param.9) | non-fusion elementwise | flops 1024 | bytes 6144 | tf_op jit(solution)/shard_map/convert_element_type | solution.py:428
  10.2 0.2 collective-permute-start.5
  10.4 0.1 maximum_bitcast_fusion
  10.5 3.7 %collective-permute-done.1 = bf16[2,3,64,128]{3,2,1,0:T(8,128)(2,1)S(1)} collective-permute-done((bf16[2,3,64,128]{3,2,1,0:T(8,128)(2,1)S(1)}, bf16[2,3,64,128]{3,2,1,0:T(8,128)(2,1)S(1)}, u32[]{:S(2)}, u32[]{:S(2)}) %collective-permute-start.1) | collective-permute-done | bytes 98336 | tf_op jit(solution)/shard_map/ppermute | solution.py:425
  14.2 0.6 collective-permute-start.2
  14.8 0.1 stack.19.place_ref
  14.9 0.0 copy-start
  14.9 0.9 %copy-done = bf16[2,8,64,128]{3,2,1,0:T(8,128)(2,1)S(1)} copy-done((bf16[2,8,64,128]{3,2,1,0:T(8,128)(2,1)S(1)}, bf16[2,8,64,128]{3,2,1,0:T(8,128)(2,1)}, u32[]{:S(2)}) %copy-start) | copy-done | bytes 262168
  15.8 1.0 %copy-done.1 = bf16[3,3,3,64,64]{4,3,2,1,0:T(8,128)(2,1)S(1)} copy-done((bf16[3,3,3,64,64]{4,3,2,1,0:T(8,128)(2,1)S(1)}, bf16[3,3,3,64,64]{4,3,2,1,0:T(8,128)(2,1)}, u32[]{:S(2)}) %copy-start.1) | copy-done | bytes 221208
  16.8 0.7 %copy-done.2 = f32[3,64]{1,0:T(4,128)S(1)} copy-done((f32[3,64]{1,0:T(4,128)S(1)}, f32[3,64]{1,0:T(4,128)}, u32[]{:S(2)}) %copy-start.2) | copy-done | bytes 792
  17.5 3.6 %shard_map.64 = (bf16[3,192,192]{2,1,0:T(8,128)(2,1)S(1)}, f32[3,64,1]{2,1,0:T(8,128)S(1)}, bf16[2,512,512]{2,1,0:T(8,128)(2,1)S(1)}, bf16[2,384,512]{2,1,0:T(8,128)(2,1)S(1)}, bf16[2,256,512]{2,1,0:T(8,128)(2,1)S(1)}) custom-call(s32[5]{0:T(128)S(1)} %stack.19.place_ref, bf16[3,3,3,64,64]{4,3,2,1,0:T(8,128)(2,1)S(1)} %copy-done.1, f32[3,64]{1,0:T(4,128)S(1)} %copy-done.2, ...), custom_call_target="tpu_custom_call" | custom-call | flops 2000000000 | bytes 4194304 | tf_op jit(solution)/shard_map/pallas_call | solution.py:442
  21.1 0.0 copy-start.3
  21.1 0.6 collective-permute-start.7
  21.7 1.1 %collective-permute-done.7.refs_5_ = bf16[13,64,128]{2,1,0:T(8,128)(2,1)S(1)} collective-permute-done((bf16[13,64,128]{2,1,0:T(8,128)(2,1)S(1)}, bf16[13,64,128]{2,1,0:T(8,128)(2,1)S(1)}, u32[]{:S(2)}, u32[]{:S(2)}) %collective-permute-start.7) | collective-permute-done | bytes 213024 | tf_op jit(solution)/shard_map/ppermute | solution.py:401
  22.8 10.2 %shard_map.65 = (f32[512,8,128]{2,1,0:T(8,128)S(1)}, bf16[8,128,128]{2,1,0:T(8,128)(2,1)S(1)}) custom-call(s32[5]{0:T(128)S(1)} %stack.19.place_ref, bf16[3,192,192]{2,1,0:T(8,128)(2,1)S(1)} %get-tuple-element.35.taps_ref, f32[3,64,1]{2,1,0:T(8,128)S(1)} %get-tuple-element.36.bias_ref, bf16[2,512,512]{2,1,0:T(8,128)(2,1)S(1)} %get-tuple-element.37.rows_ref, ...), custom_call_target="tpu_custom_call" | custom-call | flops 10000000000 | bytes 4194304 | tf_op jit(solution)/shard_map/pallas_call | solution.py:457
  33.0 3.6 %collective-permute-start.10 = (bf16[8,128,128]{2,1,0:T(8,128)(2,1)S(1)}, bf16[8,128,128]{2,1,0:T(8,128)(2,1)S(1)}, u32[]{:S(2)}, u32[]{:S(2)}) collective-permute-start(bf16[8,128,128]{2,1,0:T(8,128)(2,1)S(1)} %get-tuple-element.44.refs_0_), channel_id=1, source_target_pairs={{0,12},{4,0},{8,4},{12,8},{16,28},{20,16},{24,20},{28,24},{1,13},{... | collective-permute-start | bytes 786440 | tf_op jit(solution)/shard_map/ppermute | solution.py:481
  36.5 0.4 collective-permute-start.9
  37.0 0.2 collective-permute-start.8
  37.2 9.9 %shard_map.66 = (f32[128,8,128]{2,1,0:T(8,128)S(1)}, f32[128,16]{1,0:T(8,128)S(1)}) custom-call(s32[5]{0:T(128)S(1)} %stack.19.place_ref, s32[2]{0:T(128)S(1)} %copy-done.3, f32[512,8,128]{2,1,0:T(8,128)S(1)} %get-tuple-element.42.cost_ref), custom_call_target="tpu_custom_call" | custom-call | flops 10000000000 | bytes 4194304 | tf_op jit(solution)/shard_map/pallas_call | solution.py:488
  47.1 2.1 %collective-permute-done.9.refs_2_ = bf16[8,128,128]{2,1,0:T(8,128)(2,1)S(1)} collective-permute-done((bf16[8,128,128]{2,1,0:T(8,128)(2,1)S(1)}, bf16[8,128,128]{2,1,0:T(8,128)(2,1)S(1)}, u32[]{:S(2)}, u32[]{:S(2)}) %collective-permute-start.9) | collective-permute-done | bytes 262176 | tf_op jit(solution)/shard_map/ppermute | solution.py:481
  49.2 0.0 collective-permute-done.8.refs_1_
  49.2 1.3 %shard_map.67 = (f32[8,128,128]{2,1,0:T(8,128)S(1)}, bf16[128,128]{1,0:T(8,128)(2,1)S(1)}) custom-call(s32[5]{0:T(128)S(1)} %stack.19.place_ref, s32[2]{0:T(128)S(1)} %copy-done.3, bf16[8,128,128]{2,1,0:T(8,128)(2,1)S(1)} %get-tuple-element.44.refs_0_, bf16[8,128,128]{2,1,0:T(8,128)(2,1)S(1)} %collective-permute-done.8.refs_1_, ...), custom_call_target="tpu_custom_call" | custom-call | flops 2000000000 | bytes 4194304 | tf_op jit(solution)/shard_map/pallas_call | solution.py:498
  50.5 2.7 %collective-permute-start.11 = (bf16[128,128]{1,0:T(8,128)(2,1)S(1)}, bf16[128,128]{1,0:T(8,128)(2,1)S(1)}, u32[]{:S(2)}, u32[]{:S(2)}) collective-permute-start(bf16[128,128]{1,0:T(8,128)(2,1)S(1)} %get-tuple-element.51), channel_id=1, source_target_pairs={{0,16},{4,20},{8,24},{12,28},{16,0},{20,4},{24,8},{28,12},{1,17},{... | collective-permute-start | bytes 98312 | tf_op jit(solution)/shard_map/ppermute | solution.py:511
  53.2 10.5 %shard_map.68 = (f32[128,8,128]{2,1,0:T(8,128)S(1)}, f32[128,16]{1,0:T(8,128)}) custom-call(s32[5]{0:T(128)S(1)} %stack.19.place_ref, s32[2]{0:T(128)S(1)} %copy-done.3, f32[512,8,128]{2,1,0:T(8,128)S(1)} %get-tuple-element.42.cost_ref, f32[128,16]{1,0:T(8,128)S(1)} %get-tuple-element.53.refs_0_), custom_call_target="tpu_custom_call" | custom-call | flops 10000000000 | bytes 4194304 | tf_op jit(solution)/shard_map/pallas_call | solution.py:512
  63.7 2.8 %shard_map.69 = f32[8,128,128]{2,1,0:T(8,128)} custom-call(s32[5]{0:T(128)S(1)} %stack.19.place_ref, s32[2]{0:T(128)S(1)} %copy-done.3, bf16[8,128,128]{2,1,0:T(8,128)(2,1)S(1)} %get-tuple-element.44.refs_0_, bf16[8,128,128]{2,1,0:T(8,128)(2,1)S(1)} %collective-permute-done.8.refs_1_, bf16[8,128,128]{2,1,0:T(8,128)(2,1)S(1)} %collective-permute-done.9.refs_2_, ...), custom_call_target="tpu_custom_call" | custom-call | flops 3000000000 | bytes 4194304 | tf_op jit(solution)/shard_map/pallas_call | solution.py:520
  (15 shorter events, 0.1 us)
Async XLA Ops:
  0.0 10.2 %collective-permute-start.3 = (bf16[16,64,128]{2,1,0:T(8,128)(2,1)}, bf16[16,64,128]{2,1,0:T(8,128)(2,1)S(1)}, u32[]{:S(2)}, u32[]{:S(2)}) collective-permute-start(bf16[16,64,128]{2,1,0:T(8,128)(2,1)} %bitcast.10), channel_id=1, source_target_pairs={{0,2},{1,3},{2,0},{3,1},{4,6},{5,7},{6,4},{7,5},{8,10},{9,11},{10,... | collective-permute-start | bytes 786440 | tf_op jit(solution)/shard_map/ppermute | solution.py:401
  3.0 11.9 %collective-permute-start.4 = (bf16[16,64,128]{2,1,0:T(8,128)(2,1)}, bf16[16,64,128]{2,1,0:T(8,128)(2,1)S(1)}, u32[]{:S(2)}, u32[]{:S(2)}) collective-permute-start(bf16[16,64,128]{2,1,0:T(8,128)(2,1)} %bitcast.11), channel_id=1, source_target_pairs={{0,1},{1,0},{2,3},{3,2},{4,5},{5,4},{6,7},{7,6},{8,9},{9,8},{10,11... | collective-permute-start | bytes 786440 | tf_op jit(solution)/shard_map/ppermute | solution.py:401
  3.9 6.5 %collective-permute-start = (bf16[2,3,64,128]{3,2,1,0:T(8,128)(2,1)S(1)}, bf16[2,3,64,128]{3,2,1,0:T(8,128)(2,1)S(1)}, u32[]{:S(2)}, u32[]{:S(2)}) collective-permute-start(bf16[2,3,64,128]{3,2,1,0:T(8,128)(2,1)S(1)} %get-tuple-element.55), channel_id=1, source_target_pairs={{0,4},{4,8},{8,12},{12,16},{16,20},{20,24},{24,28},{1,5},{5,9},{9,... | collective-permute-start | bytes 294920 | tf_op jit(solution)/shard_map/ppermute | solution.py:424
  7.4 6.8 %collective-permute-start.1 = (bf16[2,3,64,128]{3,2,1,0:T(8,128)(2,1)S(1)}, bf16[2,3,64,128]{3,2,1,0:T(8,128)(2,1)S(1)}, u32[]{:S(2)}, u32[]{:S(2)}) collective-permute-start(bf16[2,3,64,128]{3,2,1,0:T(8,128)(2,1)S(1)} %get-tuple-element.56), channel_id=1, source_target_pairs={{4,0},{8,4},{12,8},{16,12},{20,16},{24,20},{28,24},{5,1},{9,5},{13... | collective-permute-start | bytes 294920 | tf_op jit(solution)/shard_map/ppermute | solution.py:425
  10.2 4.7 %collective-permute-start.5 = (bf16[16,64,128]{2,1,0:T(8,128)(2,1)S(1)}, bf16[16,64,128]{2,1,0:T(8,128)(2,1)S(1)}, u32[]{:S(2)}, u32[]{:S(2)}) collective-permute-start(bf16[16,64,128]{2,1,0:T(8,128)(2,1)S(1)} %collective-permute-done.3.refs_1_), channel_id=1, source_target_pairs={{0,1},{1,0},{2,3},{3,2},{4,5},{5,4},{6,7},{7,6},{8,9},{9,8},{10,11... | collective-permute-start | bytes 786440 | tf_op jit(solution)/shard_map/ppermute | solution.py:401
  14.2 6.9 %collective-permute-start.2 = (bf16[13,64,128]{2,1,0:T(8,128)(2,1)S(1)}, bf16[13,64,128]{2,1,0:T(8,128)(2,1)S(1)}, u32[]{:S(2)}, u32[]{:S(2)}) collective-permute-start(bf16[13,64,128]{2,1,0:T(8,128)(2,1)S(1)} %pad_maximum_fusion.refs_2_), channel_id=1, source_target_pairs={{0,2},{1,3},{2,0},{3,1},{4,6},{5,7},{6,4},{7,5},{8,10},{9,11},{10,... | collective-permute-start | bytes 638984 | tf_op jit(solution)/shard_map/ppermute | solution.py:401
  14.8 6.8 %collective-permute-start.6 = (bf16[13,64,128]{2,1,0:T(8,128)(2,1)S(1)}, bf16[13,64,128]{2,1,0:T(8,128)(2,1)S(1)}, u32[]{:S(2)}, u32[]{:S(2)}) collective-permute-start(bf16[13,64,128]{2,1,0:T(8,128)(2,1)S(1)} %pad_maximum_fusion.refs_2_), channel_id=1, source_target_pairs={{0,1},{1,0},{2,3},{3,2},{4,5},{5,4},{6,7},{7,6},{8,9},{9,8},{10,11... | collective-permute-start | bytes 638984 | tf_op jit(solution)/shard_map/ppermute | solution.py:401
  14.9 1.0 %copy-start = (bf16[2,8,64,128]{3,2,1,0:T(8,128)(2,1)S(1)}, bf16[2,8,64,128]{3,2,1,0:T(8,128)(2,1)}, u32[]{:S(2)}) copy-start(bf16[2,8,64,128]{3,2,1,0:T(8,128)(2,1)} %param.6) | copy-start | bytes 786436
  15.8 1.0 %copy-start.1 = (bf16[3,3,3,64,64]{4,3,2,1,0:T(8,128)(2,1)S(1)}, bf16[3,3,3,64,64]{4,3,2,1,0:T(8,128)(2,1)}, u32[]{:S(2)}) copy-start(bf16[3,3,3,64,64]{4,3,2,1,0:T(8,128)(2,1)} %filter_ref.1) | copy-start | bytes 663556
  16.8 0.7 %copy-start.2 = (f32[3,64]{1,0:T(4,128)S(1)}, f32[3,64]{1,0:T(4,128)}, u32[]{:S(2)}) copy-start(f32[3,64]{1,0:T(4,128)} %bias_ref.1) | copy-start | bytes 2308
  21.1 16.1 %copy-start.3 = (s32[2]{0:T(128)S(1)}, s32[2]{0:T(128)}, u32[]{:S(2)}) copy-start(s32[2]{0:T(128)} %charge_ref.7) | copy-start | bytes 28
  21.1 1.6 %collective-permute-start.7 = (bf16[13,64,128]{2,1,0:T(8,128)(2,1)S(1)}, bf16[13,64,128]{2,1,0:T(8,128)(2,1)S(1)}, u32[]{:S(2)}, u32[]{:S(2)}) collective-permute-start(bf16[13,64,128]{2,1,0:T(8,128)(2,1)S(1)} %collective-permute-done.2.refs_3_), channel_id=1, source_target_pairs={{0,1},{1,0},{2,3},{3,2},{4,5},{5,4},{6,7},{7,6},{8,9},{9,8},{10,11... | collective-permute-start | bytes 638984 | tf_op jit(solution)/shard_map/ppermute | solution.py:401
  33.0 14.1 %collective-permute-start.10 = (bf16[8,128,128]{2,1,0:T(8,128)(2,1)S(1)}, bf16[8,128,128]{2,1,0:T(8,128)(2,1)S(1)}, u32[]{:S(2)}, u32[]{:S(2)}) collective-permute-start(bf16[8,128,128]{2,1,0:T(8,128)(2,1)S(1)} %get-tuple-element.44.refs_0_), channel_id=1, source_target_pairs={{0,12},{4,0},{8,4},{12,8},{16,28},{20,16},{24,20},{28,24},{1,13},{... | collective-permute-start | bytes 786440 | tf_op jit(solution)/shard_map/ppermute | solution.py:481
  36.5 12.6 %collective-permute-start.9 = (bf16[8,128,128]{2,1,0:T(8,128)(2,1)S(1)}, bf16[8,128,128]{2,1,0:T(8,128)(2,1)S(1)}, u32[]{:S(2)}, u32[]{:S(2)}) collective-permute-start(bf16[8,128,128]{2,1,0:T(8,128)(2,1)S(1)} %get-tuple-element.44.refs_0_), channel_id=1, source_target_pairs={{0,8},{4,12},{8,0},{12,4},{16,24},{20,28},{24,16},{28,20},{1,9},{5... | collective-permute-start | bytes 786440 | tf_op jit(solution)/shard_map/ppermute | solution.py:481
  37.0 12.2 %collective-permute-start.8 = (bf16[8,128,128]{2,1,0:T(8,128)(2,1)S(1)}, bf16[8,128,128]{2,1,0:T(8,128)(2,1)S(1)}, u32[]{:S(2)}, u32[]{:S(2)}) collective-permute-start(bf16[8,128,128]{2,1,0:T(8,128)(2,1)S(1)} %get-tuple-element.44.refs_0_), channel_id=1, source_target_pairs={{0,4},{4,8},{8,12},{12,0},{16,20},{20,24},{24,28},{28,16},{1,5},{5... | collective-permute-start | bytes 786440 | tf_op jit(solution)/shard_map/ppermute | solution.py:481
  50.5 13.2 %collective-permute-start.11 = (bf16[128,128]{1,0:T(8,128)(2,1)S(1)}, bf16[128,128]{1,0:T(8,128)(2,1)S(1)}, u32[]{:S(2)}, u32[]{:S(2)}) collective-permute-start(bf16[128,128]{1,0:T(8,128)(2,1)S(1)} %get-tuple-element.51), channel_id=1, source_target_pairs={{0,16},{4,20},{8,24},{12,28},{16,0},{20,4},{24,8},{28,12},{1,17},{... | collective-permute-start | bytes 98312 | tf_op jit(solution)/shard_map/ppermute | solution.py:511

commit v3 on v2

--- a/solution.py
+++ b/solution.py
@@ -47,47 +47,6 @@
     return [c + jnp.minimum(t - least, p2) for t, c in zip(stepped(state, p1), cost)]
 
 
-def ends(values, depth):
-    row = lax.broadcasted_iota(jnp.int32, values[0].shape, 0)
-    low = [jnp.where(row == 0, jnp.inf, pltpu.roll(v, 1, 0)) for v in values[-depth:]]
-    high = [jnp.where(row == SUB - 1, jnp.inf, pltpu.roll(v, SUB - 1, 0)) for v in values[:depth]]
-    return low, high
-
-
-def walk(wide, cost, p1):
-    return [
-        c + jnp.minimum(s, jnp.minimum(l, u) + p1)
-        for l, s, u, c in zip(wide[:-2], wide[1:-1], wide[2:], cost)
-    ]
-
-
-def leap(walked, cost, jump):
-    return [jnp.minimum(w, c + jump) for w, c in zip(walked, cost)]
-
-
-def next_jump(walked, cost, jump, p2):
-    cheapest = cost
-    while len(cheapest) > 1:
-        cheapest = [jnp.minimum(a, b) for a, b in zip(cheapest[::2], cheapest[1::2])]
-    cheapest = cheapest[0]
-    for turn in (4, 2, 1):
-        cheapest = jnp.minimum(cheapest, pltpu.roll(cheapest, turn, 0))
-    return jnp.minimum(least_of(walked) + p2, (cheapest + p2) + jump)
-
-
-def advance_pair(wide, jump, first, second, p1, p2):
-    low, high = ends(first, 1)
-    beyond = low + first + high
-    walked = walk(wide, beyond, p1)
-    middle = leap(walked, beyond, jump)
-    jump_between = next_jump(walked[1:-1], first, jump, p2)
-    walked = walk(middle, second, p1)
-    low, high = ends(walked, 2)
-    cost_low, cost_high = ends(second, 2)
-    wide = leap(low + walked + high, cost_low + second + cost_high, jump_between)
-    return wide, middle[1:-1], jump_between, next_jump(walked, second, jump_between, p2)
-
-
 def charges(charge_ref):
     return (
         charge_ref[0].astype(jnp.float32) * (1.0 / 64.0),
@@ -113,14 +72,8 @@
     return max(k for k in range(1, 6) if steps % k == 0)
 
 
-def inner_kernel(masks, place_ref, filter_ref, bias_ref, *refs):
-    parts = len(masks)
-    tile_refs, (taps_ref, shift_ref, own_ref, *hidden_refs) = refs[:parts], refs[parts:]
+def stage_kernel(filter_ref, bias_ref, tile_ref, taps_ref, shift_ref, tile_out):
     layers, _, _, channels, _ = filter_ref.shape
-    width = tile_refs[0].shape[-1]
-    rows = tile_refs[0].shape[0] // 2
-    own = place_ref[2]
-
     one = lax.broadcasted_iota(jnp.int32, (channels, channels), 0)
     two = lax.broadcasted_iota(jnp.int32, (channels, channels), 1)
     for layer in range(layers):
@@ -131,7 +84,15 @@
                 ] = filter_ref[layer, a, b]
         spread_out = jnp.where(one == two, bias_ref[layer : layer + 1, :], 0.0)
         shift_ref[layer] = jnp.sum(spread_out, axis=1, keepdims=True)
-
+    tile_out[...] = tile_ref[...]
+
+
+def inner_kernel(masks, place_ref, taps_ref, shift_ref, *refs):
+    parts = len(masks)
+    tile_refs, (own_ref, *hidden_refs) = refs[:parts], refs[parts:]
+    channels, width = tile_refs[0].shape[1:]
+    rows = tile_refs[0].shape[0] // 2
+    own = place_ref[2]
     for image in range(2):
         for mask, tile_ref in zip(masks, tile_refs):
             there = pl.ds(pl.multiple_of((own ^ mask) * width, width), width)
@@ -276,30 +237,20 @@
         first_step = p * width
 
         def run(keep_right, keep_left, state):
-            def keep(i, values, jump):
-                back = jnp.concatenate([v - (jump - p2) for v in values], axis=0).T
+            def body(i, carry):
+                sums, cost = carry
+                ahead = cost_at(first_step + i + 1)
+                fresh = advance(list(sums), list(cost), p1, p2)
+                if keep_right or keep_left:
+                    back = jnp.concatenate(fresh, axis=0).T
                 if keep_right:
                     kept_ref[i] = back[0:rows]
-                else:
+                if keep_left:
                     kept_ref[width - 1 - i] = back[rows : 2 * rows]
-
-            def body(i, carry):
-                wide, jump, first = carry
-                second = cost_at(first_step + 2 * i + 1)
-                ahead = cost_at(first_step + 2 * i + 2)
-                wide, middle, between, following = advance_pair(
-                    list(wide), jump, list(first), second, p1, p2
-                )
-                if keep_right or keep_left:
-                    keep(2 * i, middle, jump)
-                    keep(2 * i + 1, wide[2:-2], between)
-                return tuple(wide), following, tuple(ahead)
-
-            low, high = ends(list(state), 2)
-            level = jnp.zeros((SUB, 2 * rows), jnp.float32) + p2
-            carry = (tuple(low + list(state) + high), level, tuple(cost_at(first_step)))
-            wide, jump, _ = lax.fori_loop(0, width // 2, body, carry, unroll=8)
-            return tuple(s - (jump - p2) for s in wide[2:-2])
+                return tuple(fresh), tuple(ahead)
+
+            carry = (state, tuple(cost_at(first_step)))
+            return lax.fori_loop(0, width, body, carry, unroll=16)[0]
 
         choice = jnp.where(p == own, 1, 0) + jnp.where(parts - 1 - p == own, 2, 0)
         return lax.switch(
@@ -423,6 +374,21 @@
     upward = [(i + 1, i) for i in range(row_count - 1)]
     before = lax.ppermute(activations[:, rows - layers :], "row", downward)
     after = lax.ppermute(activations[:, :layers], "row", upward)
+    f32, bf16 = jnp.float32, jnp.bfloat16
+    tile = activations.reshape(2 * rows, channels, width)
+    taps, upright, staged = call(
+        stage_kernel,
+        (
+            jax.ShapeDtypeStruct((layers, 3 * channels, 3 * channels), bf16),
+            jax.ShapeDtypeStruct((layers, channels, 1), f32),
+            jax.ShapeDtypeStruct(tile.shape, bf16),
+        ),
+        [VMEM()] * 3,
+        flops=10**8,
+    )(filters, biases, tile)
+    before, after, taps, upright, staged = lax.optimization_barrier(
+        (before, after, taps, upright, staged)
+    )
     extra = jnp.concatenate(
         [
             present.astype(jnp.bfloat16),
@@ -435,24 +401,19 @@
         [before.reshape(-1, channels, width), after.reshape(-1, channels, width), extra[None]],
         axis=0,
     )
-    masks, tiles, _ = spread(activations.reshape(2 * rows, channels, width), parts)
-
-    f32, bf16 = jnp.float32, jnp.bfloat16
+    masks, tiles, _ = spread(tile, parts)
+
     lead = (OFF_MOST + 2 * width - 1) // width * width
     inner = call(
         functools.partial(inner_kernel, masks),
-        (
-            jax.ShapeDtypeStruct((layers, 3 * channels, 3 * channels), bf16),
-            jax.ShapeDtypeStruct((layers, channels, 1), f32),
-            *(
-                jax.ShapeDtypeStruct((2, (rows - 2 * layer) * channels, cols), bf16)
-                for layer in range(layers)
-            ),
+        tuple(
+            jax.ShapeDtypeStruct((2, (rows - 2 * layer) * channels, cols), bf16)
+            for layer in range(layers)
         ),
         [SMEM()] + [VMEM()] * (2 + parts),
         flops=2 * 10**9,
         vmem=32,
-    )(place, filters, biases, *tiles)
+    )(place, taps, upright, staged, *tiles[1:])
     _, edges, inner = spread(edges, parts, inner)
     cost, own = call(
         functools.partial(band_kernel, masks),
@@ -473,7 +434,7 @@
         ],
         flops=10**10,
         vmem=40,
-    )(place, *inner, *edges)
+    )(place, taps, upright, *inner, *edges)
 
     blocks = [own]
     for k in range(1, half):

time: 66.8 us -> 66.1 us (0.990)
  Pallas kernels: 38.2 us -> 36.1 us
  waiting for transfers between devices: 6.92 us -> 8.13 us
    ppermute x6, waiting for transfers between devices: 1.1 us -> 5.08 us  [spread(): blocks += [lax.ppermute(held, 'col', route) for held in blocks]]
    ppermute x1, waiting for transfers between devices: 3.68 us -> 0.01 us  [per_device(): after = lax.ppermute(activations[:, :layers], 'row', upward)]
    ppermute x1, starting transfers between devices: 3.4 us -> 4.55 us  [per_device(): before = lax.ppermute(activations[:, rows - layers:], 'row', downward)]
    pallas_call x1, Pallas kernels: 9.88 us -> 8.77 us  [per_device(): call(functools.partial(across_kernel, False), halves, [SMEM(), SMEM(), VM...]
    pallas_call x1, Pallas kernels: 10.5 us -> 9.41 us  [per_device(): call(functools.partial(across_kernel, True), halves, [SMEM(), SMEM(), VME...]
    ppermute x3, waiting for transfers between devices: 2.13 us -> 3.05 us  [per_device(): blocks.append(lax.ppermute(own, 'row', turn))]
    ppermute x6, starting transfers between devices: 4.3 us -> 3.58 us  [spread(): blocks += [lax.ppermute(held, 'col', route) for held in blocks]]
    pallas_call x1 -> x2, Pallas kernels: 3.57 us -> 3.65 us  [the longest x1 3.41 us: per_device(): call(functools.partial(inner_kernel, masks), tuple((jax.ShapeDtypeStruct(...]
  transfers between devices with their start and end apart: 12 -> 12, of which waited for: 3 -> 3; matrix products, arithmetic and copies ran while one was open for 3% -> 3% of each run, Pallas kernels for 36% -> 33%
where the time goes in v3:
time: 66.1 us; the launch traced here: 65.8 us
  Pallas kernels  36.1 us (55%)
  starting transfers between devices  16.2 us (25%)
  waiting for transfers between devices  8.13 us (12%)
  local copies, waits for them, and re-layouts  3.86 us (6%)
  other arithmetic  0.8 us (1%)
  between operations  0.78 us (1%)
    pallas_call x1, Pallas kernels, per_device(): call(functools.partial(band_kernel, masks), (jax.ShapeDtypeStruct((cols,...  10.2 us
    pallas_call x1, Pallas kernels, per_device(): call(functools.partial(across_kernel, True), halves, [SMEM(), SMEM(), VME...  9.41 us
    pallas_call x1, Pallas kernels, per_device(): call(functools.partial(across_kernel, False), halves, [SMEM(), SMEM(), VM...  8.77 us
    ppermute x6, waiting for transfers between devices, spread(): blocks += [lax.ppermute(held, 'col', route) for held in blocks]  5.08 us
    ppermute x1, starting transfers between devices, per_device(): before = lax.ppermute(activations[:, rows - layers:], 'row', downward)  4.55 us
    ppermute x3, starting transfers between devices, per_device(): blocks.append(lax.ppermute(own, 'row', turn))  4.09 us
    ppermute x6, starting transfers between devices, spread(): blocks += [lax.ppermute(held, 'col', route) for held in blocks]  3.58 us
    pallas_call x1, Pallas kernels, per_device(): call(functools.partial(inner_kernel, masks), tuple((jax.ShapeDtypeStruct(...  3.41 us
  transfers between devices with their start and end apart: 12, of which 3 were waited for; matrix products, arithmetic and copies ran while one was open for 3% of the time, Pallas kernels for 33%

profile of v3, /device:TPU:0, one launch (start us, length us, event | category | flops | bytes accessed | tf_op | source)
XLA Modules:
  0.0 65.8 jit_solution(14177338724502735921)
XLA Ops:
  0.0 3.0 %collective-permute-start.3 = (bf16[16,64,128]{2,1,0:T(8,128)(2,1)}, bf16[16,64,128]{2,1,0:T(8,128)(2,1)S(1)}, u32[]{:S(2)}, u32[]{:S(2)}) collective-permute-start(bf16[16,64,128]{2,1,0:T(8,128)(2,1)} %bitcast.10), channel_id=1, source_target_pairs={{0,2},{1,3},{2,0},{3,1},{4,6},{5,7},{6,4},{7,5},{8,10},{9,11},{10,... | collective-permute-start | bytes 786440 | tf_op jit(solution)/shard_map/ppermute | solution.py:352
  3.0 0.0 collective-permute-start.4
  3.0 1.0 %fusion = (bf16[2,3,64,128]{3,2,1,0:T(8,128)(2,1)S(1)}, bf16[2,3,64,128]{3,2,1,0:T(8,128)(2,1)S(1)}) fusion(bf16[2,8,64,128]{3,2,1,0:T(8,128)(2,1)} %param.6), kind=kLoop, calls=%fused_computation.2 | loop fusion | bytes 393216 | tf_op jit(solution)/shard_map/slice | solution.py:376
  3.9 1.3 %collective-permute-start.1 = (bf16[2,3,64,128]{3,2,1,0:T(8,128)(2,1)S(1)}, bf16[2,3,64,128]{3,2,1,0:T(8,128)(2,1)S(1)}, u32[]{:S(2)}, u32[]{:S(2)}) collective-permute-start(bf16[2,3,64,128]{3,2,1,0:T(8,128)(2,1)S(1)} %get-tuple-element.63), channel_id=1, source_target_pairs={{4,0},{8,4},{12,8},{16,12},{20,16},{24,20},{28,24},{5,1},{9,5},{13... | collective-permute-start | bytes 294920 | tf_op jit(solution)/shard_map/ppermute | solution.py:376
  5.2 4.6 %collective-permute-start = (bf16[2,3,64,128]{3,2,1,0:T(8,128)(2,1)S(1)}, bf16[2,3,64,128]{3,2,1,0:T(8,128)(2,1)S(1)}, u32[]{:S(2)}, u32[]{:S(2)}) collective-permute-start(bf16[2,3,64,128]{3,2,1,0:T(8,128)(2,1)S(1)} %get-tuple-element.64), channel_id=1, source_target_pairs={{0,4},{4,8},{8,12},{12,16},{16,20},{20,24},{24,28},{1,5},{5,9},{9,... | collective-permute-start | bytes 294920 | tf_op jit(solution)/shard_map/ppermute | solution.py:375
  10.5 0.1 pad.5.clone
  10.6 0.1 pad.4.clone
  10.6 0.7 %convert_element_type.6 = bf16[8,128]{1,0:T(8,128)(2,1)S(1)} convert(s32[8,128]{1,0:T(8,128)} %param.9) | non-fusion elementwise | flops 1024 | bytes 6144 | tf_op jit(solution)/shard_map/convert_element_type | solution.py:394
  11.3 0.0 collective-permute-done.3.refs_1_
  11.3 0.1 maximum_bitcast_fusion
  11.4 0.0 copy-start
  11.4 0.9 %copy-done = bf16[2,8,64,128]{3,2,1,0:T(8,128)(2,1)S(1)} copy-done((bf16[2,8,64,128]{3,2,1,0:T(8,128)(2,1)S(1)}, bf16[2,8,64,128]{3,2,1,0:T(8,128)(2,1)}, u32[]{:S(2)}) %copy-start) | copy-done | bytes 262168
  12.4 1.0 %copy-done.1 = bf16[3,3,3,64,64]{4,3,2,1,0:T(8,128)(2,1)S(1)} copy-done((bf16[3,3,3,64,64]{4,3,2,1,0:T(8,128)(2,1)S(1)}, bf16[3,3,3,64,64]{4,3,2,1,0:T(8,128)(2,1)}, u32[]{:S(2)}) %copy-start.1) | copy-done | bytes 221208
  13.4 0.7 %copy-done.2 = f32[3,64]{1,0:T(4,128)S(1)} copy-done((f32[3,64]{1,0:T(4,128)S(1)}, f32[3,64]{1,0:T(4,128)}, u32[]{:S(2)}) %copy-start.2) | copy-done | bytes 792
  14.1 0.2 shard_map.64
  14.4 0.3 collective-permute-start.2
  14.6 0.1 stack.19.place_ref
  14.7 0.4 collective-permute-start.6
  15.1 3.4 %shard_map.65 = (bf16[2,512,512]{2,1,0:T(8,128)(2,1)S(1)}, bf16[2,384,512]{2,1,0:T(8,128)(2,1)S(1)}, bf16[2,256,512]{2,1,0:T(8,128)(2,1)S(1)}) custom-call(s32[5]{0:T(128)S(1)} %stack.19.place_ref, bf16[3,192,192]{2,1,0:T(8,128)(2,1)S(1)} %get-tuple-element.37.taps_ref, f32[3,64,1]{2,1,0:T(8,128)S(1)} %get-tuple-element.38.shift_ref.bias_ref, ...), custom_call_target="tpu_custom_call" | custom-call | flops 2000000000 | bytes 4194304 | tf_op jit(solution)/shard_map/pallas_call | solution.py:407
  18.5 3.6 %collective-permute-done.2.refs_3_ = bf16[13,64,128]{2,1,0:T(8,128)(2,1)S(1)} collective-permute-done((bf16[13,64,128]{2,1,0:T(8,128)(2,1)S(1)}, bf16[13,64,128]{2,1,0:T(8,128)(2,1)S(1)}, u32[]{:S(2)}, u32[]{:S(2)}) %collective-permute-start.2) | collective-permute-done | bytes 213024 | tf_op jit(solution)/shard_map/ppermute | solution.py:352
  22.1 1.5 %collective-permute-done.7.refs_5_ = bf16[13,64,128]{2,1,0:T(8,128)(2,1)S(1)} collective-permute-done((bf16[13,64,128]{2,1,0:T(8,128)(2,1)S(1)}, bf16[13,64,128]{2,1,0:T(8,128)(2,1)S(1)}, u32[]{:S(2)}, u32[]{:S(2)}) %collective-permute-start.7) | collective-permute-done | bytes 213024 | tf_op jit(solution)/shard_map/ppermute | solution.py:352
  23.6 10.2 %shard_map.66 = (f32[512,8,128]{2,1,0:T(8,128)S(1)}, bf16[8,128,128]{2,1,0:T(8,128)(2,1)S(1)}) custom-call(s32[5]{0:T(128)S(1)} %stack.19.place_ref, bf16[3,192,192]{2,1,0:T(8,128)(2,1)S(1)} %get-tuple-element.37.taps_ref, f32[3,64,1]{2,1,0:T(8,128)S(1)} %get-tuple-element.38.shift_ref.bias_ref, bf16[2,512,512]{2,1,0:T(8,128)(2,1)S(1)} %get-tuple-element.45.rows_ref, ...), custom_call_target="tpu_custom_call" | custom-call | flops 10000000000 | bytes 4194304 | tf_op jit(solution)/shard_map/pallas_call | solution.py:418
  33.8 3.4 %collective-permute-start.10 = (bf16[8,128,128]{2,1,0:T(8,128)(2,1)S(1)}, bf16[8,128,128]{2,1,0:T(8,128)(2,1)S(1)}, u32[]{:S(2)}, u32[]{:S(2)}) collective-permute-start(bf16[8,128,128]{2,1,0:T(8,128)(2,1)S(1)} %get-tuple-element.52.refs_0_), channel_id=1, source_target_pairs={{0,12},{4,0},{8,4},{12,8},{16,28},{20,16},{24,20},{28,24},{1,13},{... | collective-permute-start | bytes 786440 | tf_op jit(solution)/shard_map/ppermute | solution.py:442
  37.2 0.5 collective-permute-start.9
  37.7 0.2 collective-permute-start.8
  37.9 8.8 %shard_map.67 = (f32[128,8,128]{2,1,0:T(8,128)S(1)}, f32[128,16]{1,0:T(8,128)S(1)}) custom-call(s32[5]{0:T(128)S(1)} %stack.19.place_ref, s32[2]{0:T(128)S(1)} %copy-done.3, f32[512,8,128]{2,1,0:T(8,128)S(1)} %get-tuple-element.50.cost_ref), custom_call_target="tpu_custom_call" | custom-call | flops 10000000000 | bytes 4194304 | tf_op jit(solution)/shard_map/pallas_call | solution.py:449
  46.7 3.0 %collective-permute-done.9.refs_2_ = bf16[8,128,128]{2,1,0:T(8,128)(2,1)S(1)} collective-permute-done((bf16[8,128,128]{2,1,0:T(8,128)(2,1)S(1)}, bf16[8,128,128]{2,1,0:T(8,128)(2,1)S(1)}, u32[]{:S(2)}, u32[]{:S(2)}) %collective-permute-start.9) | collective-permute-done | bytes 262176 | tf_op jit(solution)/shard_map/ppermute | solution.py:442
  49.7 0.0 collective-permute-done.8.refs_1_
  49.7 1.3 %shard_map.68 = (f32[8,128,128]{2,1,0:T(8,128)S(1)}, bf16[128,128]{1,0:T(8,128)(2,1)S(1)}) custom-call(s32[5]{0:T(128)S(1)} %stack.19.place_ref, s32[2]{0:T(128)S(1)} %copy-done.3, bf16[8,128,128]{2,1,0:T(8,128)(2,1)S(1)} %get-tuple-element.52.refs_0_, bf16[8,128,128]{2,1,0:T(8,128)(2,1)S(1)} %collective-permute-done.8.refs_1_, ...), custom_call_target="tpu_custom_call" | custom-call | flops 2000000000 | bytes 4194304 | tf_op jit(solution)/shard_map/pallas_call | solution.py:459
  51.0 2.7 %collective-permute-start.11 = (bf16[128,128]{1,0:T(8,128)(2,1)S(1)}, bf16[128,128]{1,0:T(8,128)(2,1)S(1)}, u32[]{:S(2)}, u32[]{:S(2)}) collective-permute-start(bf16[128,128]{1,0:T(8,128)(2,1)S(1)} %get-tuple-element.59), channel_id=1, source_target_pairs={{0,16},{4,20},{8,24},{12,28},{16,0},{20,4},{24,8},{28,12},{1,17},{... | collective-permute-start | bytes 98312 | tf_op jit(solution)/shard_map/ppermute | solution.py:472
  53.7 9.4 %shard_map.69 = (f32[128,8,128]{2,1,0:T(8,128)S(1)}, f32[128,16]{1,0:T(8,128)}) custom-call(s32[5]{0:T(128)S(1)} %stack.19.place_ref, s32[2]{0:T(128)S(1)} %copy-done.3, f32[512,8,128]{2,1,0:T(8,128)S(1)} %get-tuple-element.50.cost_ref, f32[128,16]{1,0:T(8,128)S(1)} %get-tuple-element.61.refs_0_), custom_call_target="tpu_custom_call" | custom-call | flops 10000000000 | bytes 4194304 | tf_op jit(solution)/shard_map/pallas_call | solution.py:473
  63.1 2.7 %shard_map.70 = f32[8,128,128]{2,1,0:T(8,128)} custom-call(s32[5]{0:T(128)S(1)} %stack.19.place_ref, s32[2]{0:T(128)S(1)} %copy-done.3, bf16[8,128,128]{2,1,0:T(8,128)(2,1)S(1)} %get-tuple-element.52.refs_0_, bf16[8,128,128]{2,1,0:T(8,128)(2,1)S(1)} %collective-permute-done.8.refs_1_, bf16[8,128,128]{2,1,0:T(8,128)(2,1)S(1)} %collective-permute-done.9.refs_2_, ...), custom_call_target="tpu_custom_call" | custom-call | flops 3000000000 | bytes 4194304 | tf_op jit(solution)/shard_map/pallas_call | solution.py:481
  (16 shorter events, 0.1 us)
Async XLA Ops:
  0.0 11.3 %collective-permute-start.3 = (bf16[16,64,128]{2,1,0:T(8,128)(2,1)}, bf16[16,64,128]{2,1,0:T(8,128)(2,1)S(1)}, u32[]{:S(2)}, u32[]{:S(2)}) collective-permute-start(bf16[16,64,128]{2,1,0:T(8,128)(2,1)} %bitcast.10), channel_id=1, source_target_pairs={{0,2},{1,3},{2,0},{3,1},{4,6},{5,7},{6,4},{7,5},{8,10},{9,11},{10,... | collective-permute-start | bytes 786440 | tf_op jit(solution)/shard_map/ppermute | solution.py:352
  3.0 12.1 %collective-permute-start.4 = (bf16[16,64,128]{2,1,0:T(8,128)(2,1)}, bf16[16,64,128]{2,1,0:T(8,128)(2,1)S(1)}, u32[]{:S(2)}, u32[]{:S(2)}) collective-permute-start(bf16[16,64,128]{2,1,0:T(8,128)(2,1)} %bitcast.11), channel_id=1, source_target_pairs={{0,1},{1,0},{2,3},{3,2},{4,5},{5,4},{6,7},{7,6},{8,9},{9,8},{10,11... | collective-permute-start | bytes 786440 | tf_op jit(solution)/shard_map/ppermute | solution.py:352
  3.9 10.4 %collective-permute-start.1 = (bf16[2,3,64,128]{3,2,1,0:T(8,128)(2,1)S(1)}, bf16[2,3,64,128]{3,2,1,0:T(8,128)(2,1)S(1)}, u32[]{:S(2)}, u32[]{:S(2)}) collective-permute-start(bf16[2,3,64,128]{3,2,1,0:T(8,128)(2,1)S(1)} %get-tuple-element.63), channel_id=1, source_target_pairs={{4,0},{8,4},{12,8},{16,12},{20,16},{24,20},{28,24},{5,1},{9,5},{13... | collective-permute-start | bytes 294920 | tf_op jit(solution)/shard_map/ppermute | solution.py:376
  5.2 9.1 %collective-permute-start = (bf16[2,3,64,128]{3,2,1,0:T(8,128)(2,1)S(1)}, bf16[2,3,64,128]{3,2,1,0:T(8,128)(2,1)S(1)}, u32[]{:S(2)}, u32[]{:S(2)}) collective-permute-start(bf16[2,3,64,128]{3,2,1,0:T(8,128)(2,1)S(1)} %get-tuple-element.64), channel_id=1, source_target_pairs={{0,4},{4,8},{8,12},{12,16},{16,20},{20,24},{24,28},{1,5},{5,9},{9,... | collective-permute-start | bytes 294920 | tf_op jit(solution)/shard_map/ppermute | solution.py:375
  11.3 3.7 %collective-permute-start.5 = (bf16[16,64,128]{2,1,0:T(8,128)(2,1)S(1)}, bf16[16,64,128]{2,1,0:T(8,128)(2,1)S(1)}, u32[]{:S(2)}, u32[]{:S(2)}) collective-permute-start(bf16[16,64,128]{2,1,0:T(8,128)(2,1)S(1)} %collective-permute-done.3.refs_1_), channel_id=1, source_target_pairs={{0,1},{1,0},{2,3},{3,2},{4,5},{5,4},{6,7},{7,6},{8,9},{9,8},{10,11... | collective-permute-start | bytes 786440 | tf_op jit(solution)/shard_map/ppermute | solution.py:352
  11.4 1.0 %copy-start = (bf16[2,8,64,128]{3,2,1,0:T(8,128)(2,1)S(1)}, bf16[2,8,64,128]{3,2,1,0:T(8,128)(2,1)}, u32[]{:S(2)}) copy-start(bf16[2,8,64,128]{3,2,1,0:T(8,128)(2,1)} %param.6) | copy-start | bytes 786436
  12.4 1.0 %copy-start.1 = (bf16[3,3,3,64,64]{4,3,2,1,0:T(8,128)(2,1)S(1)}, bf16[3,3,3,64,64]{4,3,2,1,0:T(8,128)(2,1)}, u32[]{:S(2)}) copy-start(bf16[3,3,3,64,64]{4,3,2,1,0:T(8,128)(2,1)} %filter_ref.1) | copy-start | bytes 663556
  13.4 0.7 %copy-start.2 = (f32[3,64]{1,0:T(4,128)S(1)}, f32[3,64]{1,0:T(4,128)}, u32[]{:S(2)}) copy-start(f32[3,64]{1,0:T(4,128)} %bias_ref.1) | copy-start | bytes 2308
  14.4 7.7 %collective-permute-start.2 = (bf16[13,64,128]{2,1,0:T(8,128)(2,1)S(1)}, bf16[13,64,128]{2,1,0:T(8,128)(2,1)S(1)}, u32[]{:S(2)}, u32[]{:S(2)}) collective-permute-start(bf16[13,64,128]{2,1,0:T(8,128)(2,1)S(1)} %pad_maximum_fusion.refs_2_), channel_id=1, source_target_pairs={{0,2},{1,3},{2,0},{3,1},{4,6},{5,7},{6,4},{7,5},{8,10},{9,11},{10,... | collective-permute-start | bytes 638984 | tf_op jit(solution)/shard_map/ppermute | solution.py:352
  14.7 7.4 %collective-permute-start.6 = (bf16[13,64,128]{2,1,0:T(8,128)(2,1)S(1)}, bf16[13,64,128]{2,1,0:T(8,128)(2,1)S(1)}, u32[]{:S(2)}, u32[]{:S(2)}) collective-permute-start(bf16[13,64,128]{2,1,0:T(8,128)(2,1)S(1)} %pad_maximum_fusion.refs_2_), channel_id=1, source_target_pairs={{0,1},{1,0},{2,3},{3,2},{4,5},{5,4},{6,7},{7,6},{8,9},{9,8},{10,11... | collective-permute-start | bytes 638984 | tf_op jit(solution)/shard_map/ppermute | solution.py:352
  22.1 15.8 %copy-start.3 = (s32[2]{0:T(128)S(1)}, s32[2]{0:T(128)}, u32[]{:S(2)}) copy-start(s32[2]{0:T(128)} %charge_ref.7) | copy-start | bytes 28
  22.1 1.5 %collective-permute-start.7 = (bf16[13,64,128]{2,1,0:T(8,128)(2,1)S(1)}, bf16[13,64,128]{2,1,0:T(8,128)(2,1)S(1)}, u32[]{:S(2)}, u32[]{:S(2)}) collective-permute-start(bf16[13,64,128]{2,1,0:T(8,128)(2,1)S(1)} %collective-permute-done.2.refs_3_), channel_id=1, source_target_pairs={{0,1},{1,0},{2,3},{3,2},{4,5},{5,4},{6,7},{7,6},{8,9},{9,8},{10,11... | collective-permute-start | bytes 638984 | tf_op jit(solution)/shard_map/ppermute | solution.py:352
  33.8 12.9 %collective-permute-start.10 = (bf16[8,128,128]{2,1,0:T(8,128)(2,1)S(1)}, bf16[8,128,128]{2,1,0:T(8,128)(2,1)S(1)}, u32[]{:S(2)}, u32[]{:S(2)}) collective-permute-start(bf16[8,128,128]{2,1,0:T(8,128)(2,1)S(1)} %get-tuple-element.52.refs_0_), channel_id=1, source_target_pairs={{0,12},{4,0},{8,4},{12,8},{16,28},{20,16},{24,20},{28,24},{1,13},{... | collective-permute-start | bytes 786440 | tf_op jit(solution)/shard_map/ppermute | solution.py:442
  37.2 12.4 %collective-permute-start.9 = (bf16[8,128,128]{2,1,0:T(8,128)(2,1)S(1)}, bf16[8,128,128]{2,1,0:T(8,128)(2,1)S(1)}, u32[]{:S(2)}, u32[]{:S(2)}) collective-permute-start(bf16[8,128,128]{2,1,0:T(8,128)(2,1)S(1)} %get-tuple-element.52.refs_0_), channel_id=1, source_target_pairs={{0,8},{4,12},{8,0},{12,4},{16,24},{20,28},{24,16},{28,20},{1,9},{5... | collective-permute-start | bytes 786440 | tf_op jit(solution)/shard_map/ppermute | solution.py:442
  37.7 12.0 %collective-permute-start.8 = (bf16[8,128,128]{2,1,0:T(8,128)(2,1)S(1)}, bf16[8,128,128]{2,1,0:T(8,128)(2,1)S(1)}, u32[]{:S(2)}, u32[]{:S(2)}) collective-permute-start(bf16[8,128,128]{2,1,0:T(8,128)(2,1)S(1)} %get-tuple-element.52.refs_0_), channel_id=1, source_target_pairs={{0,4},{4,8},{8,12},{12,0},{16,20},{20,24},{24,28},{28,16},{1,5},{5... | collective-permute-start | bytes 786440 | tf_op jit(solution)/shard_map/ppermute | solution.py:442
  51.0 12.1 %collective-permute-start.11 = (bf16[128,128]{1,0:T(8,128)(2,1)S(1)}, bf16[128,128]{1,0:T(8,128)(2,1)S(1)}, u32[]{:S(2)}, u32[]{:S(2)}) collective-permute-start(bf16[128,128]{1,0:T(8,128)(2,1)S(1)} %get-tuple-element.59), channel_id=1, source_target_pairs={{0,16},{4,20},{8,24},{12,28},{16,0},{20,4},{24,8},{28,12},{1,17},{... | collective-permute-start | bytes 98312 | tf_op jit(solution)/shard_map/ppermute | solution.py:472

commit v4 on v3

--- a/solution.py
+++ b/solution.py
@@ -206,11 +206,16 @@
         pl.when(p != own)(functools.partial(tile_costs, False))
 
 
+def early_segments(parts):
+    return parts - parts // 4
+
+
 def across_kernel(second, place_ref, charge_ref, cost_ref, *refs):
     kept_ref, last_ref, same_ref = refs[-3:]
     cols = cost_ref.shape[0]
-    width, rows, _ = kept_ref.shape
+    _, width, rows, _ = kept_ref.shape
     parts = cols // width
+    early = early_segments(parts)
     own = place_ref[2]
     p1, p2 = charges(charge_ref)
 
@@ -240,17 +245,23 @@
             def body(i, carry):
                 sums, cost = carry
                 ahead = cost_at(first_step + i + 1)
-                fresh = advance(list(sums), list(cost), p1, p2)
+                least = least_of(list(sums))
+                jump = least + p2
+                fresh = [
+                    c + jnp.minimum(t, jump) for t, c in zip(stepped(list(sums), p1), cost)
+                ]
                 if keep_right or keep_left:
-                    back = jnp.concatenate(fresh, axis=0).T
+                    back = jnp.concatenate([f - least for f in fresh], axis=0).T
                 if keep_right:
-                    kept_ref[i] = back[0:rows]
+                    kept_ref[0, i] = back[0:rows]
                 if keep_left:
-                    kept_ref[width - 1 - i] = back[rows : 2 * rows]
+                    kept_ref[1, width - 1 - i] = back[rows : 2 * rows]
                 return tuple(fresh), tuple(ahead)
 
             carry = (state, tuple(cost_at(first_step)))
-            return lax.fori_loop(0, width, body, carry, unroll=16)[0]
+            sums = lax.fori_loop(0, width, body, carry, unroll=16)[0]
+            least = least_of(list(sums))
+            return tuple(s - least for s in sums)
 
         choice = jnp.where(p == own, 1, 0) + jnp.where(parts - 1 - p == own, 2, 0)
         return lax.switch(
@@ -261,10 +272,10 @@
 
     if second:
         state = tuple(registers(refs[0][...]))
-        span = (parts // 2, parts)
+        span = (early, parts)
     else:
         state = tuple(jnp.zeros((SUB, 2 * rows), jnp.float32) for _ in range(REGS))
-        span = (0, parts // 2)
+        span = (0, early)
     last_ref[...] = jnp.concatenate(lax.fori_loop(*span, segment, state), axis=0)
 
 
@@ -323,8 +334,12 @@
     down_or_up(place_ref[3] != 0, place_ref[4], cost_ref, state, p1, p2, keep)
     lane = lax.broadcasted_iota(jnp.int32, (width, DISPARITIES), 1)
     index = disparity_to_lane(lane)
+    right_early = place_ref[2] < place_ref[6]
+    left_early = place_ref[5] - 1 - place_ref[2] < place_ref[6]
     for row in range(rows):
-        value = total[row].T + (early_ref[:, row, :] + late_ref[:, row, :])
+        right = jnp.where(right_early, early_ref[0, :, row, :], late_ref[0, :, row, :])
+        left = jnp.where(left_early, early_ref[1, :, row, :], late_ref[1, :, row, :])
+        value = total[row].T + (right + left)
         out_ref[row] = jnp.take_along_axis(value, index, axis=1, mode="promise_in_bounds")
 
 
@@ -367,7 +382,15 @@
     half = row_count // 2
     cols = parts * width
     place = jnp.stack(
-        [row_rank, jnp.int32(row_count), col_rank, row_rank // half, row_rank % half]
+        [
+            row_rank,
+            jnp.int32(row_count),
+            col_rank,
+            row_rank // half,
+            row_rank % half,
+            jnp.int32(parts),
+            jnp.int32(early_segments(parts)),
+        ]
     ).astype(jnp.int32)
 
     downward = [(i, i + 1) for i in range(row_count - 1)]
@@ -442,7 +465,7 @@
         blocks.append(lax.ppermute(own, "row", turn))
 
     halves = (
-        jax.ShapeDtypeStruct((width, rows, DISPARITIES), f32),
+        jax.ShapeDtypeStruct((2, width, rows, DISPARITIES), f32),
         jax.ShapeDtypeStruct((DISPARITIES, 2 * rows), f32),
     )
     identity = [pltpu.VMEM((DISPARITIES, 2 * DISPARITIES), bf16)]

time: 66.1 us -> 63.3 us (0.958)
  waiting for transfers between devices: 8.13 us -> 5.09 us
    pallas_call x1, Pallas kernels: 9.41 us -> 5.6 us  [per_device(): call(functools.partial(across_kernel, True), halves, [SMEM(), SMEM(), VME...]
    pallas_call x1, Pallas kernels: 8.77 us -> 12.5 us  [per_device(): call(functools.partial(across_kernel, False), halves, [SMEM(), SMEM(), VM...]
    ppermute x3, waiting for transfers between devices: 3.05 us -> 0.01 us  [per_device(): blocks.append(lax.ppermute(own, 'row', turn))]
  transfers between devices with their start and end apart: 12 -> 12, of which waited for: 3 -> 2; matrix products, arithmetic and copies ran while one was open for 3% -> 3% of each run, Pallas kernels for 33% -> 35%
where the time goes in v4:
time: 63.3 us; the launch traced here: 63 us
  Pallas kernels  36.4 us (58%)
  starting transfers between devices  16 us (25%)
  waiting for transfers between devices  5.09 us (8%)
  local copies, waits for them, and re-layouts  3.86 us (6%)
  other arithmetic  0.8 us (1%)
  between operations  0.79 us (1%)
    pallas_call x1, Pallas kernels, per_device(): call(functools.partial(across_kernel, False), halves, [SMEM(), SMEM(), VM...  12.5 us
    pallas_call x1, Pallas kernels, per_device(): call(functools.partial(band_kernel, masks), (jax.ShapeDtypeStruct((cols,...  10.2 us
    pallas_call x1, Pallas kernels, per_device(): call(functools.partial(across_kernel, True), halves, [SMEM(), SMEM(), VME...  5.6 us
    ppermute x6, waiting for transfers between devices, spread(): blocks += [lax.ppermute(held, 'col', route) for held in blocks]  5.08 us
    ppermute x1, starting transfers between devices, per_device(): before = lax.ppermute(activations[:, rows - layers:], 'row', downward)  4.55 us
    ppermute x3, starting transfers between devices, per_device(): blocks.append(lax.ppermute(own, 'row', turn))  4.09 us
    ppermute x6, starting transfers between devices, spread(): blocks += [lax.ppermute(held, 'col', route) for held in blocks]  3.58 us
    pallas_call x1, Pallas kernels, per_device(): call(functools.partial(inner_kernel, masks), tuple((jax.ShapeDtypeStruct(...  3.41 us
  transfers between devices with their start and end apart: 12, of which 2 were waited for; matrix products, arithmetic and copies ran while one was open for 3% of the time, Pallas kernels for 35%

profile of v4, /device:TPU:0, one launch (start us, length us, event | category | flops | bytes accessed | tf_op | source)
XLA Modules:
  0.0 63.0 jit_solution(6650146599373918899)
XLA Ops:
  0.0 3.0 %collective-permute-start.3 = (bf16[16,64,128]{2,1,0:T(8,128)(2,1)}, bf16[16,64,128]{2,1,0:T(8,128)(2,1)S(1)}, u32[]{:S(2)}, u32[]{:S(2)}) collective-permute-start(bf16[16,64,128]{2,1,0:T(8,128)(2,1)} %bitcast.10), channel_id=1, source_target_pairs={{0,2},{1,3},{2,0},{3,1},{4,6},{5,7},{6,4},{7,5},{8,10},{9,11},{10,... | collective-permute-start | bytes 786440 | tf_op jit(solution)/shard_map/ppermute | solution.py:367
  3.0 0.0 collective-permute-start.4
  3.0 1.0 %fusion = (bf16[2,3,64,128]{3,2,1,0:T(8,128)(2,1)S(1)}, bf16[2,3,64,128]{3,2,1,0:T(8,128)(2,1)S(1)}) fusion(bf16[2,8,64,128]{3,2,1,0:T(8,128)(2,1)} %param.6), kind=kLoop, calls=%fused_computation.2 | loop fusion | bytes 393216 | tf_op jit(solution)/shard_map/slice | solution.py:399
  3.9 1.3 %collective-permute-start.1 = (bf16[2,3,64,128]{3,2,1,0:T(8,128)(2,1)S(1)}, bf16[2,3,64,128]{3,2,1,0:T(8,128)(2,1)S(1)}, u32[]{:S(2)}, u32[]{:S(2)}) collective-permute-start(bf16[2,3,64,128]{3,2,1,0:T(8,128)(2,1)S(1)} %get-tuple-element.63), channel_id=1, source_target_pairs={{4,0},{8,4},{12,8},{16,12},{20,16},{24,20},{28,24},{5,1},{9,5},{13... | collective-permute-start | bytes 294920 | tf_op jit(solution)/shard_map/ppermute | solution.py:399
  5.2 4.6 %collective-permute-start = (bf16[2,3,64,128]{3,2,1,0:T(8,128)(2,1)S(1)}, bf16[2,3,64,128]{3,2,1,0:T(8,128)(2,1)S(1)}, u32[]{:S(2)}, u32[]{:S(2)}) collective-permute-start(bf16[2,3,64,128]{3,2,1,0:T(8,128)(2,1)S(1)} %get-tuple-element.64), channel_id=1, source_target_pairs={{0,4},{4,8},{8,12},{12,16},{16,20},{20,24},{24,28},{1,5},{5,9},{9,... | collective-permute-start | bytes 294920 | tf_op jit(solution)/shard_map/ppermute | solution.py:398
  10.5 0.1 pad.5.clone
  10.6 0.1 pad.4.clone
  10.6 0.7 %convert_element_type.6 = bf16[8,128]{1,0:T(8,128)(2,1)S(1)} convert(s32[8,128]{1,0:T(8,128)} %param.9) | non-fusion elementwise | flops 1024 | bytes 6144 | tf_op jit(solution)/shard_map/convert_element_type | solution.py:417
  11.3 0.1 maximum_bitcast_fusion
  11.4 0.0 copy-start
  11.4 0.9 %copy-done = bf16[2,8,64,128]{3,2,1,0:T(8,128)(2,1)S(1)} copy-done((bf16[2,8,64,128]{3,2,1,0:T(8,128)(2,1)S(1)}, bf16[2,8,64,128]{3,2,1,0:T(8,128)(2,1)}, u32[]{:S(2)}) %copy-start) | copy-done | bytes 262168
  12.4 1.0 %copy-done.1 = bf16[3,3,3,64,64]{4,3,2,1,0:T(8,128)(2,1)S(1)} copy-done((bf16[3,3,3,64,64]{4,3,2,1,0:T(8,128)(2,1)S(1)}, bf16[3,3,3,64,64]{4,3,2,1,0:T(8,128)(2,1)}, u32[]{:S(2)}) %copy-start.1) | copy-done | bytes 221208
  13.4 0.7 %copy-done.2 = f32[3,64]{1,0:T(4,128)S(1)} copy-done((f32[3,64]{1,0:T(4,128)S(1)}, f32[3,64]{1,0:T(4,128)}, u32[]{:S(2)}) %copy-start.2) | copy-done | bytes 792
  14.1 0.2 shard_map.64
  14.3 0.0 collective-permute-done
  14.4 0.3 collective-permute-start.2
  14.6 0.1 stack.19.place_ref
  14.7 0.4 collective-permute-start.6
  15.1 3.4 %shard_map.65 = (bf16[2,512,512]{2,1,0:T(8,128)(2,1)S(1)}, bf16[2,384,512]{2,1,0:T(8,128)(2,1)S(1)}, bf16[2,256,512]{2,1,0:T(8,128)(2,1)S(1)}) custom-call(s32[7]{0:T(128)S(1)} %stack.19.place_ref, bf16[3,192,192]{2,1,0:T(8,128)(2,1)S(1)} %get-tuple-element.37.taps_ref, f32[3,64,1]{2,1,0:T(8,128)S(1)} %get-tuple-element.38.shift_ref.bias_ref, ...), custom_call_target="tpu_custom_call" | custom-call | flops 2000000000 | bytes 4194304 | tf_op jit(solution)/shard_map/pallas_call | solution.py:430
  18.5 3.6 %collective-permute-done.2.refs_3_ = bf16[13,64,128]{2,1,0:T(8,128)(2,1)S(1)} collective-permute-done((bf16[13,64,128]{2,1,0:T(8,128)(2,1)S(1)}, bf16[13,64,128]{2,1,0:T(8,128)(2,1)S(1)}, u32[]{:S(2)}, u32[]{:S(2)}) %collective-permute-start.2) | collective-permute-done | bytes 213024 | tf_op jit(solution)/shard_map/ppermute | solution.py:367
  22.1 1.5 %collective-permute-done.7.refs_5_ = bf16[13,64,128]{2,1,0:T(8,128)(2,1)S(1)} collective-permute-done((bf16[13,64,128]{2,1,0:T(8,128)(2,1)S(1)}, bf16[13,64,128]{2,1,0:T(8,128)(2,1)S(1)}, u32[]{:S(2)}, u32[]{:S(2)}) %collective-permute-start.7) | collective-permute-done | bytes 213024 | tf_op jit(solution)/shard_map/ppermute | solution.py:367
  23.6 10.2 %shard_map.66 = (f32[512,8,128]{2,1,0:T(8,128)S(1)}, bf16[8,128,128]{2,1,0:T(8,128)(2,1)S(1)}) custom-call(s32[7]{0:T(128)S(1)} %stack.19.place_ref, bf16[3,192,192]{2,1,0:T(8,128)(2,1)S(1)} %get-tuple-element.37.taps_ref, f32[3,64,1]{2,1,0:T(8,128)S(1)} %get-tuple-element.38.shift_ref.bias_ref, bf16[2,512,512]{2,1,0:T(8,128)(2,1)S(1)} %get-tuple-element.45.rows_ref, ...), custom_call_target="tpu_custom_call" | custom-call | flops 10000000000 | bytes 4194304 | tf_op jit(solution)/shard_map/pallas_call | solution.py:441
  33.8 3.5 %collective-permute-start.10 = (bf16[8,128,128]{2,1,0:T(8,128)(2,1)S(1)}, bf16[8,128,128]{2,1,0:T(8,128)(2,1)S(1)}, u32[]{:S(2)}, u32[]{:S(2)}) collective-permute-start(bf16[8,128,128]{2,1,0:T(8,128)(2,1)S(1)} %get-tuple-element.52.refs_0_), channel_id=1, source_target_pairs={{0,12},{4,0},{8,4},{12,8},{16,28},{20,16},{24,20},{28,24},{1,13},{... | collective-permute-start | bytes 786440 | tf_op jit(solution)/shard_map/ppermute | solution.py:465
  37.2 0.5 collective-permute-start.9
  37.7 0.2 collective-permute-start.8
  37.9 12.5 %shard_map.67 = (f32[2,128,8,128]{3,2,1,0:T(8,128)S(1)}, f32[128,16]{1,0:T(8,128)S(1)}) custom-call(s32[7]{0:T(128)S(1)} %stack.19.place_ref, s32[2]{0:T(128)S(1)} %copy-done.3, f32[512,8,128]{2,1,0:T(8,128)S(1)} %get-tuple-element.50.cost_ref), custom_call_target="tpu_custom_call" | custom-call | flops 10000000000 | bytes 4194304 | tf_op jit(solution)/shard_map/pallas_call | solution.py:472
  50.4 0.0 collective-permute-done.10.refs_3_
  50.4 0.0 collective-permute-done.8.refs_1_
  50.4 1.3 %shard_map.68 = (f32[8,128,128]{2,1,0:T(8,128)S(1)}, bf16[128,128]{1,0:T(8,128)(2,1)S(1)}) custom-call(s32[7]{0:T(128)S(1)} %stack.19.place_ref, s32[2]{0:T(128)S(1)} %copy-done.3, bf16[8,128,128]{2,1,0:T(8,128)(2,1)S(1)} %get-tuple-element.52.refs_0_, bf16[8,128,128]{2,1,0:T(8,128)(2,1)S(1)} %collective-permute-done.8.refs_1_, ...), custom_call_target="tpu_custom_call" | custom-call | flops 2000000000 | bytes 4194304 | tf_op jit(solution)/shard_map/pallas_call | solution.py:482
  51.7 2.5 %collective-permute-start.11 = (bf16[128,128]{1,0:T(8,128)(2,1)S(1)}, bf16[128,128]{1,0:T(8,128)(2,1)S(1)}, u32[]{:S(2)}, u32[]{:S(2)}) collective-permute-start(bf16[128,128]{1,0:T(8,128)(2,1)S(1)} %get-tuple-element.59), channel_id=1, source_target_pairs={{0,16},{4,20},{8,24},{12,28},{16,0},{20,4},{24,8},{28,12},{1,17},{... | collective-permute-start | bytes 98312 | tf_op jit(solution)/shard_map/ppermute | solution.py:495
  54.2 5.6 %shard_map.69 = (f32[2,128,8,128]{3,2,1,0:T(8,128)S(1)}, f32[128,16]{1,0:T(8,128)}) custom-call(s32[7]{0:T(128)S(1)} %stack.19.place_ref, s32[2]{0:T(128)S(1)} %copy-done.3, f32[512,8,128]{2,1,0:T(8,128)S(1)} %get-tuple-element.50.cost_ref, f32[128,16]{1,0:T(8,128)S(1)} %get-tuple-element.61.refs_0_), custom_call_target="tpu_custom_call" | custom-call | flops 10000000000 | bytes 4194304 | tf_op jit(solution)/shard_map/pallas_call | solution.py:496
  59.8 3.2 %shard_map.70 = f32[8,128,128]{2,1,0:T(8,128)} custom-call(s32[7]{0:T(128)S(1)} %stack.19.place_ref, s32[2]{0:T(128)S(1)} %copy-done.3, bf16[8,128,128]{2,1,0:T(8,128)(2,1)S(1)} %get-tuple-element.52.refs_0_, bf16[8,128,128]{2,1,0:T(8,128)(2,1)S(1)} %collective-permute-done.8.refs_1_, bf16[8,128,128]{2,1,0:T(8,128)(2,1)S(1)} %collective-permute-done.9.refs_2_, ...), custom_call_target="tpu_custom_call" | custom-call | flops 3000000000 | bytes 4194304 | tf_op jit(solution)/shard_map/pallas_call | solution.py:504
  (16 shorter events, 0.1 us)
Async XLA Ops:
  0.0 11.3 %collective-permute-start.3 = (bf16[16,64,128]{2,1,0:T(8,128)(2,1)}, bf16[16,64,128]{2,1,0:T(8,128)(2,1)S(1)}, u32[]{:S(2)}, u32[]{:S(2)}) collective-permute-start(bf16[16,64,128]{2,1,0:T(8,128)(2,1)} %bitcast.10), channel_id=1, source_target_pairs={{0,2},{1,3},{2,0},{3,1},{4,6},{5,7},{6,4},{7,5},{8,10},{9,11},{10,... | collective-permute-start | bytes 786440 | tf_op jit(solution)/shard_map/ppermute | solution.py:367
  3.0 12.1 %collective-permute-start.4 = (bf16[16,64,128]{2,1,0:T(8,128)(2,1)}, bf16[16,64,128]{2,1,0:T(8,128)(2,1)S(1)}, u32[]{:S(2)}, u32[]{:S(2)}) collective-permute-start(bf16[16,64,128]{2,1,0:T(8,128)(2,1)} %bitcast.11), channel_id=1, source_target_pairs={{0,1},{1,0},{2,3},{3,2},{4,5},{5,4},{6,7},{7,6},{8,9},{9,8},{10,11... | collective-permute-start | bytes 786440 | tf_op jit(solution)/shard_map/ppermute | solution.py:367
  3.9 10.4 %collective-permute-start.1 = (bf16[2,3,64,128]{3,2,1,0:T(8,128)(2,1)S(1)}, bf16[2,3,64,128]{3,2,1,0:T(8,128)(2,1)S(1)}, u32[]{:S(2)}, u32[]{:S(2)}) collective-permute-start(bf16[2,3,64,128]{3,2,1,0:T(8,128)(2,1)S(1)} %get-tuple-element.63), channel_id=1, source_target_pairs={{4,0},{8,4},{12,8},{16,12},{20,16},{24,20},{28,24},{5,1},{9,5},{13... | collective-permute-start | bytes 294920 | tf_op jit(solution)/shard_map/ppermute | solution.py:399
  5.2 9.1 %collective-permute-start = (bf16[2,3,64,128]{3,2,1,0:T(8,128)(2,1)S(1)}, bf16[2,3,64,128]{3,2,1,0:T(8,128)(2,1)S(1)}, u32[]{:S(2)}, u32[]{:S(2)}) collective-permute-start(bf16[2,3,64,128]{3,2,1,0:T(8,128)(2,1)S(1)} %get-tuple-element.64), channel_id=1, source_target_pairs={{0,4},{4,8},{8,12},{12,16},{16,20},{20,24},{24,28},{1,5},{5,9},{9,... | collective-permute-start | bytes 294920 | tf_op jit(solution)/shard_map/ppermute | solution.py:398
  11.3 3.7 %collective-permute-start.5 = (bf16[16,64,128]{2,1,0:T(8,128)(2,1)S(1)}, bf16[16,64,128]{2,1,0:T(8,128)(2,1)S(1)}, u32[]{:S(2)}, u32[]{:S(2)}) collective-permute-start(bf16[16,64,128]{2,1,0:T(8,128)(2,1)S(1)} %collective-permute-done.3.refs_1_), channel_id=1, source_target_pairs={{0,1},{1,0},{2,3},{3,2},{4,5},{5,4},{6,7},{7,6},{8,9},{9,8},{10,11... | collective-permute-start | bytes 786440 | tf_op jit(solution)/shard_map/ppermute | solution.py:367
  11.4 1.0 %copy-start = (bf16[2,8,64,128]{3,2,1,0:T(8,128)(2,1)S(1)}, bf16[2,8,64,128]{3,2,1,0:T(8,128)(2,1)}, u32[]{:S(2)}) copy-start(bf16[2,8,64,128]{3,2,1,0:T(8,128)(2,1)} %param.6) | copy-start | bytes 786436
  12.4 1.0 %copy-start.1 = (bf16[3,3,3,64,64]{4,3,2,1,0:T(8,128)(2,1)S(1)}, bf16[3,3,3,64,64]{4,3,2,1,0:T(8,128)(2,1)}, u32[]{:S(2)}) copy-start(bf16[3,3,3,64,64]{4,3,2,1,0:T(8,128)(2,1)} %filter_ref.1) | copy-start | bytes 663556
  13.4 0.7 %copy-start.2 = (f32[3,64]{1,0:T(4,128)S(1)}, f32[3,64]{1,0:T(4,128)}, u32[]{:S(2)}) copy-start(f32[3,64]{1,0:T(4,128)} %bias_ref.1) | copy-start | bytes 2308
  14.4 7.7 %collective-permute-start.2 = (bf16[13,64,128]{2,1,0:T(8,128)(2,1)S(1)}, bf16[13,64,128]{2,1,0:T(8,128)(2,1)S(1)}, u32[]{:S(2)}, u32[]{:S(2)}) collective-permute-start(bf16[13,64,128]{2,1,0:T(8,128)(2,1)S(1)} %pad_maximum_fusion.refs_2_), channel_id=1, source_target_pairs={{0,2},{1,3},{2,0},{3,1},{4,6},{5,7},{6,4},{7,5},{8,10},{9,11},{10,... | collective-permute-start | bytes 638984 | tf_op jit(solution)/shard_map/ppermute | solution.py:367
  14.7 7.4 %collective-permute-start.6 = (bf16[13,64,128]{2,1,0:T(8,128)(2,1)S(1)}, bf16[13,64,128]{2,1,0:T(8,128)(2,1)S(1)}, u32[]{:S(2)}, u32[]{:S(2)}) collective-permute-start(bf16[13,64,128]{2,1,0:T(8,128)(2,1)S(1)} %pad_maximum_fusion.refs_2_), channel_id=1, source_target_pairs={{0,1},{1,0},{2,3},{3,2},{4,5},{5,4},{6,7},{7,6},{8,9},{9,8},{10,11... | collective-permute-start | bytes 638984 | tf_op jit(solution)/shard_map/ppermute | solution.py:367
  22.1 15.8 %copy-start.3 = (s32[2]{0:T(128)S(1)}, s32[2]{0:T(128)}, u32[]{:S(2)}) copy-start(s32[2]{0:T(128)} %charge_ref.7) | copy-start | bytes 28
  22.1 1.5 %collective-permute-start.7 = (bf16[13,64,128]{2,1,0:T(8,128)(2,1)S(1)}, bf16[13,64,128]{2,1,0:T(8,128)(2,1)S(1)}, u32[]{:S(2)}, u32[]{:S(2)}) collective-permute-start(bf16[13,64,128]{2,1,0:T(8,128)(2,1)S(1)} %collective-permute-done.2.refs_3_), channel_id=1, source_target_pairs={{0,1},{1,0},{2,3},{3,2},{4,5},{5,4},{6,7},{7,6},{8,9},{9,8},{10,11... | collective-permute-start | bytes 638984 | tf_op jit(solution)/shard_map/ppermute | solution.py:367
  33.8 16.6 %collective-permute-start.10 = (bf16[8,128,128]{2,1,0:T(8,128)(2,1)S(1)}, bf16[8,128,128]{2,1,0:T(8,128)(2,1)S(1)}, u32[]{:S(2)}, u32[]{:S(2)}) collective-permute-start(bf16[8,128,128]{2,1,0:T(8,128)(2,1)S(1)} %get-tuple-element.52.refs_0_), channel_id=1, source_target_pairs={{0,12},{4,0},{8,4},{12,8},{16,28},{20,16},{24,20},{28,24},{1,13},{... | collective-permute-start | bytes 786440 | tf_op jit(solution)/shard_map/ppermute | solution.py:465
  37.2 13.2 %collective-permute-start.9 = (bf16[8,128,128]{2,1,0:T(8,128)(2,1)S(1)}, bf16[8,128,128]{2,1,0:T(8,128)(2,1)S(1)}, u32[]{:S(2)}, u32[]{:S(2)}) collective-permute-start(bf16[8,128,128]{2,1,0:T(8,128)(2,1)S(1)} %get-tuple-element.52.refs_0_), channel_id=1, source_target_pairs={{0,8},{4,12},{8,0},{12,4},{16,24},{20,28},{24,16},{28,20},{1,9},{5... | collective-permute-start | bytes 786440 | tf_op jit(solution)/shard_map/ppermute | solution.py:465
  37.7 12.7 %collective-permute-start.8 = (bf16[8,128,128]{2,1,0:T(8,128)(2,1)S(1)}, bf16[8,128,128]{2,1,0:T(8,128)(2,1)S(1)}, u32[]{:S(2)}, u32[]{:S(2)}) collective-permute-start(bf16[8,128,128]{2,1,0:T(8,128)(2,1)S(1)} %get-tuple-element.52.refs_0_), channel_id=1, source_target_pairs={{0,4},{4,8},{8,12},{12,0},{16,20},{20,24},{24,28},{28,16},{1,5},{5... | collective-permute-start | bytes 786440 | tf_op jit(solution)/shard_map/ppermute | solution.py:465
  51.7 8.1 %collective-permute-start.11 = (bf16[128,128]{1,0:T(8,128)(2,1)S(1)}, bf16[128,128]{1,0:T(8,128)(2,1)S(1)}, u32[]{:S(2)}, u32[]{:S(2)}) collective-permute-start(bf16[128,128]{1,0:T(8,128)(2,1)S(1)} %get-tuple-element.59), channel_id=1, source_target_pairs={{0,16},{4,20},{8,24},{12,28},{16,0},{20,4},{24,8},{28,12},{1,17},{... | collective-permute-start | bytes 98312 | tf_op jit(solution)/shard_map/ppermute | solution.py:495

commit v5 on v4

--- a/solution.py
+++ b/solution.py
@@ -198,7 +198,7 @@
                 chosen = jnp.where(lane <= ahead - width, product[:, 2 * width :], chosen)
                 chosen = jnp.take_along_axis(chosen, index, axis=1, mode="promise_in_bounds")
                 chosen = 1.0 - chosen
-                cost_ref[pl.ds(here, width), y, :] = chosen
+                cost_ref[pl.ds(pl.multiple_of(here * rows, rows) + y, width, stride=rows), :] = chosen
                 if mine:
                     own_ref[y] = chosen.T.astype(jnp.bfloat16)
 
@@ -212,9 +212,10 @@
 
 def across_kernel(second, place_ref, charge_ref, cost_ref, *refs):
     kept_ref, last_ref, same_ref = refs[-3:]
-    cols = cost_ref.shape[0]
-    _, width, rows, _ = kept_ref.shape
-    parts = cols // width
+    parts = cost_ref.shape[0] // kept_ref.shape[1]
+    rows = last_ref.shape[1] // 2
+    width = kept_ref.shape[1] // rows
+    cols = parts * width
     early = early_segments(parts)
     own = place_ref[2]
     p1, p2 = charges(charge_ref)
@@ -224,9 +225,12 @@
     same_ref[...] = jnp.where(place == other % DISPARITIES, 1.0, 0.0).astype(jnp.bfloat16)
     same = same_ref[...]
 
+    def at(column):
+        return pl.ds(pl.multiple_of(column * rows, rows), rows)
+
     def cost_at(step):
         step = jnp.minimum(step, cols - 1)
-        pair = jnp.concatenate([cost_ref[step], cost_ref[cols - 1 - step]], axis=0)
+        pair = jnp.concatenate([cost_ref[at(step)], cost_ref[at(cols - 1 - step)]], axis=0)
         coarse = pair.astype(jnp.bfloat16)
         fine = (pair - coarse.astype(jnp.float32)).astype(jnp.bfloat16)
         return registers(
@@ -253,9 +257,9 @@
                 if keep_right or keep_left:
                     back = jnp.concatenate([f - least for f in fresh], axis=0).T
                 if keep_right:
-                    kept_ref[0, i] = back[0:rows]
+                    kept_ref[0, at(i)] = back[0:rows]
                 if keep_left:
-                    kept_ref[1, width - 1 - i] = back[rows : 2 * rows]
+                    kept_ref[1, at(width - 1 - i)] = back[rows : 2 * rows]
                 return tuple(fresh), tuple(ahead)
 
             carry = (state, tuple(cost_at(first_step)))
@@ -337,8 +341,9 @@
     right_early = place_ref[2] < place_ref[6]
     left_early = place_ref[5] - 1 - place_ref[2] < place_ref[6]
     for row in range(rows):
-        right = jnp.where(right_early, early_ref[0, :, row, :], late_ref[0, :, row, :])
-        left = jnp.where(left_early, early_ref[1, :, row, :], late_ref[1, :, row, :])
+        this = pl.ds(row, width, stride=rows)
+        right = jnp.where(right_early, early_ref[0, this, :], late_ref[0, this, :])
+        left = jnp.where(left_early, early_ref[1, this, :], late_ref[1, this, :])
         value = total[row].T + (right + left)
         out_ref[row] = jnp.take_along_axis(value, index, axis=1, mode="promise_in_bounds")
 
@@ -441,7 +446,7 @@
     cost, own = call(
         functools.partial(band_kernel, masks),
         (
-            jax.ShapeDtypeStruct((cols, rows, DISPARITIES), f32),
+            jax.ShapeDtypeStruct((cols * rows, DISPARITIES), f32),
             jax.ShapeDtypeStruct((rows, DISPARITIES, width), bf16),
         ),
         [SMEM()] + [VMEM()] * (2 + layers + parts),
@@ -465,7 +470,7 @@
         blocks.append(lax.ppermute(own, "row", turn))
 
     halves = (
-        jax.ShapeDtypeStruct((2, width, rows, DISPARITIES), f32),
+        jax.ShapeDtypeStruct((2, width * rows, DISPARITIES), f32),
         jax.ShapeDtypeStruct((DISPARITIES, 2 * rows), f32),
     )
     identity = [pltpu.VMEM((DISPARITIES, 2 * DISPARITIES), bf16)]

time: 63.3 us -> 62.5 us (0.987)
  Pallas kernels: 36.4 us -> 35.7 us
where the time goes in v5:
time: 62.5 us; the launch traced here: 62.2 us
  Pallas kernels  35.7 us (57%)
  starting transfers between devices  16 us (26%)
  waiting for transfers between devices  5.09 us (8%)
  local copies, waits for them, and re-layouts  3.86 us (6%)
  other arithmetic  0.8 us (1%)
  between operations  0.79 us (1%)
    pallas_call x1, Pallas kernels, per_device(): call(functools.partial(across_kernel, False), halves, [SMEM(), SMEM(), VM...  12.5 us
    pallas_call x1, Pallas kernels, per_device(): call(functools.partial(band_kernel, masks), (jax.ShapeDtypeStruct((cols *...  9.96 us
    pallas_call x1, Pallas kernels, per_device(): call(functools.partial(across_kernel, True), halves, [SMEM(), SMEM(), VME...  5.6 us
    ppermute x6, waiting for transfers between devices, spread(): blocks += [lax.ppermute(held, 'col', route) for held in blocks]  5.08 us
    ppermute x1, starting transfers between devices, per_device(): before = lax.ppermute(activations[:, rows - layers:], 'row', downward)  4.55 us
    ppermute x3, starting transfers between devices, per_device(): blocks.append(lax.ppermute(own, 'row', turn))  4.09 us
    ppermute x6, starting transfers between devices, spread(): blocks += [lax.ppermute(held, 'col', route) for held in blocks]  3.58 us
    pallas_call x1, Pallas kernels, per_device(): call(functools.partial(inner_kernel, masks), tuple((jax.ShapeDtypeStruct(...  3.41 us
  transfers between devices with their start and end apart: 12, of which 2 were waited for; matrix products, arithmetic and copies ran while one was open for 3% of the time, Pallas kernels for 35%

profile of v5, /device:TPU:0, one launch (start us, length us, event | category | flops | bytes accessed | tf_op | source)
XLA Modules:
  0.0 62.2 jit_solution(11160720929563463048)
XLA Ops:
  0.0 3.0 %collective-permute-start.3 = (bf16[16,64,128]{2,1,0:T(8,128)(2,1)}, bf16[16,64,128]{2,1,0:T(8,128)(2,1)S(1)}, u32[]{:S(2)}, u32[]{:S(2)}) collective-permute-start(bf16[16,64,128]{2,1,0:T(8,128)(2,1)} %bitcast.10), channel_id=1, source_target_pairs={{0,2},{1,3},{2,0},{3,1},{4,6},{5,7},{6,4},{7,5},{8,10},{9,11},{10,... | collective-permute-start | bytes 786440 | tf_op jit(solution)/shard_map/ppermute | solution.py:372
  3.0 0.0 collective-permute-start.4
  3.0 1.0 %fusion = (bf16[2,3,64,128]{3,2,1,0:T(8,128)(2,1)S(1)}, bf16[2,3,64,128]{3,2,1,0:T(8,128)(2,1)S(1)}) fusion(bf16[2,8,64,128]{3,2,1,0:T(8,128)(2,1)} %param.6), kind=kLoop, calls=%fused_computation.2 | loop fusion | bytes 393216 | tf_op jit(solution)/shard_map/slice | solution.py:404
  3.9 1.3 %collective-permute-start.1 = (bf16[2,3,64,128]{3,2,1,0:T(8,128)(2,1)S(1)}, bf16[2,3,64,128]{3,2,1,0:T(8,128)(2,1)S(1)}, u32[]{:S(2)}, u32[]{:S(2)}) collective-permute-start(bf16[2,3,64,128]{3,2,1,0:T(8,128)(2,1)S(1)} %get-tuple-element.63), channel_id=1, source_target_pairs={{4,0},{8,4},{12,8},{16,12},{20,16},{24,20},{28,24},{5,1},{9,5},{13... | collective-permute-start | bytes 294920 | tf_op jit(solution)/shard_map/ppermute | solution.py:404
  5.2 4.6 %collective-permute-start = (bf16[2,3,64,128]{3,2,1,0:T(8,128)(2,1)S(1)}, bf16[2,3,64,128]{3,2,1,0:T(8,128)(2,1)S(1)}, u32[]{:S(2)}, u32[]{:S(2)}) collective-permute-start(bf16[2,3,64,128]{3,2,1,0:T(8,128)(2,1)S(1)} %get-tuple-element.64), channel_id=1, source_target_pairs={{0,4},{4,8},{8,12},{12,16},{16,20},{20,24},{24,28},{1,5},{5,9},{9,... | collective-permute-start | bytes 294920 | tf_op jit(solution)/shard_map/ppermute | solution.py:403
  10.5 0.1 pad.5.clone
  10.6 0.1 pad.4.clone
  10.6 0.7 %convert_element_type.6 = bf16[8,128]{1,0:T(8,128)(2,1)S(1)} convert(s32[8,128]{1,0:T(8,128)} %param.9) | non-fusion elementwise | flops 1024 | bytes 6144 | tf_op jit(solution)/shard_map/convert_element_type | solution.py:422
  11.3 0.1 maximum_bitcast_fusion
  11.4 0.0 copy-start
  11.4 0.9 %copy-done = bf16[2,8,64,128]{3,2,1,0:T(8,128)(2,1)S(1)} copy-done((bf16[2,8,64,128]{3,2,1,0:T(8,128)(2,1)S(1)}, bf16[2,8,64,128]{3,2,1,0:T(8,128)(2,1)}, u32[]{:S(2)}) %copy-start) | copy-done | bytes 262168
  12.4 1.0 %copy-done.1 = bf16[3,3,3,64,64]{4,3,2,1,0:T(8,128)(2,1)S(1)} copy-done((bf16[3,3,3,64,64]{4,3,2,1,0:T(8,128)(2,1)S(1)}, bf16[3,3,3,64,64]{4,3,2,1,0:T(8,128)(2,1)}, u32[]{:S(2)}) %copy-start.1) | copy-done | bytes 221208
  13.4 0.7 %copy-done.2 = f32[3,64]{1,0:T(4,128)S(1)} copy-done((f32[3,64]{1,0:T(4,128)S(1)}, f32[3,64]{1,0:T(4,128)}, u32[]{:S(2)}) %copy-start.2) | copy-done | bytes 792
  14.1 0.2 shard_map.64
  14.3 0.0 collective-permute-done
  14.4 0.3 collective-permute-start.2
  14.6 0.1 stack.19.place_ref
  14.7 0.4 collective-permute-start.6
  15.1 3.4 %shard_map.65 = (bf16[2,512,512]{2,1,0:T(8,128)(2,1)S(1)}, bf16[2,384,512]{2,1,0:T(8,128)(2,1)S(1)}, bf16[2,256,512]{2,1,0:T(8,128)(2,1)S(1)}) custom-call(s32[7]{0:T(128)S(1)} %stack.19.place_ref, bf16[3,192,192]{2,1,0:T(8,128)(2,1)S(1)} %get-tuple-element.37.taps_ref, f32[3,64,1]{2,1,0:T(8,128)S(1)} %get-tuple-element.38.shift_ref.bias_ref, ...), custom_call_target="tpu_custom_call" | custom-call | flops 2000000000 | bytes 4194304 | tf_op jit(solution)/shard_map/pallas_call | solution.py:435
  18.5 3.6 %collective-permute-done.2.refs_3_ = bf16[13,64,128]{2,1,0:T(8,128)(2,1)S(1)} collective-permute-done((bf16[13,64,128]{2,1,0:T(8,128)(2,1)S(1)}, bf16[13,64,128]{2,1,0:T(8,128)(2,1)S(1)}, u32[]{:S(2)}, u32[]{:S(2)}) %collective-permute-start.2) | collective-permute-done | bytes 213024 | tf_op jit(solution)/shard_map/ppermute | solution.py:372
  22.1 1.5 %collective-permute-done.7.refs_5_ = bf16[13,64,128]{2,1,0:T(8,128)(2,1)S(1)} collective-permute-done((bf16[13,64,128]{2,1,0:T(8,128)(2,1)S(1)}, bf16[13,64,128]{2,1,0:T(8,128)(2,1)S(1)}, u32[]{:S(2)}, u32[]{:S(2)}) %collective-permute-start.7) | collective-permute-done | bytes 213024 | tf_op jit(solution)/shard_map/ppermute | solution.py:372
  23.6 10.0 %shard_map.66 = (f32[4096,128]{1,0:T(8,128)S(1)}, bf16[8,128,128]{2,1,0:T(8,128)(2,1)S(1)}) custom-call(s32[7]{0:T(128)S(1)} %stack.19.place_ref, bf16[3,192,192]{2,1,0:T(8,128)(2,1)S(1)} %get-tuple-element.37.taps_ref, f32[3,64,1]{2,1,0:T(8,128)S(1)} %get-tuple-element.38.shift_ref.bias_ref, bf16[2,512,512]{2,1,0:T(8,128)(2,1)S(1)} %get-tuple-element.45.rows_ref, ...), custom_call_target="tpu_custom_call" | custom-call | flops 10000000000 | bytes 4194304 | tf_op jit(solution)/shard_map/pallas_call | solution.py:446
  33.5 3.4 %collective-permute-start.10 = (bf16[8,128,128]{2,1,0:T(8,128)(2,1)S(1)}, bf16[8,128,128]{2,1,0:T(8,128)(2,1)S(1)}, u32[]{:S(2)}, u32[]{:S(2)}) collective-permute-start(bf16[8,128,128]{2,1,0:T(8,128)(2,1)S(1)} %get-tuple-element.52.refs_0_), channel_id=1, source_target_pairs={{0,12},{4,0},{8,4},{12,8},{16,28},{20,16},{24,20},{28,24},{1,13},{... | collective-permute-start | bytes 786440 | tf_op jit(solution)/shard_map/ppermute | solution.py:470
  37.0 0.5 collective-permute-start.9
  37.4 0.2 collective-permute-start.8
  37.6 12.5 %shard_map.67 = (f32[2,1024,128]{2,1,0:T(8,128)S(1)}, f32[128,16]{1,0:T(8,128)S(1)}) custom-call(s32[7]{0:T(128)S(1)} %stack.19.place_ref, s32[2]{0:T(128)S(1)} %copy-done.3, f32[4096,128]{1,0:T(8,128)S(1)} %get-tuple-element.50.cost_ref), custom_call_target="tpu_custom_call" | custom-call | flops 10000000000 | bytes 4194304 | tf_op jit(solution)/shard_map/pallas_call | solution.py:477
  50.1 0.0 collective-permute-done.9.refs_2_
  50.1 0.0 collective-permute-done.8.refs_1_
  50.2 1.3 %shard_map.68 = (f32[8,128,128]{2,1,0:T(8,128)S(1)}, bf16[128,128]{1,0:T(8,128)(2,1)S(1)}) custom-call(s32[7]{0:T(128)S(1)} %stack.19.place_ref, s32[2]{0:T(128)S(1)} %copy-done.3, bf16[8,128,128]{2,1,0:T(8,128)(2,1)S(1)} %get-tuple-element.52.refs_0_, bf16[8,128,128]{2,1,0:T(8,128)(2,1)S(1)} %collective-permute-done.8.refs_1_, ...), custom_call_target="tpu_custom_call" | custom-call | flops 2000000000 | bytes 4194304 | tf_op jit(solution)/shard_map/pallas_call | solution.py:487
  51.5 2.5 %collective-permute-start.11 = (bf16[128,128]{1,0:T(8,128)(2,1)S(1)}, bf16[128,128]{1,0:T(8,128)(2,1)S(1)}, u32[]{:S(2)}, u32[]{:S(2)}) collective-permute-start(bf16[128,128]{1,0:T(8,128)(2,1)S(1)} %get-tuple-element.59), channel_id=1, source_target_pairs={{0,16},{4,20},{8,24},{12,28},{16,0},{20,4},{24,8},{28,12},{1,17},{... | collective-permute-start | bytes 98312 | tf_op jit(solution)/shard_map/ppermute | solution.py:500
  53.9 5.6 %shard_map.69 = (f32[2,1024,128]{2,1,0:T(8,128)S(1)}, f32[128,16]{1,0:T(8,128)}) custom-call(s32[7]{0:T(128)S(1)} %stack.19.place_ref, s32[2]{0:T(128)S(1)} %copy-done.3, f32[4096,128]{1,0:T(8,128)S(1)} %get-tuple-element.50.cost_ref, f32[128,16]{1,0:T(8,128)S(1)} %get-tuple-element.61.refs_0_), custom_call_target="tpu_custom_call" | custom-call | flops 10000000000 | bytes 4194304 | tf_op jit(solution)/shard_map/pallas_call | solution.py:501
  59.5 2.7 %shard_map.70 = f32[8,128,128]{2,1,0:T(8,128)} custom-call(s32[7]{0:T(128)S(1)} %stack.19.place_ref, s32[2]{0:T(128)S(1)} %copy-done.3, bf16[8,128,128]{2,1,0:T(8,128)(2,1)S(1)} %get-tuple-element.52.refs_0_, bf16[8,128,128]{2,1,0:T(8,128)(2,1)S(1)} %collective-permute-done.8.refs_1_, bf16[8,128,128]{2,1,0:T(8,128)(2,1)S(1)} %collective-permute-done.9.refs_2_, ...), custom_call_target="tpu_custom_call" | custom-call | flops 3000000000 | bytes 4194304 | tf_op jit(solution)/shard_map/pallas_call | solution.py:509
  (16 shorter events, 0.1 us)
Async XLA Ops:
  0.0 11.3 %collective-permute-start.3 = (bf16[16,64,128]{2,1,0:T(8,128)(2,1)}, bf16[16,64,128]{2,1,0:T(8,128)(2,1)S(1)}, u32[]{:S(2)}, u32[]{:S(2)}) collective-permute-start(bf16[16,64,128]{2,1,0:T(8,128)(2,1)} %bitcast.10), channel_id=1, source_target_pairs={{0,2},{1,3},{2,0},{3,1},{4,6},{5,7},{6,4},{7,5},{8,10},{9,11},{10,... | collective-permute-start | bytes 786440 | tf_op jit(solution)/shard_map/ppermute | solution.py:372
  3.0 12.1 %collective-permute-start.4 = (bf16[16,64,128]{2,1,0:T(8,128)(2,1)}, bf16[16,64,128]{2,1,0:T(8,128)(2,1)S(1)}, u32[]{:S(2)}, u32[]{:S(2)}) collective-permute-start(bf16[16,64,128]{2,1,0:T(8,128)(2,1)} %bitcast.11), channel_id=1, source_target_pairs={{0,1},{1,0},{2,3},{3,2},{4,5},{5,4},{6,7},{7,6},{8,9},{9,8},{10,11... | collective-permute-start | bytes 786440 | tf_op jit(solution)/shard_map/ppermute | solution.py:372
  3.9 10.4 %collective-permute-start.1 = (bf16[2,3,64,128]{3,2,1,0:T(8,128)(2,1)S(1)}, bf16[2,3,64,128]{3,2,1,0:T(8,128)(2,1)S(1)}, u32[]{:S(2)}, u32[]{:S(2)}) collective-permute-start(bf16[2,3,64,128]{3,2,1,0:T(8,128)(2,1)S(1)} %get-tuple-element.63), channel_id=1, source_target_pairs={{4,0},{8,4},{12,8},{16,12},{20,16},{24,20},{28,24},{5,1},{9,5},{13... | collective-permute-start | bytes 294920 | tf_op jit(solution)/shard_map/ppermute | solution.py:404
  5.2 9.1 %collective-permute-start = (bf16[2,3,64,128]{3,2,1,0:T(8,128)(2,1)S(1)}, bf16[2,3,64,128]{3,2,1,0:T(8,128)(2,1)S(1)}, u32[]{:S(2)}, u32[]{:S(2)}) collective-permute-start(bf16[2,3,64,128]{3,2,1,0:T(8,128)(2,1)S(1)} %get-tuple-element.64), channel_id=1, source_target_pairs={{0,4},{4,8},{8,12},{12,16},{16,20},{20,24},{24,28},{1,5},{5,9},{9,... | collective-permute-start | bytes 294920 | tf_op jit(solution)/shard_map/ppermute | solution.py:403
  11.3 3.7 %collective-permute-start.5 = (bf16[16,64,128]{2,1,0:T(8,128)(2,1)S(1)}, bf16[16,64,128]{2,1,0:T(8,128)(2,1)S(1)}, u32[]{:S(2)}, u32[]{:S(2)}) collective-permute-start(bf16[16,64,128]{2,1,0:T(8,128)(2,1)S(1)} %collective-permute-done.3.refs_1_), channel_id=1, source_target_pairs={{0,1},{1,0},{2,3},{3,2},{4,5},{5,4},{6,7},{7,6},{8,9},{9,8},{10,11... | collective-permute-start | bytes 786440 | tf_op jit(solution)/shard_map/ppermute | solution.py:372
  11.4 1.0 %copy-start = (bf16[2,8,64,128]{3,2,1,0:T(8,128)(2,1)S(1)}, bf16[2,8,64,128]{3,2,1,0:T(8,128)(2,1)}, u32[]{:S(2)}) copy-start(bf16[2,8,64,128]{3,2,1,0:T(8,128)(2,1)} %param.6) | copy-start | bytes 786436
  12.4 1.0 %copy-start.1 = (bf16[3,3,3,64,64]{4,3,2,1,0:T(8,128)(2,1)S(1)}, bf16[3,3,3,64,64]{4,3,2,1,0:T(8,128)(2,1)}, u32[]{:S(2)}) copy-start(bf16[3,3,3,64,64]{4,3,2,1,0:T(8,128)(2,1)} %filter_ref.1) | copy-start | bytes 663556
  13.4 0.7 %copy-start.2 = (f32[3,64]{1,0:T(4,128)S(1)}, f32[3,64]{1,0:T(4,128)}, u32[]{:S(2)}) copy-start(f32[3,64]{1,0:T(4,128)} %bias_ref.1) | copy-start | bytes 2308
  14.4 7.7 %collective-permute-start.2 = (bf16[13,64,128]{2,1,0:T(8,128)(2,1)S(1)}, bf16[13,64,128]{2,1,0:T(8,128)(2,1)S(1)}, u32[]{:S(2)}, u32[]{:S(2)}) collective-permute-start(bf16[13,64,128]{2,1,0:T(8,128)(2,1)S(1)} %pad_maximum_fusion.refs_2_), channel_id=1, source_target_pairs={{0,2},{1,3},{2,0},{3,1},{4,6},{5,7},{6,4},{7,5},{8,10},{9,11},{10,... | collective-permute-start | bytes 638984 | tf_op jit(solution)/shard_map/ppermute | solution.py:372
  14.7 7.4 %collective-permute-start.6 = (bf16[13,64,128]{2,1,0:T(8,128)(2,1)S(1)}, bf16[13,64,128]{2,1,0:T(8,128)(2,1)S(1)}, u32[]{:S(2)}, u32[]{:S(2)}) collective-permute-start(bf16[13,64,128]{2,1,0:T(8,128)(2,1)S(1)} %pad_maximum_fusion.refs_2_), channel_id=1, source_target_pairs={{0,1},{1,0},{2,3},{3,2},{4,5},{5,4},{6,7},{7,6},{8,9},{9,8},{10,11... | collective-permute-start | bytes 638984 | tf_op jit(solution)/shard_map/ppermute | solution.py:372
  22.1 15.5 %copy-start.3 = (s32[2]{0:T(128)S(1)}, s32[2]{0:T(128)}, u32[]{:S(2)}) copy-start(s32[2]{0:T(128)} %charge_ref.7) | copy-start | bytes 28
  22.1 1.5 %collective-permute-start.7 = (bf16[13,64,128]{2,1,0:T(8,128)(2,1)S(1)}, bf16[13,64,128]{2,1,0:T(8,128)(2,1)S(1)}, u32[]{:S(2)}, u32[]{:S(2)}) collective-permute-start(bf16[13,64,128]{2,1,0:T(8,128)(2,1)S(1)} %collective-permute-done.2.refs_3_), channel_id=1, source_target_pairs={{0,1},{1,0},{2,3},{3,2},{4,5},{5,4},{6,7},{7,6},{8,9},{9,8},{10,11... | collective-permute-start | bytes 638984 | tf_op jit(solution)/shard_map/ppermute | solution.py:372
  33.5 16.6 %collective-permute-start.10 = (bf16[8,128,128]{2,1,0:T(8,128)(2,1)S(1)}, bf16[8,128,128]{2,1,0:T(8,128)(2,1)S(1)}, u32[]{:S(2)}, u32[]{:S(2)}) collective-permute-start(bf16[8,128,128]{2,1,0:T(8,128)(2,1)S(1)} %get-tuple-element.52.refs_0_), channel_id=1, source_target_pairs={{0,12},{4,0},{8,4},{12,8},{16,28},{20,16},{24,20},{28,24},{1,13},{... | collective-permute-start | bytes 786440 | tf_op jit(solution)/shard_map/ppermute | solution.py:470
  37.0 13.2 %collective-permute-start.9 = (bf16[8,128,128]{2,1,0:T(8,128)(2,1)S(1)}, bf16[8,128,128]{2,1,0:T(8,128)(2,1)S(1)}, u32[]{:S(2)}, u32[]{:S(2)}) collective-permute-start(bf16[8,128,128]{2,1,0:T(8,128)(2,1)S(1)} %get-tuple-element.52.refs_0_), channel_id=1, source_target_pairs={{0,8},{4,12},{8,0},{12,4},{16,24},{20,28},{24,16},{28,20},{1,9},{5... | collective-permute-start | bytes 786440 | tf_op jit(solution)/shard_map/ppermute | solution.py:470
  37.4 12.7 %collective-permute-start.8 = (bf16[8,128,128]{2,1,0:T(8,128)(2,1)S(1)}, bf16[8,128,128]{2,1,0:T(8,128)(2,1)S(1)}, u32[]{:S(2)}, u32[]{:S(2)}) collective-permute-start(bf16[8,128,128]{2,1,0:T(8,128)(2,1)S(1)} %get-tuple-element.52.refs_0_), channel_id=1, source_target_pairs={{0,4},{4,8},{8,12},{12,0},{16,20},{20,24},{24,28},{28,16},{1,5},{5... | collective-permute-start | bytes 786440 | tf_op jit(solution)/shard_map/ppermute | solution.py:470
  51.5 8.1 %collective-permute-start.11 = (bf16[128,128]{1,0:T(8,128)(2,1)S(1)}, bf16[128,128]{1,0:T(8,128)(2,1)S(1)}, u32[]{:S(2)}, u32[]{:S(2)}) collective-permute-start(bf16[128,128]{1,0:T(8,128)(2,1)S(1)} %get-tuple-element.59), channel_id=1, source_target_pairs={{0,16},{4,20},{8,24},{12,28},{16,0},{20,4},{24,8},{28,12},{1,17},{... | collective-permute-start | bytes 98312 | tf_op jit(solution)/shard_map/ppermute | solution.py:500

commit v6 on v5

--- a/solution.py
+++ b/solution.py
@@ -69,7 +69,7 @@
 
 
 def grouping(steps):
-    return max(k for k in range(1, 6) if steps % k == 0)
+    return max(k for k in range(1, 9) if steps % k == 0)
 
 
 def stage_kernel(filter_ref, bias_ref, tile_ref, taps_ref, shift_ref, tile_out):
@@ -263,7 +263,7 @@
                 return tuple(fresh), tuple(ahead)
 
             carry = (state, tuple(cost_at(first_step)))
-            sums = lax.fori_loop(0, width, body, carry, unroll=16)[0]
+            sums = lax.fori_loop(0, width, body, carry, unroll=32)[0]
             least = least_of(list(sums))
             return tuple(s - least for s in sums)
 

time: 62.5 us -> 59.3 us (0.949)
  Pallas kernels: 35.7 us -> 30.3 us
  waiting for transfers between devices: 5.09 us -> 7.03 us
    pallas_call x1, Pallas kernels: 9.96 us -> 7.91 us  [per_device(): call(functools.partial(band_kernel, masks), (jax.ShapeDtypeStruct((cols *...]
    pallas_call x1, Pallas kernels: 12.5 us -> 10.6 us  [per_device(): call(functools.partial(across_kernel, False), halves, [SMEM(), SMEM(), VM...]
    ppermute x3, waiting for transfers between devices: 0.01 us -> 1.23 us  [per_device(): blocks.append(lax.ppermute(own, 'row', turn))]
    ppermute x6, waiting for transfers between devices: 5.08 us -> 5.8 us  [spread(): blocks += [lax.ppermute(held, 'col', route) for held in blocks]]
    pallas_call x1, Pallas kernels: 3.41 us -> 2.69 us  [per_device(): call(functools.partial(inner_kernel, masks), tuple((jax.ShapeDtypeStruct(...]
    pallas_call x1, Pallas kernels: 5.6 us -> 4.92 us  [per_device(): call(functools.partial(across_kernel, True), halves, [SMEM(), SMEM(), VME...]
  transfers between devices with their start and end apart: 12 -> 12, of which waited for: 2 -> 3; matrix products, arithmetic and copies ran while one was open for 3% -> 3% of each run, Pallas kernels for 35% -> 31%
where the time goes in v6:
time: 59.3 us; the launch traced here: 58.9 us
  Pallas kernels  30.3 us (51%)
  starting transfers between devices  16.2 us (27%)
  waiting for transfers between devices  7.03 us (12%)
  local copies, waits for them, and re-layouts  3.86 us (7%)
  other arithmetic  0.8 us (1%)
  between operations  0.78 us (1%)
    pallas_call x1, Pallas kernels, per_device(): call(functools.partial(across_kernel, False), halves, [SMEM(), SMEM(), VM...  10.6 us
    pallas_call x1, Pallas kernels, per_device(): call(functools.partial(band_kernel, masks), (jax.ShapeDtypeStruct((cols *...  7.91 us
    ppermute x6, waiting for transfers between devices, spread(): blocks += [lax.ppermute(held, 'col', route) for held in blocks]  5.8 us
    pallas_call x1, Pallas kernels, per_device(): call(functools.partial(across_kernel, True), halves, [SMEM(), SMEM(), VME...  4.92 us
    ppermute x1, starting transfers between devices, per_device(): before = lax.ppermute(activations[:, rows - layers:], 'row', downward)  4.55 us
    ppermute x3, starting transfers between devices, per_device(): blocks.append(lax.ppermute(own, 'row', turn))  4.1 us
    ppermute x6, starting transfers between devices, spread(): blocks += [lax.ppermute(held, 'col', route) for held in blocks]  3.58 us
    pallas_call x1, Pallas kernels, per_device(): call(functools.partial(inner_kernel, masks), tuple((jax.ShapeDtypeStruct(...  2.69 us
  transfers between devices with their start and end apart: 12, of which 3 were waited for; matrix products, arithmetic and copies ran while one was open for 3% of the time, Pallas kernels for 31%

profile of v6, /device:TPU:0, one launch (start us, length us, event | category | flops | bytes accessed | tf_op | source)
XLA Modules:
  0.0 58.9 jit_solution(14296872956258119144)
XLA Ops:
  0.0 3.0 %collective-permute-start.3 = (bf16[16,64,128]{2,1,0:T(8,128)(2,1)}, bf16[16,64,128]{2,1,0:T(8,128)(2,1)S(1)}, u32[]{:S(2)}, u32[]{:S(2)}) collective-permute-start(bf16[16,64,128]{2,1,0:T(8,128)(2,1)} %bitcast.10), channel_id=1, source_target_pairs={{0,2},{1,3},{2,0},{3,1},{4,6},{5,7},{6,4},{7,5},{8,10},{9,11},{10,... | collective-permute-start | bytes 786440 | tf_op jit(solution)/shard_map/ppermute | solution.py:372
  3.0 0.0 collective-permute-start.4
  3.0 1.0 %fusion = (bf16[2,3,64,128]{3,2,1,0:T(8,128)(2,1)S(1)}, bf16[2,3,64,128]{3,2,1,0:T(8,128)(2,1)S(1)}) fusion(bf16[2,8,64,128]{3,2,1,0:T(8,128)(2,1)} %param.6), kind=kLoop, calls=%fused_computation.2 | loop fusion | bytes 393216 | tf_op jit(solution)/shard_map/slice | solution.py:404
  3.9 1.3 %collective-permute-start.1 = (bf16[2,3,64,128]{3,2,1,0:T(8,128)(2,1)S(1)}, bf16[2,3,64,128]{3,2,1,0:T(8,128)(2,1)S(1)}, u32[]{:S(2)}, u32[]{:S(2)}) collective-permute-start(bf16[2,3,64,128]{3,2,1,0:T(8,128)(2,1)S(1)} %get-tuple-element.63), channel_id=1, source_target_pairs={{4,0},{8,4},{12,8},{16,12},{20,16},{24,20},{28,24},{5,1},{9,5},{13... | collective-permute-start | bytes 294920 | tf_op jit(solution)/shard_map/ppermute | solution.py:404
  5.2 4.6 %collective-permute-start = (bf16[2,3,64,128]{3,2,1,0:T(8,128)(2,1)S(1)}, bf16[2,3,64,128]{3,2,1,0:T(8,128)(2,1)S(1)}, u32[]{:S(2)}, u32[]{:S(2)}) collective-permute-start(bf16[2,3,64,128]{3,2,1,0:T(8,128)(2,1)S(1)} %get-tuple-element.64), channel_id=1, source_target_pairs={{0,4},{4,8},{8,12},{12,16},{16,20},{20,24},{24,28},{1,5},{5,9},{9,... | collective-permute-start | bytes 294920 | tf_op jit(solution)/shard_map/ppermute | solution.py:403
  10.5 0.1 pad.5.clone
  10.6 0.1 pad.4.clone
  10.6 0.7 %convert_element_type.6 = bf16[8,128]{1,0:T(8,128)(2,1)S(1)} convert(s32[8,128]{1,0:T(8,128)} %param.9) | non-fusion elementwise | flops 1024 | bytes 6144 | tf_op jit(solution)/shard_map/convert_element_type | solution.py:422
  11.3 0.0 collective-permute-done.3.refs_1_
  11.3 0.1 maximum_bitcast_fusion
  11.4 0.0 copy-start
  11.4 0.9 %copy-done = bf16[2,8,64,128]{3,2,1,0:T(8,128)(2,1)S(1)} copy-done((bf16[2,8,64,128]{3,2,1,0:T(8,128)(2,1)S(1)}, bf16[2,8,64,128]{3,2,1,0:T(8,128)(2,1)}, u32[]{:S(2)}) %copy-start) | copy-done | bytes 262168
  12.4 1.0 %copy-done.1 = bf16[3,3,3,64,64]{4,3,2,1,0:T(8,128)(2,1)S(1)} copy-done((bf16[3,3,3,64,64]{4,3,2,1,0:T(8,128)(2,1)S(1)}, bf16[3,3,3,64,64]{4,3,2,1,0:T(8,128)(2,1)}, u32[]{:S(2)}) %copy-start.1) | copy-done | bytes 221208
  13.4 0.7 %copy-done.2 = f32[3,64]{1,0:T(4,128)S(1)} copy-done((f32[3,64]{1,0:T(4,128)S(1)}, f32[3,64]{1,0:T(4,128)}, u32[]{:S(2)}) %copy-start.2) | copy-done | bytes 792
  14.1 0.2 shard_map.64
  14.4 0.3 collective-permute-start.2
  14.6 0.1 stack.19.place_ref
  14.7 0.4 collective-permute-start.6
  15.1 2.7 %shard_map.65 = (bf16[2,512,512]{2,1,0:T(8,128)(2,1)S(1)}, bf16[2,384,512]{2,1,0:T(8,128)(2,1)S(1)}, bf16[2,256,512]{2,1,0:T(8,128)(2,1)S(1)}) custom-call(s32[7]{0:T(128)S(1)} %stack.19.place_ref, bf16[3,192,192]{2,1,0:T(8,128)(2,1)S(1)} %get-tuple-element.37.taps_ref, f32[3,64,1]{2,1,0:T(8,128)S(1)} %get-tuple-element.38.shift_ref.bias_ref, ...), custom_call_target="tpu_custom_call" | custom-call | flops 2000000000 | bytes 4194304 | tf_op jit(solution)/shard_map/pallas_call | solution.py:435
  17.8 4.3 %collective-permute-done.2.refs_3_ = bf16[13,64,128]{2,1,0:T(8,128)(2,1)S(1)} collective-permute-done((bf16[13,64,128]{2,1,0:T(8,128)(2,1)S(1)}, bf16[13,64,128]{2,1,0:T(8,128)(2,1)S(1)}, u32[]{:S(2)}, u32[]{:S(2)}) %collective-permute-start.2) | collective-permute-done | bytes 213024 | tf_op jit(solution)/shard_map/ppermute | solution.py:372
  22.1 1.5 %collective-permute-done.7.refs_5_ = bf16[13,64,128]{2,1,0:T(8,128)(2,1)S(1)} collective-permute-done((bf16[13,64,128]{2,1,0:T(8,128)(2,1)S(1)}, bf16[13,64,128]{2,1,0:T(8,128)(2,1)S(1)}, u32[]{:S(2)}, u32[]{:S(2)}) %collective-permute-start.7) | collective-permute-done | bytes 213024 | tf_op jit(solution)/shard_map/ppermute | solution.py:372
  23.6 7.9 %shard_map.66 = (f32[4096,128]{1,0:T(8,128)S(1)}, bf16[8,128,128]{2,1,0:T(8,128)(2,1)S(1)}) custom-call(s32[7]{0:T(128)S(1)} %stack.19.place_ref, bf16[3,192,192]{2,1,0:T(8,128)(2,1)S(1)} %get-tuple-element.37.taps_ref, f32[3,64,1]{2,1,0:T(8,128)S(1)} %get-tuple-element.38.shift_ref.bias_ref, bf16[2,512,512]{2,1,0:T(8,128)(2,1)S(1)} %get-tuple-element.45.rows_ref, ...), custom_call_target="tpu_custom_call" | custom-call | flops 10000000000 | bytes 4194304 | tf_op jit(solution)/shard_map/pallas_call | solution.py:446
  31.5 3.5 %collective-permute-start.10 = (bf16[8,128,128]{2,1,0:T(8,128)(2,1)S(1)}, bf16[8,128,128]{2,1,0:T(8,128)(2,1)S(1)}, u32[]{:S(2)}, u32[]{:S(2)}) collective-permute-start(bf16[8,128,128]{2,1,0:T(8,128)(2,1)S(1)} %get-tuple-element.52.refs_0_), channel_id=1, source_target_pairs={{0,12},{4,0},{8,4},{12,8},{16,28},{20,16},{24,20},{28,24},{1,13},{... | collective-permute-start | bytes 786440 | tf_op jit(solution)/shard_map/ppermute | solution.py:470
  34.9 0.5 collective-permute-start.9
  35.4 0.2 collective-permute-start.8
  35.6 10.6 %shard_map.67 = (f32[2,1024,128]{2,1,0:T(8,128)S(1)}, f32[128,16]{1,0:T(8,128)S(1)}) custom-call(s32[7]{0:T(128)S(1)} %stack.19.place_ref, s32[2]{0:T(128)S(1)} %copy-done.3, f32[4096,128]{1,0:T(8,128)S(1)} %get-tuple-element.50.cost_ref), custom_call_target="tpu_custom_call" | custom-call | flops 10000000000 | bytes 4194304 | tf_op jit(solution)/shard_map/pallas_call | solution.py:477
  46.2 1.2 %collective-permute-done.9.refs_2_ = bf16[8,128,128]{2,1,0:T(8,128)(2,1)S(1)} collective-permute-done((bf16[8,128,128]{2,1,0:T(8,128)(2,1)S(1)}, bf16[8,128,128]{2,1,0:T(8,128)(2,1)S(1)}, u32[]{:S(2)}, u32[]{:S(2)}) %collective-permute-start.9) | collective-permute-done | bytes 262176 | tf_op jit(solution)/shard_map/ppermute | solution.py:470
  47.4 0.0 collective-permute-done.8.refs_1_
  47.4 1.3 %shard_map.68 = (f32[8,128,128]{2,1,0:T(8,128)S(1)}, bf16[128,128]{1,0:T(8,128)(2,1)S(1)}) custom-call(s32[7]{0:T(128)S(1)} %stack.19.place_ref, s32[2]{0:T(128)S(1)} %copy-done.3, bf16[8,128,128]{2,1,0:T(8,128)(2,1)S(1)} %get-tuple-element.52.refs_0_, bf16[8,128,128]{2,1,0:T(8,128)(2,1)S(1)} %collective-permute-done.8.refs_1_, ...), custom_call_target="tpu_custom_call" | custom-call | flops 2000000000 | bytes 4194304 | tf_op jit(solution)/shard_map/pallas_call | solution.py:487
  48.7 2.6 %collective-permute-start.11 = (bf16[128,128]{1,0:T(8,128)(2,1)S(1)}, bf16[128,128]{1,0:T(8,128)(2,1)S(1)}, u32[]{:S(2)}, u32[]{:S(2)}) collective-permute-start(bf16[128,128]{1,0:T(8,128)(2,1)S(1)} %get-tuple-element.59), channel_id=1, source_target_pairs={{0,16},{4,20},{8,24},{12,28},{16,0},{20,4},{24,8},{28,12},{1,17},{... | collective-permute-start | bytes 98312 | tf_op jit(solution)/shard_map/ppermute | solution.py:500
  51.3 4.9 %shard_map.69 = (f32[2,1024,128]{2,1,0:T(8,128)S(1)}, f32[128,16]{1,0:T(8,128)}) custom-call(s32[7]{0:T(128)S(1)} %stack.19.place_ref, s32[2]{0:T(128)S(1)} %copy-done.3, f32[4096,128]{1,0:T(8,128)S(1)} %get-tuple-element.50.cost_ref, f32[128,16]{1,0:T(8,128)S(1)} %get-tuple-element.61.refs_0_), custom_call_target="tpu_custom_call" | custom-call | flops 10000000000 | bytes 4194304 | tf_op jit(solution)/shard_map/pallas_call | solution.py:501
  56.3 2.7 %shard_map.70 = f32[8,128,128]{2,1,0:T(8,128)} custom-call(s32[7]{0:T(128)S(1)} %stack.19.place_ref, s32[2]{0:T(128)S(1)} %copy-done.3, bf16[8,128,128]{2,1,0:T(8,128)(2,1)S(1)} %get-tuple-element.52.refs_0_, bf16[8,128,128]{2,1,0:T(8,128)(2,1)S(1)} %collective-permute-done.8.refs_1_, bf16[8,128,128]{2,1,0:T(8,128)(2,1)S(1)} %collective-permute-done.9.refs_2_, ...), custom_call_target="tpu_custom_call" | custom-call | flops 3000000000 | bytes 4194304 | tf_op jit(solution)/shard_map/pallas_call | solution.py:509
  (16 shorter events, 0.1 us)
Async XLA Ops:
  0.0 11.3 %collective-permute-start.3 = (bf16[16,64,128]{2,1,0:T(8,128)(2,1)}, bf16[16,64,128]{2,1,0:T(8,128)(2,1)S(1)}, u32[]{:S(2)}, u32[]{:S(2)}) collective-permute-start(bf16[16,64,128]{2,1,0:T(8,128)(2,1)} %bitcast.10), channel_id=1, source_target_pairs={{0,2},{1,3},{2,0},{3,1},{4,6},{5,7},{6,4},{7,5},{8,10},{9,11},{10,... | collective-permute-start | bytes 786440 | tf_op jit(solution)/shard_map/ppermute | solution.py:372
  3.0 12.1 %collective-permute-start.4 = (bf16[16,64,128]{2,1,0:T(8,128)(2,1)}, bf16[16,64,128]{2,1,0:T(8,128)(2,1)S(1)}, u32[]{:S(2)}, u32[]{:S(2)}) collective-permute-start(bf16[16,64,128]{2,1,0:T(8,128)(2,1)} %bitcast.11), channel_id=1, source_target_pairs={{0,1},{1,0},{2,3},{3,2},{4,5},{5,4},{6,7},{7,6},{8,9},{9,8},{10,11... | collective-permute-start | bytes 786440 | tf_op jit(solution)/shard_map/ppermute | solution.py:372
  3.9 10.4 %collective-permute-start.1 = (bf16[2,3,64,128]{3,2,1,0:T(8,128)(2,1)S(1)}, bf16[2,3,64,128]{3,2,1,0:T(8,128)(2,1)S(1)}, u32[]{:S(2)}, u32[]{:S(2)}) collective-permute-start(bf16[2,3,64,128]{3,2,1,0:T(8,128)(2,1)S(1)} %get-tuple-element.63), channel_id=1, source_target_pairs={{4,0},{8,4},{12,8},{16,12},{20,16},{24,20},{28,24},{5,1},{9,5},{13... | collective-permute-start | bytes 294920 | tf_op jit(solution)/shard_map/ppermute | solution.py:404
  5.2 9.1 %collective-permute-start = (bf16[2,3,64,128]{3,2,1,0:T(8,128)(2,1)S(1)}, bf16[2,3,64,128]{3,2,1,0:T(8,128)(2,1)S(1)}, u32[]{:S(2)}, u32[]{:S(2)}) collective-permute-start(bf16[2,3,64,128]{3,2,1,0:T(8,128)(2,1)S(1)} %get-tuple-element.64), channel_id=1, source_target_pairs={{0,4},{4,8},{8,12},{12,16},{16,20},{20,24},{24,28},{1,5},{5,9},{9,... | collective-permute-start | bytes 294920 | tf_op jit(solution)/shard_map/ppermute | solution.py:403
  11.3 3.7 %collective-permute-start.5 = (bf16[16,64,128]{2,1,0:T(8,128)(2,1)S(1)}, bf16[16,64,128]{2,1,0:T(8,128)(2,1)S(1)}, u32[]{:S(2)}, u32[]{:S(2)}) collective-permute-start(bf16[16,64,128]{2,1,0:T(8,128)(2,1)S(1)} %collective-permute-done.3.refs_1_), channel_id=1, source_target_pairs={{0,1},{1,0},{2,3},{3,2},{4,5},{5,4},{6,7},{7,6},{8,9},{9,8},{10,11... | collective-permute-start | bytes 786440 | tf_op jit(solution)/shard_map/ppermute | solution.py:372
  11.4 1.0 %copy-start = (bf16[2,8,64,128]{3,2,1,0:T(8,128)(2,1)S(1)}, bf16[2,8,64,128]{3,2,1,0:T(8,128)(2,1)}, u32[]{:S(2)}) copy-start(bf16[2,8,64,128]{3,2,1,0:T(8,128)(2,1)} %param.6) | copy-start | bytes 786436
  12.4 1.0 %copy-start.1 = (bf16[3,3,3,64,64]{4,3,2,1,0:T(8,128)(2,1)S(1)}, bf16[3,3,3,64,64]{4,3,2,1,0:T(8,128)(2,1)}, u32[]{:S(2)}) copy-start(bf16[3,3,3,64,64]{4,3,2,1,0:T(8,128)(2,1)} %filter_ref.1) | copy-start | bytes 663556
  13.4 0.7 %copy-start.2 = (f32[3,64]{1,0:T(4,128)S(1)}, f32[3,64]{1,0:T(4,128)}, u32[]{:S(2)}) copy-start(f32[3,64]{1,0:T(4,128)} %bias_ref.1) | copy-start | bytes 2308
  14.4 7.7 %collective-permute-start.2 = (bf16[13,64,128]{2,1,0:T(8,128)(2,1)S(1)}, bf16[13,64,128]{2,1,0:T(8,128)(2,1)S(1)}, u32[]{:S(2)}, u32[]{:S(2)}) collective-permute-start(bf16[13,64,128]{2,1,0:T(8,128)(2,1)S(1)} %pad_maximum_fusion.refs_2_), channel_id=1, source_target_pairs={{0,2},{1,3},{2,0},{3,1},{4,6},{5,7},{6,4},{7,5},{8,10},{9,11},{10,... | collective-permute-start | bytes 638984 | tf_op jit(solution)/shard_map/ppermute | solution.py:372
  14.7 7.4 %collective-permute-start.6 = (bf16[13,64,128]{2,1,0:T(8,128)(2,1)S(1)}, bf16[13,64,128]{2,1,0:T(8,128)(2,1)S(1)}, u32[]{:S(2)}, u32[]{:S(2)}) collective-permute-start(bf16[13,64,128]{2,1,0:T(8,128)(2,1)S(1)} %pad_maximum_fusion.refs_2_), channel_id=1, source_target_pairs={{0,1},{1,0},{2,3},{3,2},{4,5},{5,4},{6,7},{7,6},{8,9},{9,8},{10,11... | collective-permute-start | bytes 638984 | tf_op jit(solution)/shard_map/ppermute | solution.py:372
  22.1 13.5 %copy-start.3 = (s32[2]{0:T(128)S(1)}, s32[2]{0:T(128)}, u32[]{:S(2)}) copy-start(s32[2]{0:T(128)} %charge_ref.7) | copy-start | bytes 28
  22.1 1.5 %collective-permute-start.7 = (bf16[13,64,128]{2,1,0:T(8,128)(2,1)S(1)}, bf16[13,64,128]{2,1,0:T(8,128)(2,1)S(1)}, u32[]{:S(2)}, u32[]{:S(2)}) collective-permute-start(bf16[13,64,128]{2,1,0:T(8,128)(2,1)S(1)} %collective-permute-done.2.refs_3_), channel_id=1, source_target_pairs={{0,1},{1,0},{2,3},{3,2},{4,5},{5,4},{6,7},{7,6},{8,9},{9,8},{10,11... | collective-permute-start | bytes 638984 | tf_op jit(solution)/shard_map/ppermute | solution.py:372
  31.5 14.7 %collective-permute-start.10 = (bf16[8,128,128]{2,1,0:T(8,128)(2,1)S(1)}, bf16[8,128,128]{2,1,0:T(8,128)(2,1)S(1)}, u32[]{:S(2)}, u32[]{:S(2)}) collective-permute-start(bf16[8,128,128]{2,1,0:T(8,128)(2,1)S(1)} %get-tuple-element.52.refs_0_), channel_id=1, source_target_pairs={{0,12},{4,0},{8,4},{12,8},{16,28},{20,16},{24,20},{28,24},{1,13},{... | collective-permute-start | bytes 786440 | tf_op jit(solution)/shard_map/ppermute | solution.py:470
  34.9 12.4 %collective-permute-start.9 = (bf16[8,128,128]{2,1,0:T(8,128)(2,1)S(1)}, bf16[8,128,128]{2,1,0:T(8,128)(2,1)S(1)}, u32[]{:S(2)}, u32[]{:S(2)}) collective-permute-start(bf16[8,128,128]{2,1,0:T(8,128)(2,1)S(1)} %get-tuple-element.52.refs_0_), channel_id=1, source_target_pairs={{0,8},{4,12},{8,0},{12,4},{16,24},{20,28},{24,16},{28,20},{1,9},{5... | collective-permute-start | bytes 786440 | tf_op jit(solution)/shard_map/ppermute | solution.py:470
  35.4 12.0 %collective-permute-start.8 = (bf16[8,128,128]{2,1,0:T(8,128)(2,1)S(1)}, bf16[8,128,128]{2,1,0:T(8,128)(2,1)S(1)}, u32[]{:S(2)}, u32[]{:S(2)}) collective-permute-start(bf16[8,128,128]{2,1,0:T(8,128)(2,1)S(1)} %get-tuple-element.52.refs_0_), channel_id=1, source_target_pairs={{0,4},{4,8},{8,12},{12,0},{16,20},{20,24},{24,28},{28,16},{1,5},{5... | collective-permute-start | bytes 786440 | tf_op jit(solution)/shard_map/ppermute | solution.py:470
  48.7 7.6 %collective-permute-start.11 = (bf16[128,128]{1,0:T(8,128)(2,1)S(1)}, bf16[128,128]{1,0:T(8,128)(2,1)S(1)}, u32[]{:S(2)}, u32[]{:S(2)}) collective-permute-start(bf16[128,128]{1,0:T(8,128)(2,1)S(1)} %get-tuple-element.59), channel_id=1, source_target_pairs={{0,16},{4,20},{8,24},{12,28},{16,0},{20,4},{24,8},{28,12},{1,17},{... | collective-permute-start | bytes 98312 | tf_op jit(solution)/shard_map/ppermute | solution.py:500

commit v7 on v6

--- a/solution.py
+++ b/solution.py
@@ -263,7 +263,7 @@
                 return tuple(fresh), tuple(ahead)
 
             carry = (state, tuple(cost_at(first_step)))
-            sums = lax.fori_loop(0, width, body, carry, unroll=32)[0]
+            sums = lax.fori_loop(0, width, body, carry, unroll=64)[0]
             least = least_of(list(sums))
             return tuple(s - least for s in sums)
 

time: 59.3 us -> 59 us (level)
  Pallas kernels: 30.3 us -> 29.2 us
  waiting for transfers between devices: 7.03 us -> 7.87 us
    ppermute x3, waiting for transfers between devices: 1.23 us -> 2.08 us  [per_device(): blocks.append(lax.ppermute(own, 'row', turn))]
    pallas_call x1, Pallas kernels: 10.6 us -> 9.74 us  [per_device(): call(functools.partial(across_kernel, False), halves, [SMEM(), SMEM(), VM...]
  transfers between devices with their start and end apart: 12 -> 12, of which waited for: 3 -> 3; matrix products, arithmetic and copies ran while one was open for 3% -> 3% of each run, Pallas kernels for 31% -> 30%
where the time goes in v7:
time: 59 us; the launch traced here: 58.7 us
  Pallas kernels  29.2 us (49%)
  starting transfers between devices  16.2 us (27%)
  waiting for transfers between devices  7.87 us (13%)
  local copies, waits for them, and re-layouts  3.86 us (7%)
  other arithmetic  0.8 us (1%)
  between operations  0.78 us (1%)
    pallas_call x1, Pallas kernels, per_device(): call(functools.partial(across_kernel, False), halves, [SMEM(), SMEM(), VM...  9.74 us
    pallas_call x1, Pallas kernels, per_device(): call(functools.partial(band_kernel, masks), (jax.ShapeDtypeStruct((cols *...  7.9 us
    ppermute x6, waiting for transfers between devices, spread(): blocks += [lax.ppermute(held, 'col', route) for held in blocks]  5.78 us
    pallas_call x1, Pallas kernels, per_device(): call(functools.partial(across_kernel, True), halves, [SMEM(), SMEM(), VME...  4.64 us
    ppermute x1, starting transfers between devices, per_device(): before = lax.ppermute(activations[:, rows - layers:], 'row', downward)  4.55 us
    ppermute x3, starting transfers between devices, per_device(): blocks.append(lax.ppermute(own, 'row', turn))  4.1 us
    ppermute x6, starting transfers between devices, spread(): blocks += [lax.ppermute(held, 'col', route) for held in blocks]  3.58 us
    pallas_call x1, Pallas kernels, per_device(): call(functools.partial(inner_kernel, masks), tuple((jax.ShapeDtypeStruct(...  2.7 us
  transfers between devices with their start and end apart: 12, of which 3 were waited for; matrix products, arithmetic and copies ran while one was open for 3% of the time, Pallas kernels for 30%

profile of v7, /device:TPU:0, one launch (start us, length us, event | category | flops | bytes accessed | tf_op | source)
XLA Modules:
  0.0 58.7 jit_solution(11181894388023022995)
XLA Ops:
  0.0 3.0 %collective-permute-start.3 = (bf16[16,64,128]{2,1,0:T(8,128)(2,1)}, bf16[16,64,128]{2,1,0:T(8,128)(2,1)S(1)}, u32[]{:S(2)}, u32[]{:S(2)}) collective-permute-start(bf16[16,64,128]{2,1,0:T(8,128)(2,1)} %bitcast.10), channel_id=1, source_target_pairs={{0,2},{1,3},{2,0},{3,1},{4,6},{5,7},{6,4},{7,5},{8,10},{9,11},{10,... | collective-permute-start | bytes 786440 | tf_op jit(solution)/shard_map/ppermute | solution.py:372
  3.0 0.0 collective-permute-start.4
  3.0 1.0 %fusion = (bf16[2,3,64,128]{3,2,1,0:T(8,128)(2,1)S(1)}, bf16[2,3,64,128]{3,2,1,0:T(8,128)(2,1)S(1)}) fusion(bf16[2,8,64,128]{3,2,1,0:T(8,128)(2,1)} %param.6), kind=kLoop, calls=%fused_computation.2 | loop fusion | bytes 393216 | tf_op jit(solution)/shard_map/slice | solution.py:404
  3.9 1.3 %collective-permute-start.1 = (bf16[2,3,64,128]{3,2,1,0:T(8,128)(2,1)S(1)}, bf16[2,3,64,128]{3,2,1,0:T(8,128)(2,1)S(1)}, u32[]{:S(2)}, u32[]{:S(2)}) collective-permute-start(bf16[2,3,64,128]{3,2,1,0:T(8,128)(2,1)S(1)} %get-tuple-element.63), channel_id=1, source_target_pairs={{4,0},{8,4},{12,8},{16,12},{20,16},{24,20},{28,24},{5,1},{9,5},{13... | collective-permute-start | bytes 294920 | tf_op jit(solution)/shard_map/ppermute | solution.py:404
  5.2 4.6 %collective-permute-start = (bf16[2,3,64,128]{3,2,1,0:T(8,128)(2,1)S(1)}, bf16[2,3,64,128]{3,2,1,0:T(8,128)(2,1)S(1)}, u32[]{:S(2)}, u32[]{:S(2)}) collective-permute-start(bf16[2,3,64,128]{3,2,1,0:T(8,128)(2,1)S(1)} %get-tuple-element.64), channel_id=1, source_target_pairs={{0,4},{4,8},{8,12},{12,16},{16,20},{20,24},{24,28},{1,5},{5,9},{9,... | collective-permute-start | bytes 294920 | tf_op jit(solution)/shard_map/ppermute | solution.py:403
  10.5 0.1 pad.5.clone
  10.6 0.1 pad.4.clone
  10.6 0.7 %convert_element_type.6 = bf16[8,128]{1,0:T(8,128)(2,1)S(1)} convert(s32[8,128]{1,0:T(8,128)} %param.9) | non-fusion elementwise | flops 1024 | bytes 6144 | tf_op jit(solution)/shard_map/convert_element_type | solution.py:422
  11.3 0.1 maximum_bitcast_fusion
  11.4 0.0 copy-start
  11.4 0.9 %copy-done = bf16[2,8,64,128]{3,2,1,0:T(8,128)(2,1)S(1)} copy-done((bf16[2,8,64,128]{3,2,1,0:T(8,128)(2,1)S(1)}, bf16[2,8,64,128]{3,2,1,0:T(8,128)(2,1)}, u32[]{:S(2)}) %copy-start) | copy-done | bytes 262168
  12.4 1.0 %copy-done.1 = bf16[3,3,3,64,64]{4,3,2,1,0:T(8,128)(2,1)S(1)} copy-done((bf16[3,3,3,64,64]{4,3,2,1,0:T(8,128)(2,1)S(1)}, bf16[3,3,3,64,64]{4,3,2,1,0:T(8,128)(2,1)}, u32[]{:S(2)}) %copy-start.1) | copy-done | bytes 221208
  13.4 0.7 %copy-done.2 = f32[3,64]{1,0:T(4,128)S(1)} copy-done((f32[3,64]{1,0:T(4,128)S(1)}, f32[3,64]{1,0:T(4,128)}, u32[]{:S(2)}) %copy-start.2) | copy-done | bytes 792
  14.1 0.2 shard_map.64
  14.3 0.0 collective-permute-done
  14.4 0.3 collective-permute-start.2
  14.6 0.1 stack.19.place_ref
  14.7 0.4 collective-permute-start.6
  15.1 2.7 %shard_map.65 = (bf16[2,512,512]{2,1,0:T(8,128)(2,1)S(1)}, bf16[2,384,512]{2,1,0:T(8,128)(2,1)S(1)}, bf16[2,256,512]{2,1,0:T(8,128)(2,1)S(1)}) custom-call(s32[7]{0:T(128)S(1)} %stack.19.place_ref, bf16[3,192,192]{2,1,0:T(8,128)(2,1)S(1)} %get-tuple-element.37.taps_ref, f32[3,64,1]{2,1,0:T(8,128)S(1)} %get-tuple-element.38.shift_ref.bias_ref, ...), custom_call_target="tpu_custom_call" | custom-call | flops 2000000000 | bytes 4194304 | tf_op jit(solution)/shard_map/pallas_call | solution.py:435
  17.8 4.3 %collective-permute-done.2.refs_3_ = bf16[13,64,128]{2,1,0:T(8,128)(2,1)S(1)} collective-permute-done((bf16[13,64,128]{2,1,0:T(8,128)(2,1)S(1)}, bf16[13,64,128]{2,1,0:T(8,128)(2,1)S(1)}, u32[]{:S(2)}, u32[]{:S(2)}) %collective-permute-start.2) | collective-permute-done | bytes 213024 | tf_op jit(solution)/shard_map/ppermute | solution.py:372
  22.1 1.5 %collective-permute-done.7.refs_5_ = bf16[13,64,128]{2,1,0:T(8,128)(2,1)S(1)} collective-permute-done((bf16[13,64,128]{2,1,0:T(8,128)(2,1)S(1)}, bf16[13,64,128]{2,1,0:T(8,128)(2,1)S(1)}, u32[]{:S(2)}, u32[]{:S(2)}) %collective-permute-start.7) | collective-permute-done | bytes 213024 | tf_op jit(solution)/shard_map/ppermute | solution.py:372
  23.6 7.9 %shard_map.66 = (f32[4096,128]{1,0:T(8,128)S(1)}, bf16[8,128,128]{2,1,0:T(8,128)(2,1)S(1)}) custom-call(s32[7]{0:T(128)S(1)} %stack.19.place_ref, bf16[3,192,192]{2,1,0:T(8,128)(2,1)S(1)} %get-tuple-element.37.taps_ref, f32[3,64,1]{2,1,0:T(8,128)S(1)} %get-tuple-element.38.shift_ref.bias_ref, bf16[2,512,512]{2,1,0:T(8,128)(2,1)S(1)} %get-tuple-element.45.rows_ref, ...), custom_call_target="tpu_custom_call" | custom-call | flops 10000000000 | bytes 4194304 | tf_op jit(solution)/shard_map/pallas_call | solution.py:446
  31.5 3.5 %collective-permute-start.10 = (bf16[8,128,128]{2,1,0:T(8,128)(2,1)S(1)}, bf16[8,128,128]{2,1,0:T(8,128)(2,1)S(1)}, u32[]{:S(2)}, u32[]{:S(2)}) collective-permute-start(bf16[8,128,128]{2,1,0:T(8,128)(2,1)S(1)} %get-tuple-element.52.refs_0_), channel_id=1, source_target_pairs={{0,12},{4,0},{8,4},{12,8},{16,28},{20,16},{24,20},{28,24},{1,13},{... | collective-permute-start | bytes 786440 | tf_op jit(solution)/shard_map/ppermute | solution.py:470
  34.9 0.5 collective-permute-start.9
  35.4 0.2 collective-permute-start.8
  35.6 9.7 %shard_map.67 = (f32[2,1024,128]{2,1,0:T(8,128)S(1)}, f32[128,16]{1,0:T(8,128)S(1)}) custom-call(s32[7]{0:T(128)S(1)} %stack.19.place_ref, s32[2]{0:T(128)S(1)} %copy-done.3, f32[4096,128]{1,0:T(8,128)S(1)} %get-tuple-element.50.cost_ref), custom_call_target="tpu_custom_call" | custom-call | flops 10000000000 | bytes 4194304 | tf_op jit(solution)/shard_map/pallas_call | solution.py:477
  45.3 2.0 %collective-permute-done.9.refs_2_ = bf16[8,128,128]{2,1,0:T(8,128)(2,1)S(1)} collective-permute-done((bf16[8,128,128]{2,1,0:T(8,128)(2,1)S(1)}, bf16[8,128,128]{2,1,0:T(8,128)(2,1)S(1)}, u32[]{:S(2)}, u32[]{:S(2)}) %collective-permute-start.9) | collective-permute-done | bytes 262176 | tf_op jit(solution)/shard_map/ppermute | solution.py:470
  47.4 0.0 collective-permute-done.8.refs_1_
  47.4 1.3 %shard_map.68 = (f32[8,128,128]{2,1,0:T(8,128)S(1)}, bf16[128,128]{1,0:T(8,128)(2,1)S(1)}) custom-call(s32[7]{0:T(128)S(1)} %stack.19.place_ref, s32[2]{0:T(128)S(1)} %copy-done.3, bf16[8,128,128]{2,1,0:T(8,128)(2,1)S(1)} %get-tuple-element.52.refs_0_, bf16[8,128,128]{2,1,0:T(8,128)(2,1)S(1)} %collective-permute-done.8.refs_1_, ...), custom_call_target="tpu_custom_call" | custom-call | flops 2000000000 | bytes 4194304 | tf_op jit(solution)/shard_map/pallas_call | solution.py:487
  48.7 2.7 %collective-permute-start.11 = (bf16[128,128]{1,0:T(8,128)(2,1)S(1)}, bf16[128,128]{1,0:T(8,128)(2,1)S(1)}, u32[]{:S(2)}, u32[]{:S(2)}) collective-permute-start(bf16[128,128]{1,0:T(8,128)(2,1)S(1)} %get-tuple-element.59), channel_id=1, source_target_pairs={{0,16},{4,20},{8,24},{12,28},{16,0},{20,4},{24,8},{28,12},{1,17},{... | collective-permute-start | bytes 98312 | tf_op jit(solution)/shard_map/ppermute | solution.py:500
  51.4 4.6 %shard_map.69 = (f32[2,1024,128]{2,1,0:T(8,128)S(1)}, f32[128,16]{1,0:T(8,128)}) custom-call(s32[7]{0:T(128)S(1)} %stack.19.place_ref, s32[2]{0:T(128)S(1)} %copy-done.3, f32[4096,128]{1,0:T(8,128)S(1)} %get-tuple-element.50.cost_ref, f32[128,16]{1,0:T(8,128)S(1)} %get-tuple-element.61.refs_0_), custom_call_target="tpu_custom_call" | custom-call | flops 10000000000 | bytes 4194304 | tf_op jit(solution)/shard_map/pallas_call | solution.py:501
  56.0 2.7 %shard_map.70 = f32[8,128,128]{2,1,0:T(8,128)} custom-call(s32[7]{0:T(128)S(1)} %stack.19.place_ref, s32[2]{0:T(128)S(1)} %copy-done.3, bf16[8,128,128]{2,1,0:T(8,128)(2,1)S(1)} %get-tuple-element.52.refs_0_, bf16[8,128,128]{2,1,0:T(8,128)(2,1)S(1)} %collective-permute-done.8.refs_1_, bf16[8,128,128]{2,1,0:T(8,128)(2,1)S(1)} %collective-permute-done.9.refs_2_, ...), custom_call_target="tpu_custom_call" | custom-call | flops 3000000000 | bytes 4194304 | tf_op jit(solution)/shard_map/pallas_call | solution.py:509
  (16 shorter events, 0.1 us)
Async XLA Ops:
  0.0 11.3 %collective-permute-start.3 = (bf16[16,64,128]{2,1,0:T(8,128)(2,1)}, bf16[16,64,128]{2,1,0:T(8,128)(2,1)S(1)}, u32[]{:S(2)}, u32[]{:S(2)}) collective-permute-start(bf16[16,64,128]{2,1,0:T(8,128)(2,1)} %bitcast.10), channel_id=1, source_target_pairs={{0,2},{1,3},{2,0},{3,1},{4,6},{5,7},{6,4},{7,5},{8,10},{9,11},{10,... | collective-permute-start | bytes 786440 | tf_op jit(solution)/shard_map/ppermute | solution.py:372
  3.0 12.1 %collective-permute-start.4 = (bf16[16,64,128]{2,1,0:T(8,128)(2,1)}, bf16[16,64,128]{2,1,0:T(8,128)(2,1)S(1)}, u32[]{:S(2)}, u32[]{:S(2)}) collective-permute-start(bf16[16,64,128]{2,1,0:T(8,128)(2,1)} %bitcast.11), channel_id=1, source_target_pairs={{0,1},{1,0},{2,3},{3,2},{4,5},{5,4},{6,7},{7,6},{8,9},{9,8},{10,11... | collective-permute-start | bytes 786440 | tf_op jit(solution)/shard_map/ppermute | solution.py:372
  3.9 10.4 %collective-permute-start.1 = (bf16[2,3,64,128]{3,2,1,0:T(8,128)(2,1)S(1)}, bf16[2,3,64,128]{3,2,1,0:T(8,128)(2,1)S(1)}, u32[]{:S(2)}, u32[]{:S(2)}) collective-permute-start(bf16[2,3,64,128]{3,2,1,0:T(8,128)(2,1)S(1)} %get-tuple-element.63), channel_id=1, source_target_pairs={{4,0},{8,4},{12,8},{16,12},{20,16},{24,20},{28,24},{5,1},{9,5},{13... | collective-permute-start | bytes 294920 | tf_op jit(solution)/shard_map/ppermute | solution.py:404
  5.2 9.1 %collective-permute-start = (bf16[2,3,64,128]{3,2,1,0:T(8,128)(2,1)S(1)}, bf16[2,3,64,128]{3,2,1,0:T(8,128)(2,1)S(1)}, u32[]{:S(2)}, u32[]{:S(2)}) collective-permute-start(bf16[2,3,64,128]{3,2,1,0:T(8,128)(2,1)S(1)} %get-tuple-element.64), channel_id=1, source_target_pairs={{0,4},{4,8},{8,12},{12,16},{16,20},{20,24},{24,28},{1,5},{5,9},{9,... | collective-permute-start | bytes 294920 | tf_op jit(solution)/shard_map/ppermute | solution.py:403
  11.3 3.7 %collective-permute-start.5 = (bf16[16,64,128]{2,1,0:T(8,128)(2,1)S(1)}, bf16[16,64,128]{2,1,0:T(8,128)(2,1)S(1)}, u32[]{:S(2)}, u32[]{:S(2)}) collective-permute-start(bf16[16,64,128]{2,1,0:T(8,128)(2,1)S(1)} %collective-permute-done.3.refs_1_), channel_id=1, source_target_pairs={{0,1},{1,0},{2,3},{3,2},{4,5},{5,4},{6,7},{7,6},{8,9},{9,8},{10,11... | collective-permute-start | bytes 786440 | tf_op jit(solution)/shard_map/ppermute | solution.py:372
  11.4 1.0 %copy-start = (bf16[2,8,64,128]{3,2,1,0:T(8,128)(2,1)S(1)}, bf16[2,8,64,128]{3,2,1,0:T(8,128)(2,1)}, u32[]{:S(2)}) copy-start(bf16[2,8,64,128]{3,2,1,0:T(8,128)(2,1)} %param.6) | copy-start | bytes 786436
  12.4 1.0 %copy-start.1 = (bf16[3,3,3,64,64]{4,3,2,1,0:T(8,128)(2,1)S(1)}, bf16[3,3,3,64,64]{4,3,2,1,0:T(8,128)(2,1)}, u32[]{:S(2)}) copy-start(bf16[3,3,3,64,64]{4,3,2,1,0:T(8,128)(2,1)} %filter_ref.1) | copy-start | bytes 663556
  13.4 0.7 %copy-start.2 = (f32[3,64]{1,0:T(4,128)S(1)}, f32[3,64]{1,0:T(4,128)}, u32[]{:S(2)}) copy-start(f32[3,64]{1,0:T(4,128)} %bias_ref.1) | copy-start | bytes 2308
  14.4 7.7 %collective-permute-start.2 = (bf16[13,64,128]{2,1,0:T(8,128)(2,1)S(1)}, bf16[13,64,128]{2,1,0:T(8,128)(2,1)S(1)}, u32[]{:S(2)}, u32[]{:S(2)}) collective-permute-start(bf16[13,64,128]{2,1,0:T(8,128)(2,1)S(1)} %pad_maximum_fusion.refs_2_), channel_id=1, source_target_pairs={{0,2},{1,3},{2,0},{3,1},{4,6},{5,7},{6,4},{7,5},{8,10},{9,11},{10,... | collective-permute-start | bytes 638984 | tf_op jit(solution)/shard_map/ppermute | solution.py:372
  14.7 7.4 %collective-permute-start.6 = (bf16[13,64,128]{2,1,0:T(8,128)(2,1)S(1)}, bf16[13,64,128]{2,1,0:T(8,128)(2,1)S(1)}, u32[]{:S(2)}, u32[]{:S(2)}) collective-permute-start(bf16[13,64,128]{2,1,0:T(8,128)(2,1)S(1)} %pad_maximum_fusion.refs_2_), channel_id=1, source_target_pairs={{0,1},{1,0},{2,3},{3,2},{4,5},{5,4},{6,7},{7,6},{8,9},{9,8},{10,11... | collective-permute-start | bytes 638984 | tf_op jit(solution)/shard_map/ppermute | solution.py:372
  22.1 13.5 %copy-start.3 = (s32[2]{0:T(128)S(1)}, s32[2]{0:T(128)}, u32[]{:S(2)}) copy-start(s32[2]{0:T(128)} %charge_ref.7) | copy-start | bytes 28
  22.1 1.5 %collective-permute-start.7 = (bf16[13,64,128]{2,1,0:T(8,128)(2,1)S(1)}, bf16[13,64,128]{2,1,0:T(8,128)(2,1)S(1)}, u32[]{:S(2)}, u32[]{:S(2)}) collective-permute-start(bf16[13,64,128]{2,1,0:T(8,128)(2,1)S(1)} %collective-permute-done.2.refs_3_), channel_id=1, source_target_pairs={{0,1},{1,0},{2,3},{3,2},{4,5},{5,4},{6,7},{7,6},{8,9},{9,8},{10,11... | collective-permute-start | bytes 638984 | tf_op jit(solution)/shard_map/ppermute | solution.py:372
  31.5 13.9 %collective-permute-start.10 = (bf16[8,128,128]{2,1,0:T(8,128)(2,1)S(1)}, bf16[8,128,128]{2,1,0:T(8,128)(2,1)S(1)}, u32[]{:S(2)}, u32[]{:S(2)}) collective-permute-start(bf16[8,128,128]{2,1,0:T(8,128)(2,1)S(1)} %get-tuple-element.52.refs_0_), channel_id=1, source_target_pairs={{0,12},{4,0},{8,4},{12,8},{16,28},{20,16},{24,20},{28,24},{1,13},{... | collective-permute-start | bytes 786440 | tf_op jit(solution)/shard_map/ppermute | solution.py:470
  34.9 12.4 %collective-permute-start.9 = (bf16[8,128,128]{2,1,0:T(8,128)(2,1)S(1)}, bf16[8,128,128]{2,1,0:T(8,128)(2,1)S(1)}, u32[]{:S(2)}, u32[]{:S(2)}) collective-permute-start(bf16[8,128,128]{2,1,0:T(8,128)(2,1)S(1)} %get-tuple-element.52.refs_0_), channel_id=1, source_target_pairs={{0,8},{4,12},{8,0},{12,4},{16,24},{20,28},{24,16},{28,20},{1,9},{5... | collective-permute-start | bytes 786440 | tf_op jit(solution)/shard_map/ppermute | solution.py:470
  35.4 12.0 %collective-permute-start.8 = (bf16[8,128,128]{2,1,0:T(8,128)(2,1)S(1)}, bf16[8,128,128]{2,1,0:T(8,128)(2,1)S(1)}, u32[]{:S(2)}, u32[]{:S(2)}) collective-permute-start(bf16[8,128,128]{2,1,0:T(8,128)(2,1)S(1)} %get-tuple-element.52.refs_0_), channel_id=1, source_target_pairs={{0,4},{4,8},{8,12},{12,0},{16,20},{20,24},{24,28},{28,16},{1,5},{5... | collective-permute-start | bytes 786440 | tf_op jit(solution)/shard_map/ppermute | solution.py:470
  48.7 7.3 %collective-permute-start.11 = (bf16[128,128]{1,0:T(8,128)(2,1)S(1)}, bf16[128,128]{1,0:T(8,128)(2,1)S(1)}, u32[]{:S(2)}, u32[]{:S(2)}) collective-permute-start(bf16[128,128]{1,0:T(8,128)(2,1)S(1)} %get-tuple-element.59), channel_id=1, source_target_pairs={{0,16},{4,20},{8,24},{12,28},{16,0},{20,4},{24,8},{28,12},{1,17},{... | collective-permute-start | bytes 98312 | tf_op jit(solution)/shard_map/ppermute | solution.py:500

commit v8 on v7

--- a/solution.py
+++ b/solution.py
@@ -207,7 +207,7 @@
 
 
 def early_segments(parts):
-    return parts - parts // 4
+    return 2 * parts - parts // 4
 
 
 def across_kernel(second, place_ref, charge_ref, cost_ref, *refs):
@@ -243,7 +243,10 @@
         )
 
     def segment(p, state):
-        first_step = p * width
+        half = width // 2
+        first_step = p * half
+        tile = p // 2
+        inner = (p % 2) * half
 
         def run(keep_right, keep_left, state):
             def body(i, carry):
@@ -257,17 +260,17 @@
                 if keep_right or keep_left:
                     back = jnp.concatenate([f - least for f in fresh], axis=0).T
                 if keep_right:
-                    kept_ref[0, at(i)] = back[0:rows]
+                    kept_ref[0, at(inner + i)] = back[0:rows]
                 if keep_left:
-                    kept_ref[1, at(width - 1 - i)] = back[rows : 2 * rows]
+                    kept_ref[1, at(width - 1 - inner - i)] = back[rows : 2 * rows]
                 return tuple(fresh), tuple(ahead)
 
             carry = (state, tuple(cost_at(first_step)))
-            sums = lax.fori_loop(0, width, body, carry, unroll=64)[0]
+            sums = lax.fori_loop(0, half, body, carry, unroll=64)[0]
             least = least_of(list(sums))
             return tuple(s - least for s in sums)
 
-        choice = jnp.where(p == own, 1, 0) + jnp.where(parts - 1 - p == own, 2, 0)
+        choice = jnp.where(tile == own, 1, 0) + jnp.where(parts - 1 - tile == own, 2, 0)
         return lax.switch(
             choice,
             [functools.partial(run, k == 1, k == 2) for k in range(3)],
@@ -276,7 +279,7 @@
 
     if second:
         state = tuple(registers(refs[0][...]))
-        span = (early, parts)
+        span = (early, 2 * parts)
     else:
         state = tuple(jnp.zeros((SUB, 2 * rows), jnp.float32) for _ in range(REGS))
         span = (0, early)
@@ -338,8 +341,9 @@
     down_or_up(place_ref[3] != 0, place_ref[4], cost_ref, state, p1, p2, keep)
     lane = lax.broadcasted_iota(jnp.int32, (width, DISPARITIES), 1)
     index = disparity_to_lane(lane)
-    right_early = place_ref[2] < place_ref[6]
-    left_early = place_ref[5] - 1 - place_ref[2] < place_ref[6]
+    column = place_ref[2] * width + lax.broadcasted_iota(jnp.int32, (width, DISPARITIES), 0)
+    right_early = column < place_ref[6]
+    left_early = place_ref[5] * width - 1 - column < place_ref[6]
     for row in range(rows):
         this = pl.ds(row, width, stride=rows)
         right = jnp.where(right_early, early_ref[0, this, :], late_ref[0, this, :])
@@ -394,7 +398,7 @@
             row_rank // half,
             row_rank % half,
             jnp.int32(parts),
-            jnp.int32(early_segments(parts)),
+            jnp.int32(early_segments(parts) * (width // 2)),
         ]
     ).astype(jnp.int32)
 

time: 59 us -> 57.1 us (0.968)
  waiting for transfers between devices: 7.87 us -> 6.59 us
  Pallas kernels: 29.2 us -> 28.6 us
    pallas_call x1, Pallas kernels: 4.64 us -> 2.74 us  [per_device(): call(functools.partial(across_kernel, True), halves, [SMEM(), SMEM(), VME...]
    pallas_call x1, Pallas kernels: 9.74 us -> 11 us  [per_device(): call(functools.partial(across_kernel, False), halves, [SMEM(), SMEM(), VM...]
    ppermute x3, waiting for transfers between devices: 2.08 us -> 0.8 us  [per_device(): blocks.append(lax.ppermute(own, 'row', turn))]
  transfers between devices with their start and end apart: 12 -> 12, of which waited for: 3 -> 3; matrix products, arithmetic and copies ran while one was open for 3% -> 4% of each run, Pallas kernels for 30% -> 29%
where the time goes in v8:
time: 57.1 us; the launch traced here: 56.8 us
  Pallas kernels  28.6 us (50%)
  starting transfers between devices  16.2 us (28%)
  waiting for transfers between devices  6.59 us (12%)
  local copies, waits for them, and re-layouts  3.86 us (7%)
  other arithmetic  0.8 us (1%)
  between operations  0.78 us (1%)
    pallas_call x1, Pallas kernels, per_device(): call(functools.partial(across_kernel, False), halves, [SMEM(), SMEM(), VM...  11 us
    pallas_call x1, Pallas kernels, per_device(): call(functools.partial(band_kernel, masks), (jax.ShapeDtypeStruct((cols *...  7.9 us
    ppermute x6, waiting for transfers between devices, spread(): blocks += [lax.ppermute(held, 'col', route) for held in blocks]  5.78 us
    ppermute x1, starting transfers between devices, per_device(): before = lax.ppermute(activations[:, rows - layers:], 'row', downward)  4.55 us
    ppermute x3, starting transfers between devices, per_device(): blocks.append(lax.ppermute(own, 'row', turn))  4.11 us
    ppermute x6, starting transfers between devices, spread(): blocks += [lax.ppermute(held, 'col', route) for held in blocks]  3.58 us
    pallas_call x1, Pallas kernels, per_device(): call(functools.partial(across_kernel, True), halves, [SMEM(), SMEM(), VME...  2.74 us
    pallas_call x1, Pallas kernels, per_device(): call(second_vertical_kernel, jax.ShapeDtypeStruct((rows, width, DISPARITI...  2.71 us
  transfers between devices with their start and end apart: 12, of which 3 were waited for; matrix products, arithmetic and copies ran while one was open for 4% of the time, Pallas kernels for 29%

profile of v8, /device:TPU:0, one launch (start us, length us, event | category | flops | bytes accessed | tf_op | source)
XLA Modules:
  0.0 56.8 jit_solution(4379013332930127346)
XLA Ops:
  0.0 3.0 %collective-permute-start.3 = (bf16[16,64,128]{2,1,0:T(8,128)(2,1)}, bf16[16,64,128]{2,1,0:T(8,128)(2,1)S(1)}, u32[]{:S(2)}, u32[]{:S(2)}) collective-permute-start(bf16[16,64,128]{2,1,0:T(8,128)(2,1)} %bitcast.10), channel_id=1, source_target_pairs={{0,2},{1,3},{2,0},{3,1},{4,6},{5,7},{6,4},{7,5},{8,10},{9,11},{10,... | collective-permute-start | bytes 786440 | tf_op jit(solution)/shard_map/ppermute | solution.py:376
  3.0 1.0 %fusion = (bf16[2,3,64,128]{3,2,1,0:T(8,128)(2,1)S(1)}, bf16[2,3,64,128]{3,2,1,0:T(8,128)(2,1)S(1)}) fusion(bf16[2,8,64,128]{3,2,1,0:T(8,128)(2,1)} %param.6), kind=kLoop, calls=%fused_computation.2 | loop fusion | bytes 393216 | tf_op jit(solution)/shard_map/slice | solution.py:408
  3.9 1.3 %collective-permute-start.1 = (bf16[2,3,64,128]{3,2,1,0:T(8,128)(2,1)S(1)}, bf16[2,3,64,128]{3,2,1,0:T(8,128)(2,1)S(1)}, u32[]{:S(2)}, u32[]{:S(2)}) collective-permute-start(bf16[2,3,64,128]{3,2,1,0:T(8,128)(2,1)S(1)} %get-tuple-element.63), channel_id=1, source_target_pairs={{4,0},{8,4},{12,8},{16,12},{20,16},{24,20},{28,24},{5,1},{9,5},{13... | collective-permute-start | bytes 294920 | tf_op jit(solution)/shard_map/ppermute | solution.py:408
  5.2 4.6 %collective-permute-start = (bf16[2,3,64,128]{3,2,1,0:T(8,128)(2,1)S(1)}, bf16[2,3,64,128]{3,2,1,0:T(8,128)(2,1)S(1)}, u32[]{:S(2)}, u32[]{:S(2)}) collective-permute-start(bf16[2,3,64,128]{3,2,1,0:T(8,128)(2,1)S(1)} %get-tuple-element.64), channel_id=1, source_target_pairs={{0,4},{4,8},{8,12},{12,16},{16,20},{20,24},{24,28},{1,5},{5,9},{9,... | collective-permute-start | bytes 294920 | tf_op jit(solution)/shard_map/ppermute | solution.py:407
  10.5 0.1 pad.5.clone
  10.6 0.1 pad.4.clone
  10.6 0.7 %convert_element_type.6 = bf16[8,128]{1,0:T(8,128)(2,1)S(1)} convert(s32[8,128]{1,0:T(8,128)} %param.9) | non-fusion elementwise | flops 1024 | bytes 6144 | tf_op jit(solution)/shard_map/convert_element_type | solution.py:426
  11.3 0.0 collective-permute-start.5
  11.3 0.1 maximum_bitcast_fusion
  11.4 0.0 copy-start
  11.4 0.9 %copy-done = bf16[2,8,64,128]{3,2,1,0:T(8,128)(2,1)S(1)} copy-done((bf16[2,8,64,128]{3,2,1,0:T(8,128)(2,1)S(1)}, bf16[2,8,64,128]{3,2,1,0:T(8,128)(2,1)}, u32[]{:S(2)}) %copy-start) | copy-done | bytes 262168
  12.4 1.0 %copy-done.1 = bf16[3,3,3,64,64]{4,3,2,1,0:T(8,128)(2,1)S(1)} copy-done((bf16[3,3,3,64,64]{4,3,2,1,0:T(8,128)(2,1)S(1)}, bf16[3,3,3,64,64]{4,3,2,1,0:T(8,128)(2,1)}, u32[]{:S(2)}) %copy-start.1) | copy-done | bytes 221208
  13.4 0.7 %copy-done.2 = f32[3,64]{1,0:T(4,128)S(1)} copy-done((f32[3,64]{1,0:T(4,128)S(1)}, f32[3,64]{1,0:T(4,128)}, u32[]{:S(2)}) %copy-start.2) | copy-done | bytes 792
  14.1 0.2 shard_map.64
  14.3 0.0 collective-permute-done.1
  14.4 0.3 collective-permute-start.2
  14.6 0.1 stack.19.place_ref
  14.7 0.4 collective-permute-start.6
  15.1 2.7 %shard_map.65 = (bf16[2,512,512]{2,1,0:T(8,128)(2,1)S(1)}, bf16[2,384,512]{2,1,0:T(8,128)(2,1)S(1)}, bf16[2,256,512]{2,1,0:T(8,128)(2,1)S(1)}) custom-call(s32[7]{0:T(128)S(1)} %stack.19.place_ref, bf16[3,192,192]{2,1,0:T(8,128)(2,1)S(1)} %get-tuple-element.37.taps_ref, f32[3,64,1]{2,1,0:T(8,128)S(1)} %get-tuple-element.38.shift_ref.bias_ref, ...), custom_call_target="tpu_custom_call" | custom-call | flops 2000000000 | bytes 4194304 | tf_op jit(solution)/shard_map/pallas_call | solution.py:439
  17.8 4.3 %collective-permute-done.2.refs_3_ = bf16[13,64,128]{2,1,0:T(8,128)(2,1)S(1)} collective-permute-done((bf16[13,64,128]{2,1,0:T(8,128)(2,1)S(1)}, bf16[13,64,128]{2,1,0:T(8,128)(2,1)S(1)}, u32[]{:S(2)}, u32[]{:S(2)}) %collective-permute-start.2) | collective-permute-done | bytes 213024 | tf_op jit(solution)/shard_map/ppermute | solution.py:376
  22.1 1.5 %collective-permute-done.7.refs_5_ = bf16[13,64,128]{2,1,0:T(8,128)(2,1)S(1)} collective-permute-done((bf16[13,64,128]{2,1,0:T(8,128)(2,1)S(1)}, bf16[13,64,128]{2,1,0:T(8,128)(2,1)S(1)}, u32[]{:S(2)}, u32[]{:S(2)}) %collective-permute-start.7) | collective-permute-done | bytes 213024 | tf_op jit(solution)/shard_map/ppermute | solution.py:376
  23.6 7.9 %shard_map.66 = (f32[4096,128]{1,0:T(8,128)S(1)}, bf16[8,128,128]{2,1,0:T(8,128)(2,1)S(1)}) custom-call(s32[7]{0:T(128)S(1)} %stack.19.place_ref, bf16[3,192,192]{2,1,0:T(8,128)(2,1)S(1)} %get-tuple-element.37.taps_ref, f32[3,64,1]{2,1,0:T(8,128)S(1)} %get-tuple-element.38.shift_ref.bias_ref, bf16[2,512,512]{2,1,0:T(8,128)(2,1)S(1)} %get-tuple-element.45.rows_ref, ...), custom_call_target="tpu_custom_call" | custom-call | flops 10000000000 | bytes 4194304 | tf_op jit(solution)/shard_map/pallas_call | solution.py:450
  31.5 3.5 %collective-permute-start.10 = (bf16[8,128,128]{2,1,0:T(8,128)(2,1)S(1)}, bf16[8,128,128]{2,1,0:T(8,128)(2,1)S(1)}, u32[]{:S(2)}, u32[]{:S(2)}) collective-permute-start(bf16[8,128,128]{2,1,0:T(8,128)(2,1)S(1)} %get-tuple-element.52.refs_0_), channel_id=1, source_target_pairs={{0,12},{4,0},{8,4},{12,8},{16,28},{20,16},{24,20},{28,24},{1,13},{... | collective-permute-start | bytes 786440 | tf_op jit(solution)/shard_map/ppermute | solution.py:474
  34.9 0.5 collective-permute-start.9
  35.4 0.2 collective-permute-start.8
  35.6 11.0 %shard_map.67 = (f32[2,1024,128]{2,1,0:T(8,128)S(1)}, f32[128,16]{1,0:T(8,128)S(1)}) custom-call(s32[7]{0:T(128)S(1)} %stack.19.place_ref, s32[2]{0:T(128)S(1)} %copy-done.3, f32[4096,128]{1,0:T(8,128)S(1)} %get-tuple-element.50.cost_ref), custom_call_target="tpu_custom_call" | custom-call | flops 10000000000 | bytes 4194304 | tf_op jit(solution)/shard_map/pallas_call | solution.py:481
  46.6 0.8 %collective-permute-done.9.refs_2_ = bf16[8,128,128]{2,1,0:T(8,128)(2,1)S(1)} collective-permute-done((bf16[8,128,128]{2,1,0:T(8,128)(2,1)S(1)}, bf16[8,128,128]{2,1,0:T(8,128)(2,1)S(1)}, u32[]{:S(2)}, u32[]{:S(2)}) %collective-permute-start.9) | collective-permute-done | bytes 262176 | tf_op jit(solution)/shard_map/ppermute | solution.py:474
  47.4 0.0 collective-permute-done.8.refs_1_
  47.4 1.3 %shard_map.68 = (f32[8,128,128]{2,1,0:T(8,128)S(1)}, bf16[128,128]{1,0:T(8,128)(2,1)S(1)}) custom-call(s32[7]{0:T(128)S(1)} %stack.19.place_ref, s32[2]{0:T(128)S(1)} %copy-done.3, bf16[8,128,128]{2,1,0:T(8,128)(2,1)S(1)} %get-tuple-element.52.refs_0_, bf16[8,128,128]{2,1,0:T(8,128)(2,1)S(1)} %collective-permute-done.8.refs_1_, ...), custom_call_target="tpu_custom_call" | custom-call | flops 2000000000 | bytes 4194304 | tf_op jit(solution)/shard_map/pallas_call | solution.py:491
  48.7 2.7 %collective-permute-start.11 = (bf16[128,128]{1,0:T(8,128)(2,1)S(1)}, bf16[128,128]{1,0:T(8,128)(2,1)S(1)}, u32[]{:S(2)}, u32[]{:S(2)}) collective-permute-start(bf16[128,128]{1,0:T(8,128)(2,1)S(1)} %get-tuple-element.59), channel_id=1, source_target_pairs={{0,16},{4,20},{8,24},{12,28},{16,0},{20,4},{24,8},{28,12},{1,17},{... | collective-permute-start | bytes 98312 | tf_op jit(solution)/shard_map/ppermute | solution.py:504
  51.4 2.7 %shard_map.69 = (f32[2,1024,128]{2,1,0:T(8,128)S(1)}, f32[128,16]{1,0:T(8,128)}) custom-call(s32[7]{0:T(128)S(1)} %stack.19.place_ref, s32[2]{0:T(128)S(1)} %copy-done.3, f32[4096,128]{1,0:T(8,128)S(1)} %get-tuple-element.50.cost_ref, f32[128,16]{1,0:T(8,128)S(1)} %get-tuple-element.61.refs_0_), custom_call_target="tpu_custom_call" | custom-call | flops 10000000000 | bytes 4194304 | tf_op jit(solution)/shard_map/pallas_call | solution.py:505
  54.1 2.7 %shard_map.70 = f32[8,128,128]{2,1,0:T(8,128)} custom-call(s32[7]{0:T(128)S(1)} %stack.19.place_ref, s32[2]{0:T(128)S(1)} %copy-done.3, bf16[8,128,128]{2,1,0:T(8,128)(2,1)S(1)} %get-tuple-element.52.refs_0_, bf16[8,128,128]{2,1,0:T(8,128)(2,1)S(1)} %collective-permute-done.8.refs_1_, bf16[8,128,128]{2,1,0:T(8,128)(2,1)S(1)} %collective-permute-done.9.refs_2_, ...), custom_call_target="tpu_custom_call" | custom-call | flops 3000000000 | bytes 4194304 | tf_op jit(solution)/shard_map/pallas_call | solution.py:513
  (16 shorter events, 0.1 us)
Async XLA Ops:
  0.0 11.3 %collective-permute-start.3 = (bf16[16,64,128]{2,1,0:T(8,128)(2,1)}, bf16[16,64,128]{2,1,0:T(8,128)(2,1)S(1)}, u32[]{:S(2)}, u32[]{:S(2)}) collective-permute-start(bf16[16,64,128]{2,1,0:T(8,128)(2,1)} %bitcast.10), channel_id=1, source_target_pairs={{0,2},{1,3},{2,0},{3,1},{4,6},{5,7},{6,4},{7,5},{8,10},{9,11},{10,... | collective-permute-start | bytes 786440 | tf_op jit(solution)/shard_map/ppermute | solution.py:376
  3.0 12.1 %collective-permute-start.4 = (bf16[16,64,128]{2,1,0:T(8,128)(2,1)}, bf16[16,64,128]{2,1,0:T(8,128)(2,1)S(1)}, u32[]{:S(2)}, u32[]{:S(2)}) collective-permute-start(bf16[16,64,128]{2,1,0:T(8,128)(2,1)} %bitcast.11), channel_id=1, source_target_pairs={{0,1},{1,0},{2,3},{3,2},{4,5},{5,4},{6,7},{7,6},{8,9},{9,8},{10,11... | collective-permute-start | bytes 786440 | tf_op jit(solution)/shard_map/ppermute | solution.py:376
  3.9 10.4 %collective-permute-start.1 = (bf16[2,3,64,128]{3,2,1,0:T(8,128)(2,1)S(1)}, bf16[2,3,64,128]{3,2,1,0:T(8,128)(2,1)S(1)}, u32[]{:S(2)}, u32[]{:S(2)}) collective-permute-start(bf16[2,3,64,128]{3,2,1,0:T(8,128)(2,1)S(1)} %get-tuple-element.63), channel_id=1, source_target_pairs={{4,0},{8,4},{12,8},{16,12},{20,16},{24,20},{28,24},{5,1},{9,5},{13... | collective-permute-start | bytes 294920 | tf_op jit(solution)/shard_map/ppermute | solution.py:408
  5.2 9.1 %collective-permute-start = (bf16[2,3,64,128]{3,2,1,0:T(8,128)(2,1)S(1)}, bf16[2,3,64,128]{3,2,1,0:T(8,128)(2,1)S(1)}, u32[]{:S(2)}, u32[]{:S(2)}) collective-permute-start(bf16[2,3,64,128]{3,2,1,0:T(8,128)(2,1)S(1)} %get-tuple-element.64), channel_id=1, source_target_pairs={{0,4},{4,8},{8,12},{12,16},{16,20},{20,24},{24,28},{1,5},{5,9},{9,... | collective-permute-start | bytes 294920 | tf_op jit(solution)/shard_map/ppermute | solution.py:407
  11.3 3.7 %collective-permute-start.5 = (bf16[16,64,128]{2,1,0:T(8,128)(2,1)S(1)}, bf16[16,64,128]{2,1,0:T(8,128)(2,1)S(1)}, u32[]{:S(2)}, u32[]{:S(2)}) collective-permute-start(bf16[16,64,128]{2,1,0:T(8,128)(2,1)S(1)} %collective-permute-done.3.refs_1_), channel_id=1, source_target_pairs={{0,1},{1,0},{2,3},{3,2},{4,5},{5,4},{6,7},{7,6},{8,9},{9,8},{10,11... | collective-permute-start | bytes 786440 | tf_op jit(solution)/shard_map/ppermute | solution.py:376
  11.4 1.0 %copy-start = (bf16[2,8,64,128]{3,2,1,0:T(8,128)(2,1)S(1)}, bf16[2,8,64,128]{3,2,1,0:T(8,128)(2,1)}, u32[]{:S(2)}) copy-start(bf16[2,8,64,128]{3,2,1,0:T(8,128)(2,1)} %param.6) | copy-start | bytes 786436
  12.4 1.0 %copy-start.1 = (bf16[3,3,3,64,64]{4,3,2,1,0:T(8,128)(2,1)S(1)}, bf16[3,3,3,64,64]{4,3,2,1,0:T(8,128)(2,1)}, u32[]{:S(2)}) copy-start(bf16[3,3,3,64,64]{4,3,2,1,0:T(8,128)(2,1)} %filter_ref.1) | copy-start | bytes 663556
  13.4 0.7 %copy-start.2 = (f32[3,64]{1,0:T(4,128)S(1)}, f32[3,64]{1,0:T(4,128)}, u32[]{:S(2)}) copy-start(f32[3,64]{1,0:T(4,128)} %bias_ref.1) | copy-start | bytes 2308
  14.4 7.7 %collective-permute-start.2 = (bf16[13,64,128]{2,1,0:T(8,128)(2,1)S(1)}, bf16[13,64,128]{2,1,0:T(8,128)(2,1)S(1)}, u32[]{:S(2)}, u32[]{:S(2)}) collective-permute-start(bf16[13,64,128]{2,1,0:T(8,128)(2,1)S(1)} %pad_maximum_fusion.refs_2_), channel_id=1, source_target_pairs={{0,2},{1,3},{2,0},{3,1},{4,6},{5,7},{6,4},{7,5},{8,10},{9,11},{10,... | collective-permute-start | bytes 638984 | tf_op jit(solution)/shard_map/ppermute | solution.py:376
  14.7 7.4 %collective-permute-start.6 = (bf16[13,64,128]{2,1,0:T(8,128)(2,1)S(1)}, bf16[13,64,128]{2,1,0:T(8,128)(2,1)S(1)}, u32[]{:S(2)}, u32[]{:S(2)}) collective-permute-start(bf16[13,64,128]{2,1,0:T(8,128)(2,1)S(1)} %pad_maximum_fusion.refs_2_), channel_id=1, source_target_pairs={{0,1},{1,0},{2,3},{3,2},{4,5},{5,4},{6,7},{7,6},{8,9},{9,8},{10,11... | collective-permute-start | bytes 638984 | tf_op jit(solution)/shard_map/ppermute | solution.py:376
  22.1 13.5 %copy-start.3 = (s32[2]{0:T(128)S(1)}, s32[2]{0:T(128)}, u32[]{:S(2)}) copy-start(s32[2]{0:T(128)} %charge_ref.7) | copy-start | bytes 28
  22.1 1.5 %collective-permute-start.7 = (bf16[13,64,128]{2,1,0:T(8,128)(2,1)S(1)}, bf16[13,64,128]{2,1,0:T(8,128)(2,1)S(1)}, u32[]{:S(2)}, u32[]{:S(2)}) collective-permute-start(bf16[13,64,128]{2,1,0:T(8,128)(2,1)S(1)} %collective-permute-done.2.refs_3_), channel_id=1, source_target_pairs={{0,1},{1,0},{2,3},{3,2},{4,5},{5,4},{6,7},{7,6},{8,9},{9,8},{10,11... | collective-permute-start | bytes 638984 | tf_op jit(solution)/shard_map/ppermute | solution.py:376
  31.5 15.1 %collective-permute-start.10 = (bf16[8,128,128]{2,1,0:T(8,128)(2,1)S(1)}, bf16[8,128,128]{2,1,0:T(8,128)(2,1)S(1)}, u32[]{:S(2)}, u32[]{:S(2)}) collective-permute-start(bf16[8,128,128]{2,1,0:T(8,128)(2,1)S(1)} %get-tuple-element.52.refs_0_), channel_id=1, source_target_pairs={{0,12},{4,0},{8,4},{12,8},{16,28},{20,16},{24,20},{28,24},{1,13},{... | collective-permute-start | bytes 786440 | tf_op jit(solution)/shard_map/ppermute | solution.py:474
  34.9 12.4 %collective-permute-start.9 = (bf16[8,128,128]{2,1,0:T(8,128)(2,1)S(1)}, bf16[8,128,128]{2,1,0:T(8,128)(2,1)S(1)}, u32[]{:S(2)}, u32[]{:S(2)}) collective-permute-start(bf16[8,128,128]{2,1,0:T(8,128)(2,1)S(1)} %get-tuple-element.52.refs_0_), channel_id=1, source_target_pairs={{0,8},{4,12},{8,0},{12,4},{16,24},{20,28},{24,16},{28,20},{1,9},{5... | collective-permute-start | bytes 786440 | tf_op jit(solution)/shard_map/ppermute | solution.py:474
  35.4 12.0 %collective-permute-start.8 = (bf16[8,128,128]{2,1,0:T(8,128)(2,1)S(1)}, bf16[8,128,128]{2,1,0:T(8,128)(2,1)S(1)}, u32[]{:S(2)}, u32[]{:S(2)}) collective-permute-start(bf16[8,128,128]{2,1,0:T(8,128)(2,1)S(1)} %get-tuple-element.52.refs_0_), channel_id=1, source_target_pairs={{0,4},{4,8},{8,12},{12,0},{16,20},{20,24},{24,28},{28,16},{1,5},{5... | collective-permute-start | bytes 786440 | tf_op jit(solution)/shard_map/ppermute | solution.py:474
  48.7 5.4 %collective-permute-start.11 = (bf16[128,128]{1,0:T(8,128)(2,1)S(1)}, bf16[128,128]{1,0:T(8,128)(2,1)S(1)}, u32[]{:S(2)}, u32[]{:S(2)}) collective-permute-start(bf16[128,128]{1,0:T(8,128)(2,1)S(1)} %get-tuple-element.59), channel_id=1, source_target_pairs={{0,16},{4,20},{8,24},{12,28},{16,0},{20,4},{24,8},{28,12},{1,17},{... | collective-permute-start | bytes 98312 | tf_op jit(solution)/shard_map/ppermute | solution.py:504
